TPU v7x, 32 devices: a whole 2x2x4 slice. The times are simulated.
32 devices in a mesh: asset: 16 (over z, y, x), rhs: 2 (over core).
Axes of the slice: x: 2, y: 2, z: 4, core: 2. Of those that a mesh axis runs over, the one named last changes fastest.
Arguments:
- targets: float32 [16384, 256], P('asset', 'rhs'), may hold values from -27 to 27
- ridge: float32 [16384], P('asset'), may hold values from 0.8 to 2.5
- blocks: bfloat16 [128, 16, 128, 128], P('asset', None, 'rhs'), may hold values from -0.046875 to 0.046875
- col_index: int32 [128, 16], P('asset'), may hold values from 0 to 127, as said below
- row_length: int32 [128], P('asset'), may hold values from 8 to 16, as said below
Outputs:
- solution: float32 [16384, 256], P('asset', 'rhs')
- residual: float32 [16384, 256], P('asset', 'rhs')
Inputs may be any that keep to these rules, and one draw needn't show every extreme that they name: `col_index`: the block columns of row i are distinct and lie within 8 blocks of i, counted cyclically modulo 128; slots at or past row_length[i] hold such columns too and are ignored. `row_length`: each aligned group of 8 block rows holds at least one row with 16 used slots.
All inputs are finite; a program needn't handle non-finite values.
Results may differ from a plain program's by a relative error of at most 0.0075.
Values may be sent and summed in bfloat16 or wider, within the bound.
No kernel may reach another device: no remote copies, remote signals or barrier semaphores. Data moves between devices by JAX's collectives and lax.ppermute only.
A program may use at most 64 MiB of HBM per device.

v0:
```python
import jax
import jax.numpy as jnp
from jax import lax
from jax.sharding import PartitionSpec as P

ITERS = 3


def from_behind(block, axis, distance):
    devices = range(lax.axis_size(axis))
    route = [((i - distance) % len(devices), i) for i in devices]
    return lax.ppermute(block, axis, route)


def extended_2(shard, sides, width):
    for axis, dim in sides:
        devices, length = (lax.axis_size(axis), shard.shape[dim])
        up = [(i, (i + 1) % devices) for i in range(devices)]
        down = [(j, i) for i, j in up]
        last = lax.slice_in_dim(shard, length - width, length, axis=dim)
        first = lax.slice_in_dim(shard, 0, width, axis=dim)
        before = lax.ppermute(last, axis, up)
        after = lax.ppermute(first, axis, down)
        shard = jnp.concatenate([before, shard, after], axis=dim)
    return shard


def shards(targets, ridge, blocks, col_index, row_length):
    rows = col_index.shape[0]
    slots = col_index.shape[1]
    width = blocks.shape[3]
    cols = targets.shape[1]
    total = rows * lax.axis_size("asset")
    start = lax.axis_index("asset") * rows
    used = jnp.arange(slots)[None, :] < row_length[:, None]
    masked_shard = blocks * used[:, :, None, None].astype(jnp.bfloat16)
    local_pos = (col_index - start + rows) % total
    onehot = (local_pos[None, :, :] == jnp.arange(3 * rows, dtype=jnp.int32)[:, None, None]).astype(
        jnp.bfloat16
    )
    own_blocks = lax.all_gather(masked_shard, "rhs", axis=2, tiled=True)
    weave = jnp.einsum(
        "cik,ikab->ciab", onehot, own_blocks, preferred_element_type=jnp.float32
    ).astype(jnp.bfloat16)

    def squares(values):
        return lax.psum(jnp.sum(values * values, axis=0), "asset")

    solution = jnp.zeros_like(targets)
    residual = targets
    direction = targets
    norm_now = squares(residual)
    for step in range(ITERS):
        rounded = direction.astype(jnp.bfloat16)
        operate_extended = extended_2(rounded, (("asset", 0),), rows * width)
        operate_extended = operate_extended.reshape(3 * rows, width, cols)
        picked = jnp.take(operate_extended, local_pos, axis=0)
        forward = jnp.einsum(
            "ikab,ikbn->ian", own_blocks, picked, preferred_element_type=jnp.float32
        )
        slab = jnp.einsum(
            "qjpt,jpu->qtu",
            weave,
            operate_extended[rows : 2 * rows],
            preferred_element_type=jnp.float32,
        )
        from_upper = from_behind(slab[:rows].astype(jnp.bfloat16), "asset", -1).astype(jnp.float32)
        from_lower = from_behind(slab[2 * rows :].astype(jnp.bfloat16), "asset", 1).astype(
            jnp.float32
        )
        backward = slab[rows : 2 * rows] + from_upper + from_lower
        image = ridge[:, None] * direction + 0.5 * (forward + backward).reshape(rows * width, cols)
        curve = lax.psum(jnp.sum(direction * image, axis=0), "asset")
        alpha = norm_now / curve
        solution = solution + alpha * direction
        residual = residual - alpha * image
        norm_next = squares(residual)
        direction = residual + norm_next / norm_now * direction
        norm_now = norm_next
    return (solution, residual)


def solution(mesh):
    return jax.shard_map(
        shards,
        mesh=mesh,
        in_specs=(
            P("asset", "rhs"),
            P("asset"),
            P("asset", None, "rhs", None),
            P("asset", None),
            P("asset"),
        ),
        out_specs=(P("asset", "rhs"), P("asset", "rhs")),
        check_vma=False,
    )
```

profile of v0, /device:TPU:0, one launch (start us, length us, event | category | flops | bytes accessed | tf_op | source)
XLA Modules:
  0.0 324.0 jit_solution(736840629473532589)
XLA Ops:
  7.2 0.0 copy-start
  7.2 0.0 copy-start.2
  7.2 0.0 all-gather.2.cloned.1.call-start
  7.2 0.8 fusion.39
  8.0 3.1 broadcast_multiply_fusion
  11.2 0.0 all-gather.2.cloned.1.call-update
  11.2 0.0 copy-done
  11.2 7.0 %collective-permute-start.1 = (bf16[1024,128]{1,0:T(8,128)(2,1)S(1)}, bf16[1024,128]{1,0:T(8,128)(2,1)S(1)}, u32[]{:S(2)}, u32[]{:S(2)}) collective-permute-start(bf16[1024,128]{1,0:T(8,128)(2,1)S(1)} %convert_element_type.49), channel_id=1, source_target_pairs={{2,0},{4,2},{6,4},{8,6},{10,8},{12,10},{14,12},{16,14},{18,16},{20... | collective-permute-start | bytes 786440 | tf_op jit(solution)/shard_map/ppermute | solution.py:23
  18.2 0.0 collective-permute-start
  18.2 0.0 copy-done.2
  18.2 0.1 reshape.93
  18.3 9.4 %all-gather.2.cloned.1.call-done = bf16[8,16,128,128]{3,2,1,0:T(8,128)(2,1)} async-done(((bf16[8,16,64,128]{3,2,1,0:T(8,128)(2,1)}), bf16[8,16,128,128]{3,2,1,0:T(8,128)(2,1)}) %all-gather.2.cloned.1.call-update) | async-done | bytes 4194320 | tf_op jit(solution)/shard_map/all_gather | solution.py:41
  27.7 8.0 %convert_bitcast_fusion = bf16[24,8,128,128]{3,0,2,1:T(8,128)(2,1)} fusion(bf16[8,16,128,128]{3,2,1,0:T(8,128)(2,1)} %all-gather.2.cloned.1.call-done, s32[8,16]{1,0:T(8,128)S(1)} %get-tuple-element.12), kind=kOutput, calls=%fused_computation.3 | convolution fusion | flops 103812096 | bytes 10486272 | tf_op jit(solution)/shard_map/cik,ikab->ciab/dot_general | solution.py:42
  35.7 9.0 %copy.8 = bf16[24,8,128,128]{2,3,1,0:T(8,128)(2,1)} copy(bf16[24,8,128,128]{3,0,2,1:T(8,128)(2,1)} %convert_bitcast_fusion) | data formatting | bytes 12582912 | tf_op jit(solution)/shard_map/convert_element_type | solution.py:44
  44.7 4.6 %fusion.53 = (bf16[24,128,128]{2,1,0:T(8,128)(2,1)S(1)}, f32[24,128,128]{2,1,0:T(8,128)S(1)}) fusion(bf16[24,8,128,128]{2,3,1,0:T(8,128)(2,1)} %copy.8, bf16[8,128,128,1]{2,1,0,3:T(8,128)(2,1)S(1)} %bitcast.88), kind=kOutput, calls=%fused_computation.75 | convolution fusion | flops 805699584 | bytes 8912896 | tf_op jit(solution)/shard_map/qjpt,jpu->qtu/dot_general | solution.py:61
  49.3 0.8 fusion.52
  50.1 1.7 collective-permute-start.3
  51.9 3.9 %collective-permute-start.2 = (bf16[8,128,128]{2,1,0:T(8,128)(2,1)}, bf16[8,128,128]{2,1,0:T(8,128)(2,1)}, u32[]{:S(2)}, u32[]{:S(2)}) collective-permute-start(bf16[8,128,128]{2,1,0:T(8,128)(2,1)} %get-tuple-element.19), channel_id=1, source_target_pairs={{2,0},{4,2},{6,4},{8,6},{10,8},{12,10},{14,12},{16,14},{18,16},{20... | collective-permute-start | bytes 786440 | tf_op jit(solution)/shard_map/ppermute | solution.py:12
  55.8 0.0 collective-permute-done.1
  55.8 0.0 collective-permute-done
  55.8 1.0 pad_maximum_fusion
  56.8 3.1 gather_fusion
  59.9 3.9 %collective-permute-done.3 = bf16[8,128,128]{2,1,0:T(8,128)(2,1)} collective-permute-done((bf16[8,128,128]{2,1,0:T(8,128)(2,1)}, bf16[8,128,128]{2,1,0:T(8,128)(2,1)}, u32[]{:S(2)}, u32[]{:S(2)}) %collective-permute-start.3) | collective-permute-done | bytes 262176 | tf_op jit(solution)/shard_map/ppermute | solution.py:12
  63.8 1.9 collective-permute-done.2
  65.8 0.0 copy-start.1
  65.8 4.9 %fusion.33 = f32[8,128,128]{2,1,0:T(8,128)S(1)} fusion(f32[24,128,128]{2,1,0:T(8,128)S(1)} %get-tuple-element.22, bf16[8,128,128]{2,1,0:T(8,128)(2,1)} %collective-permute-done.3, bf16[8,128,128]{2,1,0:T(8,128)(2,1)} %collective-permute-done.2, bf16[8,16,128,128]{3,2,1,0:T(8,128)(2,1)} %all-gather.2.cloned.1.call-done, ...), kind=kOutput, calls=%fused_computation.39 | convolution fusion | flops 539754496 | bytes 9961600 | tf_op jit(solution)/shard_map/ikab,ikbn->ian/dot_general | solution.py:58
  70.6 0.0 copy-done.1
  70.7 0.2 multiply_reduce_fusion.4
  70.9 39.8 %all-reduce = (f32[128]{0:T(128)S(1)}, f32[128]{0:T(128)S(1)}) all-reduce(f32[128]{0:T(128)S(1)} %get-tuple-element.4, f32[128]{0:T(128)S(1)} %get-tuple-element.3), channel_id=1, replica_groups=mesh['asset'=16,'rhs'=2] {'asset'}, use_global_device_ids=true, to_apply=%region_1.2 | all-reduce | flops 256 | bytes 2048 | tf_op jit(solution)/shard_map/psum | solution.py:47
  110.7 0.2 multiply_reduce_fusion.3
  110.9 36.9 %psum.44 = f32[128]{0:T(128)S(1)} all-reduce(f32[128]{0:T(128)S(1)} %multiply_reduce_fusion.3), channel_id=1, replica_groups=mesh['asset'=16,'rhs'=2] {'asset'}, use_global_device_ids=true, to_apply=%region_5.7 | all-reduce | flops 128 | bytes 1024 | tf_op jit(solution)/shard_map/psum | solution.py:47
  147.8 0.2 fusion.49
  148.0 1.8 collective-permute-start.5
  149.9 0.3 collective-permute-start.4
  150.1 5.7 %fusion.54 = (bf16[24,128,128]{2,1,0:T(8,128)(2,1)S(1)}, f32[24,128,128]{2,1,0:T(8,128)}) fusion(bf16[24,8,128,128]{2,3,1,0:T(8,128)(2,1)} %copy.8, bf16[8,128,128,1]{2,1,0,3:T(8,128)(2,1)S(1)} %bitcast.89), kind=kOutput, calls=%fused_computation.76 | convolution fusion | flops 805699584 | bytes 8912896 | tf_op jit(solution)/shard_map/qjpt,jpu->qtu/dot_general | solution.py:61
  155.9 2.9 collective-permute-start.7
  158.8 2.8 collective-permute-start.6
  161.6 0.0 collective-permute-done.5
  161.6 0.0 collective-permute-done.4
  161.6 0.1 pad_maximum_fusion.1
  161.6 3.1 gather_fusion.1
  164.8 1.3 collective-permute-done.7
  166.1 0.0 collective-permute-done.6
  166.1 4.9 %fusion.30 = f32[8,128,128]{2,1,0:T(8,128)S(1)} fusion(f32[24,128,128]{2,1,0:T(8,128)} %get-tuple-element.24, bf16[8,128,128]{2,1,0:T(8,128)(2,1)S(1)} %collective-permute-done.7, bf16[8,128,128]{2,1,0:T(8,128)(2,1)S(1)} %collective-permute-done.6, bf16[8,16,128,128]{3,2,1,0:T(8,128)(2,1)} %all-gather.2.cloned.1.call-done, ...), kind=kOutput, calls=%fused_computation.35 | convolution fusion | flops 539754496 | bytes 9961600 | tf_op jit(solution)/shard_map/ikab,ikbn->ian/dot_general | solution.py:58
  171.0 0.2 multiply_reduce_fusion.2
  171.2 42.1 %psum.45 = f32[128]{0:T(128)S(1)} all-reduce(f32[128]{0:T(128)S(1)} %multiply_reduce_fusion.2), channel_id=1, replica_groups=mesh['asset'=16,'rhs'=2] {'asset'}, use_global_device_ids=true, to_apply=%region_7.9 | all-reduce | flops 128 | bytes 1024 | tf_op jit(solution)/shard_map/psum | solution.py:73
  213.3 0.3 multiply_reduce_fusion.1
  213.6 36.8 %psum.46 = f32[128]{0:T(128)S(1)} all-reduce(f32[128]{0:T(128)S(1)} %get-tuple-element.7), channel_id=1, replica_groups=mesh['asset'=16,'rhs'=2] {'asset'}, use_global_device_ids=true, to_apply=%region_9.11 | all-reduce | flops 128 | bytes 1024 | tf_op jit(solution)/shard_map/psum | solution.py:47
  250.4 0.1 fusion.34
  250.4 2.1 collective-permute-start.9
  252.6 0.0 collective-permute-start.8
  252.6 5.7 %fusion.55 = (bf16[24,128,128]{2,1,0:T(8,128)(2,1)S(1)}, f32[24,128,128]{2,1,0:T(8,128)}) fusion(bf16[24,8,128,128]{2,3,1,0:T(8,128)(2,1)} %copy.8, bf16[8,128,128,1]{2,1,0,3:T(8,128)(2,1)S(1)} %bitcast.90), kind=kOutput, calls=%fused_computation.77 | convolution fusion | flops 805699584 | bytes 8912896 | tf_op jit(solution)/shard_map/qjpt,jpu->qtu/dot_general | solution.py:61
  258.4 2.9 collective-permute-start.11
  261.3 2.8 collective-permute-start.10
  264.1 0.0 collective-permute-done.9
  264.1 0.0 collective-permute-done.8
  264.1 0.1 pad_maximum_fusion.2
  264.1 3.0 gather_fusion.2
  267.1 1.4 collective-permute-done.11
  268.6 0.1 collective-permute-done.10
  268.7 5.0 %fusion.27 = f32[8,128,128]{2,1,0:T(8,128)S(1)} fusion(f32[24,128,128]{2,1,0:T(8,128)} %get-tuple-element.26, bf16[8,128,128]{2,1,0:T(8,128)(2,1)} %collective-permute-done.11, bf16[8,128,128]{2,1,0:T(8,128)(2,1)} %collective-permute-done.10, bf16[8,16,128,128]{3,2,1,0:T(8,128)(2,1)} %all-gather.2.cloned.1.call-done, ...), kind=kOutput, calls=%fused_computation.31 | convolution fusion | flops 539754496 | bytes 9961600 | tf_op jit(solution)/shard_map/ikab,ikbn->ian/dot_general | solution.py:58
  273.7 0.2 multiply_reduce_fusion
  274.0 42.0 %psum.47 = f32[128]{0:T(128)S(1)} all-reduce(f32[128]{0:T(128)S(1)} %multiply_reduce_fusion), channel_id=1, replica_groups=mesh['asset'=16,'rhs'=2] {'asset'}, use_global_device_ids=true, to_apply=%region_11.13 | all-reduce | flops 128 | bytes 1024 | tf_op jit(solution)/shard_map/psum | solution.py:73
  316.0 1.2 multiply_subtract_fusion
  (11 shorter events, 0.2 us)
Async XLA Ops:
  7.2 4.0 %copy-start = (f32[1024,128]{1,0:T(8,128)S(1)}, f32[1024,128]{1,0:T(8,128)}, u32[]{:S(2)}) copy-start(f32[1024,128]{1,0:T(8,128)} %param.7) | copy-start | bytes 1572868
  7.2 11.0 %copy-start.2 = (s32[8,16]{1,0:T(8,128)S(1)}, s32[8,16]{1,0:T(8,128)}, u32[]{:S(2)}) copy-start(s32[8,16]{1,0:T(8,128)} %param.10) | copy-start | bytes 1540
  7.2 20.5 %all-gather.2.cloned.1.call-start = ((), (), s32[]{:S(2)}) async-start(), calls=%async_computation | async-start | bytes 6291456 | tf_op jit(solution)/shard_map/all_gather | solution.py:41
  11.2 44.5 %collective-permute-start.1 = (bf16[1024,128]{1,0:T(8,128)(2,1)S(1)}, bf16[1024,128]{1,0:T(8,128)(2,1)S(1)}, u32[]{:S(2)}, u32[]{:S(2)}) collective-permute-start(bf16[1024,128]{1,0:T(8,128)(2,1)S(1)} %convert_element_type.49), channel_id=1, source_target_pairs={{2,0},{4,2},{6,4},{8,6},{10,8},{12,10},{14,12},{16,14},{18,16},{20... | collective-permute-start | bytes 786440 | tf_op jit(solution)/shard_map/ppermute | solution.py:23
  18.2 37.6 %collective-permute-start = (bf16[1024,128]{1,0:T(8,128)(2,1)S(1)}, bf16[1024,128]{1,0:T(8,128)(2,1)}, u32[]{:S(2)}, u32[]{:S(2)}) collective-permute-start(bf16[1024,128]{1,0:T(8,128)(2,1)S(1)} %convert_element_type.49), channel_id=1, source_target_pairs={{0,2},{2,4},{4,6},{6,8},{8,10},{10,12},{12,14},{14,16},{16,18},{18... | collective-permute-start | bytes 786440 | tf_op jit(solution)/shard_map/ppermute | solution.py:22
  50.1 13.7 %collective-permute-start.3 = (bf16[8,128,128]{2,1,0:T(8,128)(2,1)}, bf16[8,128,128]{2,1,0:T(8,128)(2,1)}, u32[]{:S(2)}, u32[]{:S(2)}) collective-permute-start(bf16[8,128,128]{2,1,0:T(8,128)(2,1)} %get-tuple-element.20), channel_id=1, source_target_pairs={{30,0},{0,2},{2,4},{4,6},{6,8},{8,10},{10,12},{12,14},{14,16},{16,... | collective-permute-start | bytes 786440 | tf_op jit(solution)/shard_map/ppermute | solution.py:12
  51.9 13.9 %collective-permute-start.2 = (bf16[8,128,128]{2,1,0:T(8,128)(2,1)}, bf16[8,128,128]{2,1,0:T(8,128)(2,1)}, u32[]{:S(2)}, u32[]{:S(2)}) collective-permute-start(bf16[8,128,128]{2,1,0:T(8,128)(2,1)} %get-tuple-element.19), channel_id=1, source_target_pairs={{2,0},{4,2},{6,4},{8,6},{10,8},{12,10},{14,12},{16,14},{18,16},{20... | collective-permute-start | bytes 786440 | tf_op jit(solution)/shard_map/ppermute | solution.py:12
  65.8 4.9 %copy-start.1 = (f32[1024]{0:T(1024)S(1)}, f32[1024]{0:T(1024)}, u32[]{:S(2)}) copy-start(f32[1024]{0:T(1024)} %param.8) | copy-start | bytes 12292
  148.0 13.5 %collective-permute-start.5 = (bf16[1024,128]{1,0:T(8,128)(2,1)S(1)}, bf16[1024,128]{1,0:T(8,128)(2,1)S(1)}, u32[]{:S(2)}, u32[]{:S(2)}) collective-permute-start(bf16[1024,128]{1,0:T(8,128)(2,1)S(1)} %get-tuple-element.9), channel_id=1, source_target_pairs={{2,0},{4,2},{6,4},{8,6},{10,8},{12,10},{14,12},{16,14},{18,16},{20... | collective-permute-start | bytes 786440 | tf_op jit(solution)/shard_map/ppermute | solution.py:23
  149.9 11.7 %collective-permute-start.4 = (bf16[1024,128]{1,0:T(8,128)(2,1)S(1)}, bf16[1024,128]{1,0:T(8,128)(2,1)S(1)}, u32[]{:S(2)}, u32[]{:S(2)}) collective-permute-start(bf16[1024,128]{1,0:T(8,128)(2,1)S(1)} %get-tuple-element.9), channel_id=1, source_target_pairs={{0,2},{2,4},{4,6},{6,8},{8,10},{10,12},{12,14},{14,16},{16,18},{18... | collective-permute-start | bytes 786440 | tf_op jit(solution)/shard_map/ppermute | solution.py:22
  155.9 10.2 %collective-permute-start.7 = (bf16[8,128,128]{2,1,0:T(8,128)(2,1)S(1)}, bf16[8,128,128]{2,1,0:T(8,128)(2,1)S(1)}, u32[]{:S(2)}, u32[]{:S(2)}) collective-permute-start(bf16[8,128,128]{2,1,0:T(8,128)(2,1)S(1)} %get-tuple-element.18), channel_id=1, source_target_pairs={{30,0},{0,2},{2,4},{4,6},{6,8},{8,10},{10,12},{12,14},{14,16},{16,... | collective-permute-start | bytes 786440 | tf_op jit(solution)/shard_map/ppermute | solution.py:12
  158.8 7.3 %collective-permute-start.6 = (bf16[8,128,128]{2,1,0:T(8,128)(2,1)S(1)}, bf16[8,128,128]{2,1,0:T(8,128)(2,1)S(1)}, u32[]{:S(2)}, u32[]{:S(2)}) collective-permute-start(bf16[8,128,128]{2,1,0:T(8,128)(2,1)S(1)} %get-tuple-element.17), channel_id=1, source_target_pairs={{2,0},{4,2},{6,4},{8,6},{10,8},{12,10},{14,12},{16,14},{18,16},{20... | collective-permute-start | bytes 786440 | tf_op jit(solution)/shard_map/ppermute | solution.py:12
  250.4 13.7 %collective-permute-start.9 = (bf16[1024,128]{1,0:T(8,128)(2,1)S(1)}, bf16[1024,128]{1,0:T(8,128)(2,1)S(1)}, u32[]{:S(2)}, u32[]{:S(2)}) collective-permute-start(bf16[1024,128]{1,0:T(8,128)(2,1)S(1)} %fusion.34), channel_id=1, source_target_pairs={{2,0},{4,2},{6,4},{8,6},{10,8},{12,10},{14,12},{16,14},{18,16},{20... | collective-permute-start | bytes 786440 | tf_op jit(solution)/shard_map/ppermute | solution.py:23
  252.6 11.5 %collective-permute-start.8 = (bf16[1024,128]{1,0:T(8,128)(2,1)S(1)}, bf16[1024,128]{1,0:T(8,128)(2,1)S(1)}, u32[]{:S(2)}, u32[]{:S(2)}) collective-permute-start(bf16[1024,128]{1,0:T(8,128)(2,1)S(1)} %fusion.34), channel_id=1, source_target_pairs={{0,2},{2,4},{4,6},{6,8},{8,10},{10,12},{12,14},{14,16},{16,18},{18... | collective-permute-start | bytes 786440 | tf_op jit(solution)/shard_map/ppermute | solution.py:22
  258.4 10.2 %collective-permute-start.11 = (bf16[8,128,128]{2,1,0:T(8,128)(2,1)S(1)}, bf16[8,128,128]{2,1,0:T(8,128)(2,1)}, u32[]{:S(2)}, u32[]{:S(2)}) collective-permute-start(bf16[8,128,128]{2,1,0:T(8,128)(2,1)S(1)} %get-tuple-element.16), channel_id=1, source_target_pairs={{30,0},{0,2},{2,4},{4,6},{6,8},{8,10},{10,12},{12,14},{14,16},{16,... | collective-permute-start | bytes 786440 | tf_op jit(solution)/shard_map/ppermute | solution.py:12
  261.3 7.4 %collective-permute-start.10 = (bf16[8,128,128]{2,1,0:T(8,128)(2,1)S(1)}, bf16[8,128,128]{2,1,0:T(8,128)(2,1)}, u32[]{:S(2)}, u32[]{:S(2)}) collective-permute-start(bf16[8,128,128]{2,1,0:T(8,128)(2,1)S(1)} %get-tuple-element.15), channel_id=1, source_target_pairs={{2,0},{4,2},{6,4},{8,6},{10,8},{12,10},{14,12},{16,14},{18,16},{20... | collective-permute-start | bytes 786440 | tf_op jit(solution)/shard_map/ppermute | solution.py:12
Sparse Core Ops, SparseCore 0:
  11.3 16.3 all-gather.1
where the time goes:
time: 325 us; the launch traced here: 324 us
  blocking collectives  198 us (61%)
  matrix products  38.8 us (12%)
  starting transfers between devices  28.3 us (9%)
  local copies, waits for them, and re-layouts  19.3 us (6%)
  waiting for transfers between devices  18.1 us (6%)
  between operations  14.2 us (4%)
  other arithmetic  7.72 us (2%)
    psum x3, blocking collectives, squares(): return lax.psum(jnp.sum(values * values, axis=0), 'asset')  113 us
    psum x2, blocking collectives, shards(): curve = lax.psum(jnp.sum(direction * image, axis=0), 'asset')  84.2 us
    ppermute x6, starting transfers between devices, from_behind(): return lax.ppermute(block, axis, route)  17 us
    dot_general x3, matrix products, shards(): jnp.einsum('qjpt,jpu->qtu', weave, operate_extended[rows:2 * rows], prefe...  16 us
    dot_general x3, matrix products, shards(): jnp.einsum('ikab,ikbn->ian', own_blocks, picked, preferred_element_type=j...  14.8 us
    ppermute x3, starting transfers between devices, extended_2(): after = lax.ppermute(first, axis, down)  10.9 us
    all_gather x1, waiting for transfers between devices, shards(): own_blocks = lax.all_gather(masked_shard, 'rhs', axis=2, tiled=True)  9.37 us
    gather x3, local copies, waits for them, and re-layouts, shards(): picked = jnp.take(operate_extended, local_pos, axis=0)  9.25 us
  transfers between devices with their start and end apart: 13, of which 6 were waited for; matrix products, arithmetic and copies ran while one was open for 14% of the time, Pallas kernels for 0%

commit v1 on v0

v1 whole, which is shorter than its diff:
```python
import jax
import jax.numpy as jnp
from jax import lax
from jax.experimental import pallas as pl
from jax.experimental.pallas import tpu as pltpu
from jax.sharding import PartitionSpec as P

F32 = jnp.float32
BF16 = jnp.bfloat16
VMEM = pl.BlockSpec(memory_space=pltpu.VMEM)
SMEM = pl.BlockSpec(memory_space=pltpu.SMEM)
LIMIT = 24 * 1024 * 1024
NN = (((1,), (0,)), ((), ()))
NT = (((1,), (1,)), ((), ()))


def call(kernel, out_shape, args, smem=0):
    return pl.pallas_call(
        kernel,
        out_shape=out_shape,
        in_specs=[SMEM] * smem + [VMEM] * (len(args) - smem),
        out_specs=jax.tree.map(lambda _: VMEM, out_shape),
        compiler_params=pltpu.CompilerParams(vmem_limit_bytes=LIMIT),
    )(*args)


def column_sums(values, width):
    folded = values[:, :width]
    for at in range(width, values.shape[1], width):
        folded = folded + values[:, at : at + width]
    return jnp.sum(folded.T, axis=0, keepdims=True)


def prepare_kernel(targets_ref, base_ref, rounded_ref, moment_ref):
    width = moment_ref.shape[1]
    for at in range(0, targets_ref.shape[0], width):
        tile = targets_ref[at : at + width, :].T
        base_ref[:, at : at + width] = tile
        rounded_ref[:, at : at + width] = tile.astype(BF16)
    values = targets_ref[...]
    moment_ref[...] = jnp.sum(values * values, axis=0, keepdims=True)


def spread_kernel(place_ref, length_ref, offset_ref, *refs):
    parts, (before_ref, own_ref, after_ref) = refs[:-3], refs[-3:]
    rows, slots, height, _ = parts[0].shape
    for ref in (before_ref, own_ref, after_ref):
        ref[...] = jnp.zeros_like(ref)

    def one_row(row, carry):
        def one_slot(slot, inner):
            place = place_ref[row, slot]
            for part, ref in enumerate(parts):
                start = row * (height * len(parts)) + offset_ref[part]
                at = pl.ds(pl.multiple_of(start, height), height)
                for side, out in enumerate((before_ref, own_ref, after_ref)):

                    @pl.when(place // rows == side)
                    def _():
                        out[place % rows, at, :] = ref[row, slot]

            return inner

        return lax.fori_loop(0, length_ref[row], one_slot, carry)

    lax.fori_loop(0, rows, one_row, 0)


def columns(ref, first, last, rows):
    return jnp.concatenate([ref[c, rows, :] for c in range(first, last)], axis=1)


def products_kernel(before_ref, after_ref, v_ref, up_ref, down_ref):
    rows, _, width = before_ref.shape
    for j in range(0, rows, 2):
        out = slice(j * width, (j + 2) * width)
        low = slice(0, (j + 2) * width)
        up_ref[:, out] = lax.dot_general(
            v_ref[:, low], columns(before_ref, j, j + 2, low), NN, preferred_element_type=F32
        ).astype(BF16)
        high = slice(j * width, rows * width)
        down_ref[:, out] = lax.dot_general(
            v_ref[:, high], columns(after_ref, j, j + 2, high), NN, preferred_element_type=F32
        ).astype(BF16)


def local_kernel(own_ref, v_ref, out_ref):
    rows, _, width = own_ref.shape
    every = slice(0, rows * width)
    for j in range(0, rows, 2):
        out = slice(j * width, (j + 2) * width)
        out_ref[:, out] = lax.dot_general(
            v_ref[...], columns(own_ref, j, j + 2, every), NN, preferred_element_type=F32
        ) + lax.dot_general(
            v_ref[...], columns(own_ref, 0, rows, out), NT, preferred_element_type=F32
        )


def finish_kernel(
    before_ref, after_ref, ridge_ref, k_ref, local_ref, vb_ref, va_ref, qb_ref, qa_ref,
    next_ref, rounded_ref, moment_ref
):
    rows, _, width = before_ref.shape
    for j in range(0, rows, 2):
        out = slice(j * width, (j + 2) * width)
        matrix = jnp.concatenate(
            [columns(before_ref, j, rows, out), columns(after_ref, 0, j + 2, out)], axis=1
        )
        field = jnp.concatenate(
            [vb_ref[:, j * width :], va_ref[:, : (j + 2) * width]], axis=1
        )
        both = lax.dot_general(field, matrix, NT, preferred_element_type=F32)
        both = both + local_ref[:, out] + qb_ref[:, out].astype(F32) + qa_ref[:, out].astype(F32)
        value = ridge_ref[:, out] * k_ref[:, out] + 0.5 * both
        next_ref[:, out] = value
        rounded_ref[:, out] = value.astype(BF16)
    value = next_ref[...]
    moment_ref[0:1, :] = column_sums(k_ref[...] * value, width)
    moment_ref[1:2, :] = column_sums(value * value, width)


def share(above, below):
    return jnp.where(below == 0, 0.0, above / below)


def scalars(m, shift, iters):
    zero = jnp.zeros_like(m[0])
    solution = [zero] * iters
    residual = [zero + 1.0] + [zero] * iters
    direction = [zero + 1.0] + [zero] * (iters - 1)

    def inner(a, b):
        total = zero
        for i, left in enumerate(a):
            for j, right in enumerate(b):
                if i + j < len(m):
                    total = total + left * right * m[i + j]
        return total

    now = m[0]
    for step in range(iters):
        used = direction[: step + 1]
        image = [shift * value for value in used] + [zero]
        for i, value in enumerate(used):
            image[i + 1] = image[i + 1] + value
        alpha = share(now, inner(used, image))
        for i, value in enumerate(used):
            solution[i] = solution[i] + alpha * value
        for i, value in enumerate(image):
            residual[i] = residual[i] - alpha * value
        if step + 1 < iters:
            left = residual[: step + 2]
            new = inner(left, left)
            beta = share(new, now)
            direction = [r + beta * d for r, d in zip(residual[:iters], direction, strict=True)]
            now = new
    return solution, residual


def combine_kernel(shift_ref, moment_ref, targets_ref, k1_ref, k2_ref, k3_ref, solution_ref, residual_ref):
    width = moment_ref.shape[2]
    summed = moment_ref[0]
    for i in range(1, moment_ref.shape[0]):
        summed = summed + moment_ref[i]
    m = [summed[i : i + 1, :] for i in range(6)]
    x, r = scalars(m, shift_ref[0:1, :], 3)
    for at in range(0, targets_ref.shape[0], width):
        out = slice(at, at + width)
        k0 = targets_ref[out, :]
        k1, k2, k3 = k1_ref[:, out].T, k2_ref[:, out].T, k3_ref[:, out].T
        solution_ref[out, :] = x[0] * k0 + x[1] * k1 + x[2] * k2
        residual_ref[out, :] = r[0] * k0 + r[1] * k1 + r[2] * k2 + r[3] * k3


def moved(value, axis, distance):
    count = lax.axis_size(axis)
    return lax.ppermute(value, axis, [(i, (i + distance) % count) for i in range(count)])


def to_all(value, axis):
    count = lax.axis_size(axis)
    return lax.all_to_all(jnp.broadcast_to(value[None], (count,) + value.shape), axis, 0, 0)


def shards(targets, ridge, blocks, col_index, row_length):
    rows, slots, height, width = blocks.shape
    cols = targets.shape[1]
    assets = rows * width
    devices = lax.axis_size("asset")
    halves = lax.axis_size("rhs")
    start = lax.axis_index("asset") * rows
    place = (col_index - start + rows) % (rows * devices)
    if halves == 2:
        mine = lax.axis_index("rhs") * height
        parts = [blocks, moved(blocks, "rhs", 1)]
        offsets = jnp.stack([mine, height - mine]).astype(jnp.int32)
    else:
        parts = [lax.all_gather(blocks, "rhs", axis=2, tiled=True)]
        offsets = jnp.zeros((1,), jnp.int32)

    def shape(kind, *dims):
        return jax.ShapeDtypeStruct(dims, kind)

    field, rounded = shape(F32, cols, assets), shape(BF16, cols, assets)
    base, v, m0 = call(prepare_kernel, (field, rounded, shape(F32, 1, cols)), (targets,))
    sums = to_all(jnp.broadcast_to(jnp.sum(ridge), (1, 128)), "asset")
    shift = jnp.sum(sums, axis=0) / (devices * assets)
    shifted = ridge[None, :] - shift[0, 0]

    band = shape(BF16, rows, assets, width)
    before, own, after = call(
        spread_kernel, (band,) * 3, (place, row_length, offsets, *parts), smem=3
    )
    basis, moments = [base], [m0]
    for step in range(3):
        vb, va = moved(v, "asset", 1), moved(v, "asset", -1)
        up, down = call(products_kernel, (rounded,) * 2, (before, after, v))
        qa, qb = moved(up, "asset", -1), moved(down, "asset", 1)
        local = call(local_kernel, field, (own, v))
        following, v, pair = call(
            finish_kernel,
            (field, rounded, shape(F32, 2, cols)),
            (before, after, shifted, basis[-1], local, vb, va, qb, qa),
        )
        basis.append(following)
        moments.append(pair)
    gathered = to_all(jnp.concatenate(moments + [jnp.zeros((1, cols), F32)]), "asset")
    out = shape(F32, assets, cols)
    return call(combine_kernel, (out, out), (shift, gathered, targets, *basis[1:]))


def solution(mesh):
    return jax.shard_map(
        shards,
        mesh=mesh,
        in_specs=(
            P("asset", "rhs"),
            P("asset"),
            P("asset", None, "rhs", None),
            P("asset", None),
            P("asset"),
        ),
        out_specs=(P("asset", "rhs"), P("asset", "rhs")),
        check_vma=False,
    )
```

time: 325 us -> 112 us (0.34)
  blocking collectives: 198 us -> 14.4 us
  matrix products: 38.8 us -> 0 us
  Pallas kernels: 0 us -> 17.2 us
  waiting for transfers between devices: 18.1 us -> 34 us
  local copies, waits for them, and re-layouts: 19.3 us -> 4.57 us
  between operations: 14.2 us -> 0.79 us
  starting transfers between devices: 28.3 us -> 39 us
  other arithmetic: 7.72 us -> 2.12 us
    psum x5 -> x0, blocking collectives: 198 us -> none  [the longest x3 113 us: squares(): return lax.psum(jnp.sum(values * values, axis=0), 'asset')]
    dot_general x7 -> x0, matrix products: 38.8 us -> none  [the longest x3 16 us: shards(): jnp.einsum('qjpt,jpu->qtu', weave, operate_extended[rows:2 * rows], prefe...]
    ppermute x12 -> x13, waiting for transfers between devices: 8.74 us -> 27.6 us  [moved(): lax.ppermute(value, axis, [(i, (i + distance) % count) for i in range(cou...]
    pallas_call x0 -> x12, Pallas kernels: none -> 17.2 us  [call(): pl.pallas_call(kernel, out_shape=out_shape, in_specs=[SMEM] * smem + [VME...]
    all_to_all x0 -> x1, blocking collectives: none -> 14.4 us  [to_all(): lax.all_to_all(jnp.broadcast_to(value[None], (count,) + value.shape), axi...]
    all_gather x1 -> x0, waiting for transfers between devices: 9.37 us -> none  [shards(): own_blocks = lax.all_gather(masked_shard, 'rhs', axis=2, tiled=True)]
    gather x3 -> x0, local copies, waits for them, and re-layouts: 9.25 us -> none  [shards(): picked = jnp.take(operate_extended, local_pos, axis=0)]
    convert_element_type x1 -> x0, local copies, waits for them, and re-layouts: 9.03 us -> none  [shards(): weave = jnp.einsum('cik,ikab->ciab', onehot, own_blocks, preferred_elemen...]
  transfers between devices with their start and end apart: 13 -> 14, of which waited for: 6 -> 9; matrix products, arithmetic and copies ran while one was open for 14% -> 3% of each run, Pallas kernels for 0% -> 10%
where the time goes in v1:
time: 112 us
  starting transfers between devices  39 us (35%)
  waiting for transfers between devices  34 us (30%)
  Pallas kernels  17.2 us (15%)
  blocking collectives  14.4 us (13%)
  local copies, waits for them, and re-layouts  4.57 us (4%)
  other arithmetic  2.12 us (2%)
    ppermute x13, starting transfers between devices, moved(): lax.ppermute(value, axis, [(i, (i + distance) % count) for i in range(cou...  35.5 us
    ppermute x13, waiting for transfers between devices, moved(): lax.ppermute(value, axis, [(i, (i + distance) % count) for i in range(cou...  27.6 us
    pallas_call x12, Pallas kernels, call(): pl.pallas_call(kernel, out_shape=out_shape, in_specs=[SMEM] * smem + [VME...  17.2 us
    all_to_all x1, blocking collectives, to_all(): lax.all_to_all(jnp.broadcast_to(value[None], (count,) + value.shape), axi...  14.4 us
    all_to_all x1, waiting for transfers between devices, to_all(): lax.all_to_all(jnp.broadcast_to(value[None], (count,) + value.shape), axi...  6.38 us
    all_to_all x1, starting transfers between devices, to_all(): lax.all_to_all(jnp.broadcast_to(value[None], (count,) + value.shape), axi...  3.47 us
    unnamed x10, local copies, waits for them, and re-layouts  3.29 us
  transfers between devices with their start and end apart: 14, of which 9 were waited for; matrix products, arithmetic and copies ran while one was open for 3% of the time, Pallas kernels for 10%

profile of v1, /device:TPU:0, one launch (start us, length us, event | category | flops | bytes accessed | tf_op | source)
XLA Modules:
  0.0 112.0 jit_solution(11286859690960569529)
XLA Ops:
  0.6 0.5 collective-permute-start
  1.1 0.0 copy-start
  1.1 1.0 copy-done
  2.2 0.2 shard_map.68
  2.4 2.6 %collective-permute-start.1 = (bf16[128,1024]{1,0:T(8,128)(2,1)S(1)}, bf16[128,1024]{1,0:T(8,128)(2,1)S(1)}, u32[]{:S(2)}, u32[]{:S(2)}) collective-permute-start(bf16[128,1024]{1,0:T(8,128)(2,1)S(1)} %get-tuple-element.27.v_ref), channel_id=1, source_target_pairs={{0,2},{2,4},{4,6},{6,8},{8,10},{10,12},{12,14},{14,16},{16,18},{18... | collective-permute-start | bytes 786440 | tf_op jit(solution)/shard_map/ppermute | solution.py:177
  5.0 4.1 %collective-permute-start.2 = (bf16[128,1024]{1,0:T(8,128)(2,1)S(1)}, bf16[128,1024]{1,0:T(8,128)(2,1)S(1)}, u32[]{:S(2)}, u32[]{:S(2)}) collective-permute-start(bf16[128,1024]{1,0:T(8,128)(2,1)S(1)} %get-tuple-element.27.v_ref), channel_id=1, source_target_pairs={{0,30},{2,0},{4,2},{6,4},{8,6},{10,8},{12,10},{14,12},{16,14},{18,... | collective-permute-start | bytes 786440 | tf_op jit(solution)/shard_map/ppermute | solution.py:177
  9.0 1.3 %reduce_sum.18 = f32[]{:T(128)} reduce(f32[1024]{0:T(1024)} %param.6, f32[]{:T(128)} %constant.12.clone.1), dimensions={0}, to_apply=%region_0.1 | reduce | flops 1023 | bytes 4104 | tf_op jit(solution)/shard_map/reduce_sum | solution.py:206
  10.3 1.2 %broadcast_in_dim_broadcast_in_dim_broadcast_in_dim.3 = f32[16,1,128]{2,1,0:T(1,128)} broadcast(f32[]{:T(128)} %reduce_sum.18), dimensions={} | broadcast | bytes 8196 | tf_op jit(solution)/shard_map/broadcast_in_dim;broadcast_in_dim;broadcast_in_dim | solution.py:182
  11.6 3.5 %all-to-all-start = ((f32[16,1,128]{2,1,0:T(1,128)}), f32[16,1,128]{2,1,0:T(1,128)S(1)}, u32[]{:S(2)}, u32[]{:S(2)}) async-start(f32[16,1,128]{2,1,0:T(1,128)} %broadcast_in_dim_broadcast_in_dim_broadcast_in_dim.3), calls=%async_computation | async-start | bytes 16384 | tf_op jit(solution)/shard_map/all_to_all | solution.py:182
  15.0 0.7 add_select_fusion.place_ref
  15.7 0.1 pad_add_fusion.offset_ref
  15.8 6.4 %all-to-all-done = f32[16,1,128]{2,1,0:T(1,128)S(1)} async-done(((f32[16,1,128]{2,1,0:T(1,128)}), f32[16,1,128]{2,1,0:T(1,128)S(1)}, u32[]{:S(2)}, u32[]{:S(2)}) %all-to-all-start) | async-done | bytes 8224 | tf_op jit(solution)/shard_map/all_to_all | solution.py:182
  22.2 0.0 collective-permute-done.refs_1_
  22.2 0.0 copy-start.2
  22.2 1.6 %copy-done.2 = bf16[8,16,64,128]{3,2,1,0:T(8,128)(2,1)S(1)} copy-done((bf16[8,16,64,128]{3,2,1,0:T(8,128)(2,1)S(1)}, bf16[8,16,64,128]{3,2,1,0:T(8,128)(2,1)}, u32[]{:S(2)}) %copy-start.2) | copy-done | bytes 2097176
  23.8 0.0 copy-start.3
  23.8 0.7 copy-done.3
  24.5 6.5 %shard_map.69 = (bf16[8,1024,128]{2,1,0:T(8,128)(2,1)S(1)}, bf16[8,1024,128]{2,1,0:T(8,128)(2,1)S(1)}, bf16[8,1024,128]{2,1,0:T(8,128)(2,1)S(1)}) custom-call(s32[8,16]{1,0:T(8,128)S(1)} %add_select_fusion.place_ref, s32[8]{0:T(128)S(1)} %copy-done.3, s32[2]{0:T(128)S(1)} %pad_add_fusion.offset_ref, bf16[8,16,64,128]{3,2,1,0:T(8,128)(2,1)S(1)} %copy-done.2, ...), custom_call_target="tpu_custom_call" | custom-call | tf_op jit(solution)/shard_map/pallas_call | solution.py:18
  31.0 0.0 copy-start.4
  31.0 0.5 shard_map.71
  31.5 0.9 collective-permute-start.3
  32.4 4.8 %collective-permute-start.4 = (bf16[128,1024]{1,0:T(8,128)(2,1)S(1)}, bf16[128,1024]{1,0:T(8,128)(2,1)S(1)}, u32[]{:S(2)}, u32[]{:S(2)}) collective-permute-start(bf16[128,1024]{1,0:T(8,128)(2,1)S(1)} %get-tuple-element.29), channel_id=1, source_target_pairs={{0,30},{2,0},{4,2},{6,4},{8,6},{10,8},{12,10},{14,12},{16,14},{18,... | collective-permute-start | bytes 786440 | tf_op jit(solution)/shard_map/ppermute | solution.py:177
  37.2 0.0 copy-done.4
  37.2 1.1 %shard_map.70.local_ref = f32[128,1024]{1,0:T(8,128)S(1)} custom-call(bf16[8,1024,128]{2,1,0:T(8,128)(2,1)S(1)} %get-tuple-element.26.own_ref, bf16[128,1024]{1,0:T(8,128)(2,1)S(1)} %get-tuple-element.27.v_ref), custom_call_target="tpu_custom_call" | custom-call | tf_op jit(solution)/shard_map/pallas_call | solution.py:18
  38.4 0.0 collective-permute-done.1.vb_ref
  38.4 0.0 collective-permute-done.2.va_ref
  38.4 4.4 %collective-permute-done.3.qb_ref = bf16[128,1024]{1,0:T(8,128)(2,1)S(1)} collective-permute-done((bf16[128,1024]{1,0:T(8,128)(2,1)S(1)}, bf16[128,1024]{1,0:T(8,128)(2,1)S(1)}, u32[]{:S(2)}, u32[]{:S(2)}) %collective-permute-start.3) | collective-permute-done | bytes 262176 | tf_op jit(solution)/shard_map/ppermute | solution.py:177
  42.8 1.5 %collective-permute-done.4.qa_ref = bf16[128,1024]{1,0:T(8,128)(2,1)S(1)} collective-permute-done((bf16[128,1024]{1,0:T(8,128)(2,1)S(1)}, bf16[128,1024]{1,0:T(8,128)(2,1)S(1)}, u32[]{:S(2)}, u32[]{:S(2)}) %collective-permute-start.4) | collective-permute-done | bytes 262176 | tf_op jit(solution)/shard_map/ppermute | solution.py:177
  44.4 1.2 %shard_map.72 = (f32[128,1024]{1,0:T(8,128)S(1)}, bf16[128,1024]{1,0:T(8,128)(2,1)S(1)}, f32[2,128]{1,0:T(2,128)S(1)}) custom-call(bf16[8,1024,128]{2,1,0:T(8,128)(2,1)S(1)} %get-tuple-element.23.before_ref, bf16[8,1024,128]{2,1,0:T(8,128)(2,1)S(1)} %get-tuple-element.24.after_ref, f32[1,1024]{1,0:T(1,128)S(1)} %bitcast.8, ...), custom_call_target="tpu_custom_call" | custom-call | tf_op jit(solution)/shard_map/pallas_call | solution.py:18
  45.5 1.0 collective-permute-start.5
  46.5 4.7 %collective-permute-start.6 = (bf16[128,1024]{1,0:T(8,128)(2,1)S(1)}, bf16[128,1024]{1,0:T(8,128)(2,1)S(1)}, u32[]{:S(2)}, u32[]{:S(2)}) collective-permute-start(bf16[128,1024]{1,0:T(8,128)(2,1)S(1)} %get-tuple-element.32.v_ref), channel_id=1, source_target_pairs={{0,30},{2,0},{4,2},{6,4},{8,6},{10,8},{12,10},{14,12},{16,14},{18,... | collective-permute-start | bytes 786440 | tf_op jit(solution)/shard_map/ppermute | solution.py:177
  51.2 0.5 shard_map.74
  51.8 0.1 collective-permute-start.7
  51.8 5.6 %collective-permute-start.8 = (bf16[128,1024]{1,0:T(8,128)(2,1)S(1)}, bf16[128,1024]{1,0:T(8,128)(2,1)S(1)}, u32[]{:S(2)}, u32[]{:S(2)}) collective-permute-start(bf16[128,1024]{1,0:T(8,128)(2,1)S(1)} %get-tuple-element.34), channel_id=1, source_target_pairs={{0,30},{2,0},{4,2},{6,4},{8,6},{10,8},{12,10},{14,12},{16,14},{18,... | collective-permute-start | bytes 786440 | tf_op jit(solution)/shard_map/ppermute | solution.py:177
  57.4 1.1 %shard_map.73.local_ref = f32[128,1024]{1,0:T(8,128)S(1)} custom-call(bf16[8,1024,128]{2,1,0:T(8,128)(2,1)S(1)} %get-tuple-element.26.own_ref, bf16[128,1024]{1,0:T(8,128)(2,1)S(1)} %get-tuple-element.32.v_ref), custom_call_target="tpu_custom_call" | custom-call | tf_op jit(solution)/shard_map/pallas_call | solution.py:18
  58.6 5.7 %collective-permute-done.5.vb_ref = bf16[128,1024]{1,0:T(8,128)(2,1)S(1)} collective-permute-done((bf16[128,1024]{1,0:T(8,128)(2,1)S(1)}, bf16[128,1024]{1,0:T(8,128)(2,1)S(1)}, u32[]{:S(2)}, u32[]{:S(2)}) %collective-permute-start.5) | collective-permute-done | bytes 262176 | tf_op jit(solution)/shard_map/ppermute | solution.py:177
  64.2 0.0 collective-permute-done.6.va_ref
  64.3 3.0 %collective-permute-done.7.qb_ref = bf16[128,1024]{1,0:T(8,128)(2,1)S(1)} collective-permute-done((bf16[128,1024]{1,0:T(8,128)(2,1)S(1)}, bf16[128,1024]{1,0:T(8,128)(2,1)S(1)}, u32[]{:S(2)}, u32[]{:S(2)}) %collective-permute-start.7) | collective-permute-done | bytes 262176 | tf_op jit(solution)/shard_map/ppermute | solution.py:177
  67.3 2.9 %collective-permute-done.8.qa_ref = bf16[128,1024]{1,0:T(8,128)(2,1)S(1)} collective-permute-done((bf16[128,1024]{1,0:T(8,128)(2,1)S(1)}, bf16[128,1024]{1,0:T(8,128)(2,1)S(1)}, u32[]{:S(2)}, u32[]{:S(2)}) %collective-permute-start.8) | collective-permute-done | bytes 262176 | tf_op jit(solution)/shard_map/ppermute | solution.py:177
  70.2 1.2 %shard_map.75 = (f32[128,1024]{1,0:T(8,128)S(1)}, bf16[128,1024]{1,0:T(8,128)(2,1)S(1)}, f32[2,128]{1,0:T(2,128)S(1)}) custom-call(bf16[8,1024,128]{2,1,0:T(8,128)(2,1)S(1)} %get-tuple-element.23.before_ref, bf16[8,1024,128]{2,1,0:T(8,128)(2,1)S(1)} %get-tuple-element.24.after_ref, f32[1,1024]{1,0:T(1,128)S(1)} %bitcast.9, ...), custom_call_target="tpu_custom_call" | custom-call | tf_op jit(solution)/shard_map/pallas_call | solution.py:18
  71.4 0.3 collective-permute-start.9
  71.7 5.3 %collective-permute-start.10 = (bf16[128,1024]{1,0:T(8,128)(2,1)S(1)}, bf16[128,1024]{1,0:T(8,128)(2,1)S(1)}, u32[]{:S(2)}, u32[]{:S(2)}) collective-permute-start(bf16[128,1024]{1,0:T(8,128)(2,1)S(1)} %get-tuple-element.37.v_ref), channel_id=1, source_target_pairs={{0,30},{2,0},{4,2},{6,4},{8,6},{10,8},{12,10},{14,12},{16,14},{18,... | collective-permute-start | bytes 786440 | tf_op jit(solution)/shard_map/ppermute | solution.py:177
  77.0 0.5 shard_map.77
  77.6 0.1 collective-permute-start.11
  77.7 5.6 %collective-permute-start.12 = (bf16[128,1024]{1,0:T(8,128)(2,1)S(1)}, bf16[128,1024]{1,0:T(8,128)(2,1)S(1)}, u32[]{:S(2)}, u32[]{:S(2)}) collective-permute-start(bf16[128,1024]{1,0:T(8,128)(2,1)S(1)} %get-tuple-element.39), channel_id=1, source_target_pairs={{0,30},{2,0},{4,2},{6,4},{8,6},{10,8},{12,10},{14,12},{16,14},{18,... | collective-permute-start | bytes 786440 | tf_op jit(solution)/shard_map/ppermute | solution.py:177
  83.3 1.1 shard_map.76.local_ref
  84.4 3.1 %collective-permute-done.9.vb_ref = bf16[128,1024]{1,0:T(8,128)(2,1)S(1)} collective-permute-done((bf16[128,1024]{1,0:T(8,128)(2,1)S(1)}, bf16[128,1024]{1,0:T(8,128)(2,1)S(1)}, u32[]{:S(2)}, u32[]{:S(2)}) %collective-permute-start.9) | collective-permute-done | bytes 262176 | tf_op jit(solution)/shard_map/ppermute | solution.py:177
  87.5 0.0 collective-permute-done.10.va_ref
  87.5 4.9 %collective-permute-done.11.qb_ref = bf16[128,1024]{1,0:T(8,128)(2,1)S(1)} collective-permute-done((bf16[128,1024]{1,0:T(8,128)(2,1)S(1)}, bf16[128,1024]{1,0:T(8,128)(2,1)S(1)}, u32[]{:S(2)}, u32[]{:S(2)}) %collective-permute-start.11) | collective-permute-done | bytes 262176 | tf_op jit(solution)/shard_map/ppermute | solution.py:177
  92.4 1.9 %collective-permute-done.12.qa_ref = bf16[128,1024]{1,0:T(8,128)(2,1)S(1)} collective-permute-done((bf16[128,1024]{1,0:T(8,128)(2,1)S(1)}, bf16[128,1024]{1,0:T(8,128)(2,1)S(1)}, u32[]{:S(2)}, u32[]{:S(2)}) %collective-permute-start.12) | collective-permute-done | bytes 262176 | tf_op jit(solution)/shard_map/ppermute | solution.py:177
  94.4 0.0 copy-start.1
  94.4 1.8 %shard_map.78 = (f32[128,1024]{1,0:T(8,128)S(1)}, bf16[128,1024]{1,0:T(8,128)(2,1)}, f32[2,128]{1,0:T(2,128)S(1)}) custom-call(bf16[8,1024,128]{2,1,0:T(8,128)(2,1)S(1)} %get-tuple-element.23.before_ref, bf16[8,1024,128]{2,1,0:T(8,128)(2,1)S(1)} %get-tuple-element.24.after_ref, f32[1,1024]{1,0:T(1,128)S(1)} %bitcast.10, ...), custom_call_target="tpu_custom_call" | custom-call | tf_op jit(solution)/shard_map/pallas_call | solution.py:18
  96.2 14.4 %all_to_all.10.moment_ref = f32[16,8,128]{2,1,0:T(8,128)S(1)} all-to-all(f32[16,8,128]{2,1,0:T(8,128)S(1)} %broadcast_in_dim.5), channel_id=1, replica_groups=mesh['asset'=16,'rhs'=2] {'asset'}, dimensions={0} | all-to-all | bytes 131072 | tf_op jit(solution)/shard_map/all_to_all | solution.py:182
  110.6 0.0 copy-done.1
  110.6 1.4 %shard_map.79 = (f32[1024,128]{1,0:T(8,128)}, f32[1024,128]{1,0:T(8,128)}) custom-call(f32[1,128]{1,0:T(1,128)S(1)} %multiply_bitcast_fusion.shift_ref, f32[16,8,128]{2,1,0:T(8,128)S(1)} %all_to_all.10.moment_ref, f32[1024,128]{1,0:T(8,128)S(1)} %copy-done.1, f32[128,1024]{1,0:T(8,128)S(1)} %get-tuple-element.31.k_ref.k1_ref, ...), custom_call_target="tpu_custom_call" | custom-call | tf_op jit(solution)/shard_map/pallas_call | solution.py:18
  (6 shorter events, 0.1 us)
Async XLA Ops:
  0.6 21.6 %collective-permute-start = (bf16[8,16,64,128]{3,2,1,0:T(8,128)(2,1)}, bf16[8,16,64,128]{3,2,1,0:T(8,128)(2,1)S(1)}, u32[]{:S(2)}, u32[]{:S(2)}) collective-permute-start(bf16[8,16,64,128]{3,2,1,0:T(8,128)(2,1)} %refs_0_.1), channel_id=1, source_target_pairs={{0,1},{1,0},{2,3},{3,2},{4,5},{5,4},{6,7},{7,6},{8,9},{9,8},{10,11... | collective-permute-start | bytes 6291464 | tf_op jit(solution)/shard_map/ppermute | solution.py:177
  1.1 1.0 copy-start
  2.4 36.0 %collective-permute-start.1 = (bf16[128,1024]{1,0:T(8,128)(2,1)S(1)}, bf16[128,1024]{1,0:T(8,128)(2,1)S(1)}, u32[]{:S(2)}, u32[]{:S(2)}) collective-permute-start(bf16[128,1024]{1,0:T(8,128)(2,1)S(1)} %get-tuple-element.27.v_ref), channel_id=1, source_target_pairs={{0,2},{2,4},{4,6},{6,8},{8,10},{10,12},{12,14},{14,16},{16,18},{18... | collective-permute-start | bytes 786440 | tf_op jit(solution)/shard_map/ppermute | solution.py:177
  5.0 33.4 %collective-permute-start.2 = (bf16[128,1024]{1,0:T(8,128)(2,1)S(1)}, bf16[128,1024]{1,0:T(8,128)(2,1)S(1)}, u32[]{:S(2)}, u32[]{:S(2)}) collective-permute-start(bf16[128,1024]{1,0:T(8,128)(2,1)S(1)} %get-tuple-element.27.v_ref), channel_id=1, source_target_pairs={{0,30},{2,0},{4,2},{6,4},{8,6},{10,8},{12,10},{14,12},{16,14},{18,... | collective-permute-start | bytes 786440 | tf_op jit(solution)/shard_map/ppermute | solution.py:177
  11.6 10.6 %all-to-all-start = ((f32[16,1,128]{2,1,0:T(1,128)}), f32[16,1,128]{2,1,0:T(1,128)S(1)}, u32[]{:S(2)}, u32[]{:S(2)}) async-start(f32[16,1,128]{2,1,0:T(1,128)} %broadcast_in_dim_broadcast_in_dim_broadcast_in_dim.3), calls=%async_computation | async-start | bytes 16384 | tf_op jit(solution)/shard_map/all_to_all | solution.py:182
  22.2 1.6 %copy-start.2 = (bf16[8,16,64,128]{3,2,1,0:T(8,128)(2,1)S(1)}, bf16[8,16,64,128]{3,2,1,0:T(8,128)(2,1)}, u32[]{:S(2)}) copy-start(bf16[8,16,64,128]{3,2,1,0:T(8,128)(2,1)} %refs_0_.1) | copy-start | bytes 6291460
  23.8 0.7 copy-start.3
  31.0 6.2 %copy-start.4 = (f32[1024]{0:T(1024)S(1)}, f32[1024]{0:T(1024)}, u32[]{:S(2)}) copy-start(f32[1024]{0:T(1024)} %param.6) | copy-start | bytes 12292
  31.5 11.3 %collective-permute-start.3 = (bf16[128,1024]{1,0:T(8,128)(2,1)S(1)}, bf16[128,1024]{1,0:T(8,128)(2,1)S(1)}, u32[]{:S(2)}, u32[]{:S(2)}) collective-permute-start(bf16[128,1024]{1,0:T(8,128)(2,1)S(1)} %get-tuple-element.28), channel_id=1, source_target_pairs={{0,2},{2,4},{4,6},{6,8},{8,10},{10,12},{12,14},{14,16},{16,18},{18... | collective-permute-start | bytes 786440 | tf_op jit(solution)/shard_map/ppermute | solution.py:177
  32.4 12.0 %collective-permute-start.4 = (bf16[128,1024]{1,0:T(8,128)(2,1)S(1)}, bf16[128,1024]{1,0:T(8,128)(2,1)S(1)}, u32[]{:S(2)}, u32[]{:S(2)}) collective-permute-start(bf16[128,1024]{1,0:T(8,128)(2,1)S(1)} %get-tuple-element.29), channel_id=1, source_target_pairs={{0,30},{2,0},{4,2},{6,4},{8,6},{10,8},{12,10},{14,12},{16,14},{18,... | collective-permute-start | bytes 786440 | tf_op jit(solution)/shard_map/ppermute | solution.py:177
  45.5 18.7 %collective-permute-start.5 = (bf16[128,1024]{1,0:T(8,128)(2,1)S(1)}, bf16[128,1024]{1,0:T(8,128)(2,1)S(1)}, u32[]{:S(2)}, u32[]{:S(2)}) collective-permute-start(bf16[128,1024]{1,0:T(8,128)(2,1)S(1)} %get-tuple-element.32.v_ref), channel_id=1, source_target_pairs={{0,2},{2,4},{4,6},{6,8},{8,10},{10,12},{12,14},{14,16},{16,18},{18... | collective-permute-start | bytes 786440 | tf_op jit(solution)/shard_map/ppermute | solution.py:177
  46.5 17.7 %collective-permute-start.6 = (bf16[128,1024]{1,0:T(8,128)(2,1)S(1)}, bf16[128,1024]{1,0:T(8,128)(2,1)S(1)}, u32[]{:S(2)}, u32[]{:S(2)}) collective-permute-start(bf16[128,1024]{1,0:T(8,128)(2,1)S(1)} %get-tuple-element.32.v_ref), channel_id=1, source_target_pairs={{0,30},{2,0},{4,2},{6,4},{8,6},{10,8},{12,10},{14,12},{16,14},{18,... | collective-permute-start | bytes 786440 | tf_op jit(solution)/shard_map/ppermute | solution.py:177
  51.8 15.5 %collective-permute-start.7 = (bf16[128,1024]{1,0:T(8,128)(2,1)S(1)}, bf16[128,1024]{1,0:T(8,128)(2,1)S(1)}, u32[]{:S(2)}, u32[]{:S(2)}) collective-permute-start(bf16[128,1024]{1,0:T(8,128)(2,1)S(1)} %get-tuple-element.33), channel_id=1, source_target_pairs={{0,2},{2,4},{4,6},{6,8},{8,10},{10,12},{12,14},{14,16},{16,18},{18... | collective-permute-start | bytes 786440 | tf_op jit(solution)/shard_map/ppermute | solution.py:177
  51.8 18.4 %collective-permute-start.8 = (bf16[128,1024]{1,0:T(8,128)(2,1)S(1)}, bf16[128,1024]{1,0:T(8,128)(2,1)S(1)}, u32[]{:S(2)}, u32[]{:S(2)}) collective-permute-start(bf16[128,1024]{1,0:T(8,128)(2,1)S(1)} %get-tuple-element.34), channel_id=1, source_target_pairs={{0,30},{2,0},{4,2},{6,4},{8,6},{10,8},{12,10},{14,12},{16,14},{18,... | collective-permute-start | bytes 786440 | tf_op jit(solution)/shard_map/ppermute | solution.py:177
  71.4 16.2 %collective-permute-start.9 = (bf16[128,1024]{1,0:T(8,128)(2,1)S(1)}, bf16[128,1024]{1,0:T(8,128)(2,1)S(1)}, u32[]{:S(2)}, u32[]{:S(2)}) collective-permute-start(bf16[128,1024]{1,0:T(8,128)(2,1)S(1)} %get-tuple-element.37.v_ref), channel_id=1, source_target_pairs={{0,2},{2,4},{4,6},{6,8},{8,10},{10,12},{12,14},{14,16},{16,18},{18... | collective-permute-start | bytes 786440 | tf_op jit(solution)/shard_map/ppermute | solution.py:177
  71.7 15.8 %collective-permute-start.10 = (bf16[128,1024]{1,0:T(8,128)(2,1)S(1)}, bf16[128,1024]{1,0:T(8,128)(2,1)S(1)}, u32[]{:S(2)}, u32[]{:S(2)}) collective-permute-start(bf16[128,1024]{1,0:T(8,128)(2,1)S(1)} %get-tuple-element.37.v_ref), channel_id=1, source_target_pairs={{0,30},{2,0},{4,2},{6,4},{8,6},{10,8},{12,10},{14,12},{16,14},{18,... | collective-permute-start | bytes 786440 | tf_op jit(solution)/shard_map/ppermute | solution.py:177
  77.6 14.9 %collective-permute-start.11 = (bf16[128,1024]{1,0:T(8,128)(2,1)S(1)}, bf16[128,1024]{1,0:T(8,128)(2,1)S(1)}, u32[]{:S(2)}, u32[]{:S(2)}) collective-permute-start(bf16[128,1024]{1,0:T(8,128)(2,1)S(1)} %get-tuple-element.38), channel_id=1, source_target_pairs={{0,2},{2,4},{4,6},{6,8},{8,10},{10,12},{12,14},{14,16},{16,18},{18... | collective-permute-start | bytes 786440 | tf_op jit(solution)/shard_map/ppermute | solution.py:177
  77.7 16.7 %collective-permute-start.12 = (bf16[128,1024]{1,0:T(8,128)(2,1)S(1)}, bf16[128,1024]{1,0:T(8,128)(2,1)S(1)}, u32[]{:S(2)}, u32[]{:S(2)}) collective-permute-start(bf16[128,1024]{1,0:T(8,128)(2,1)S(1)} %get-tuple-element.39), channel_id=1, source_target_pairs={{0,30},{2,0},{4,2},{6,4},{8,6},{10,8},{12,10},{14,12},{16,14},{18,... | collective-permute-start | bytes 786440 | tf_op jit(solution)/shard_map/ppermute | solution.py:177
  94.4 16.2 %copy-start.1 = (f32[1024,128]{1,0:T(8,128)S(1)}, f32[1024,128]{1,0:T(8,128)}, u32[]{:S(2)}) copy-start(f32[1024,128]{1,0:T(8,128)} %targets_ref.3) | copy-start | bytes 1572868

commit v2 on v1

v2 whole, which is shorter than its diff:
```python
import jax
import jax.numpy as jnp
from jax import lax
from jax.experimental import pallas as pl
from jax.experimental.pallas import tpu as pltpu
from jax.sharding import PartitionSpec as P

F32 = jnp.float32
BF16 = jnp.bfloat16
VMEM = pl.BlockSpec(memory_space=pltpu.VMEM)
SMEM = pl.BlockSpec(memory_space=pltpu.SMEM)
LIMIT = 8 * 1024 * 1024
HBM = pl.BlockSpec(memory_space=pltpu.HBM)
NN = (((1,), (0,)), ((), ()))
NT = (((1,), (1,)), ((), ()))


def call(kernel, out_shape, args, smem=0, outside=(), scratch=(), aliases=None):
    specs = [SMEM] * smem + [VMEM] * (len(args) - smem)
    for at in outside:
        specs[at] = HBM
    return pl.pallas_call(
        kernel,
        out_shape=out_shape,
        in_specs=specs,
        out_specs=jax.tree.map(lambda _: VMEM, out_shape),
        scratch_shapes=scratch,
        input_output_aliases=aliases or {},
        compiler_params=pltpu.CompilerParams(vmem_limit_bytes=LIMIT),
    )(*args)


def column_sums(values, width):
    folded = values[:, :width]
    for at in range(width, values.shape[1], width):
        folded = folded + values[:, at : at + width]
    return jnp.sum(folded.T, axis=0, keepdims=True)


def prepare_kernel(targets_ref, ridge_ref, base_ref, message_ref, moment_ref):
    assets, cols = targets_ref.shape
    width = moment_ref.shape[1]
    for at in range(0, assets, width):
        tile = targets_ref[at : at + width, :].T
        base_ref[:, at : at + width] = tile
        message_ref[:cols, at : at + width] = tile.astype(BF16)
    values = targets_ref[...]
    moment_ref[...] = jnp.sum(values * values, axis=0, keepdims=True)
    mean = jnp.sum(ridge_ref[...], axis=1, keepdims=True) / assets
    rest = message_ref.shape[0] - cols
    message_ref[cols:, :] = jnp.broadcast_to(mean, (rest, assets)).astype(BF16)


def place_blocks(col_ref, length_ref, offset, part_ref, band_ref):
    rows, slots, height, width = part_ref.shape
    spare = band_ref.shape[0] - 1
    total = rows * lax.axis_size("asset")
    first = lax.axis_index("asset") * rows - rows

    def one_row(row, carry):
        at = pl.ds(pl.multiple_of(row * width + offset, height), height)
        for slot in range(slots):
            place = col_ref[row, slot] - first
            place = jnp.where(place < 0, place + total, place)
            place = jnp.where(place >= total, place - total, place)
            place = jnp.where(slot < length_ref[row], place, spare)
            band_ref[place, at, :] = part_ref[row, slot]
        return carry

    lax.fori_loop(0, rows, one_row, 0)


def spread_first_kernel(col_ref, length_ref, part_ref, band_ref):
    band_ref[...] = jnp.zeros_like(band_ref)
    height = part_ref.shape[2]
    mine = 0 if height == part_ref.shape[3] else lax.axis_index("rhs") * height
    place_blocks(col_ref, length_ref, mine, part_ref, band_ref)


def spread_other_kernel(col_ref, length_ref, part_ref, _, band_ref):
    height = part_ref.shape[2]
    place_blocks(col_ref, length_ref, (1 - lax.axis_index("rhs")) * height, part_ref, band_ref)


def is_odd(dims):
    return jnp.full(dims, lax.axis_index("asset") % 2, jnp.int32) == 1


def columns(ref, first, last, rows):
    return jnp.concatenate([ref[c, rows, :] for c in range(first, last)], axis=1)


def products_kernel(band_ref, v_ref, near_ref, far_ref):
    places, _, width = band_ref.shape
    rows = places // 3
    cols = near_ref.shape[0]
    odd = is_odd((cols, 2 * width))
    for j in range(0, rows, 2):
        out = slice(j * width, (j + 2) * width)
        low = slice(0, (j + 2) * width)
        high = slice(j * width, rows * width)
        before = lax.dot_general(
            v_ref[:cols, low], columns(band_ref, j, j + 2, low), NN, preferred_element_type=F32
        )
        after = lax.dot_general(
            v_ref[:cols, high],
            columns(band_ref, 2 * rows + j, 2 * rows + j + 2, high),
            NN,
            preferred_element_type=F32,
        )
        near_ref[:, out] = jnp.where(odd, before, after).astype(BF16)
        far_ref[:, out] = jnp.where(odd, after, before).astype(BF16)


def products_third_kernel(
    band_ref, shift_ref, mean_ref, near1_ref, far1_ref, v_ref, near_ref, far_ref, near2_ref, far2_ref
):
    products_kernel(band_ref, v_ref, near2_ref, far2_ref)
    gap = 2 * (mean_ref[0:1, 0:1] - shift_ref[0:1, 0:1])
    near_ref[...] = (near2_ref[...].astype(F32) + gap * near1_ref[...].astype(F32)).astype(BF16)
    far_ref[...] = (far2_ref[...].astype(F32) + gap * far1_ref[...].astype(F32)).astype(BF16)


def local_kernel(band_ref, v_ref, out_ref):
    places, _, width = band_ref.shape
    rows = places // 3
    cols = out_ref.shape[0]
    every = slice(0, rows * width)
    for j in range(0, rows, 2):
        out = slice(j * width, (j + 2) * width)
        out_ref[:, out] = lax.dot_general(
            v_ref[:cols, :],
            columns(band_ref, rows + j, rows + j + 2, every),
            NN,
            preferred_element_type=F32,
        ) + lax.dot_general(
            v_ref[:cols, :], columns(band_ref, rows, 2 * rows, out), NT, preferred_element_type=F32
        )


def neighbours(near_ref, far_ref, cols):
    near, far = near_ref[:cols, :].astype(F32), far_ref[:cols, :].astype(F32)
    odd = is_odd(near.shape)
    return jnp.where(odd, near, far).astype(BF16), jnp.where(odd, far, near).astype(BF16)


def forward_products(band_ref, before, after, j):
    places, _, width = band_ref.shape
    rows = places // 3
    out = slice(j * width, (j + 2) * width)
    return out, lax.dot_general(
        before[:, j * width :], columns(band_ref, j, rows, out), NT, preferred_element_type=F32
    ), lax.dot_general(
        after[:, : (j + 2) * width],
        columns(band_ref, 2 * rows, 2 * rows + j + 2, out),
        NT,
        preferred_element_type=F32,
    )


def cross_first_kernel(
    band_ref, ridge_ref, k_ref, local_ref, own_ref, near_ref, far_ref,
    sum_ref, before_ref, after_ref, mean_ref
):
    cols, width = k_ref.shape[0], mean_ref.shape[1]
    before, after = neighbours(near_ref, far_ref, cols)
    means = [ref[cols : cols + 8, :width].astype(F32)[:1] for ref in (own_ref, near_ref, far_ref)]
    odd = is_odd(means[0].shape)
    means += [jnp.where(odd, means[1], means[2]), jnp.where(odd, means[2], means[1])]
    means.append(means[0] + means[1])
    for i, value in enumerate(means):
        mean_ref[i : i + 1, :] = value
    for j in range(0, band_ref.shape[0] // 3, 2):
        out, first, second = forward_products(band_ref, before, after, j)
        before_ref[:, out] = first
        after_ref[:, out] = second
        sum_ref[:, out] = ridge_ref[:, out] * k_ref[:, out] + 0.5 * (local_ref[:, out] + first + second)


def finish_first_kernel(k_ref, mean_ref, sum_ref, near_ref, far_ref, next_ref, rounded_ref):
    value = sum_ref[...] + 0.5 * (near_ref[...].astype(F32) + far_ref[...].astype(F32))
    next_ref[...] = value
    rounded_ref[...] = (value - mean_ref[0:1, 0:1] * k_ref[...]).astype(BF16)


def cross_second_kernel(
    band_ref, ridge_ref, mean_ref, k_ref, local0_ref, local_ref, before0_ref, after0_ref, qn0_ref, qf0_ref,
    near_ref, far_ref, sum_ref, before_ref, after_ref
):
    own, mean_near, mean_far, mean_before, mean_after = (mean_ref[i : i + 1, 0:1] for i in range(5))
    before, after = neighbours(near_ref, far_ref, k_ref.shape[0])
    for j in range(0, band_ref.shape[0] // 3, 2):
        out, first, second = forward_products(band_ref, before, after, j)
        before_ref[:, out] = first
        after_ref[:, out] = second
        known = own * local0_ref[:, out] + mean_before * before0_ref[:, out] + mean_after * after0_ref[:, out]
        known = known + mean_near * qn0_ref[:, out].astype(F32) + mean_far * qf0_ref[:, out].astype(F32)
        both = local_ref[:, out] + first + second + known
        sum_ref[:, out] = ridge_ref[:, out] * k_ref[:, out] + 0.5 * both


def finish_second_kernel(k0_ref, k_ref, mean_ref, sum_ref, q_ref, next_ref, rounded_ref):
    value = sum_ref[...] + 0.5 * q_ref[...].astype(F32)
    next_ref[...] = value
    own = mean_ref[0:1, 0:1]
    rounded_ref[...] = (value - 2 * own * k_ref[...] + own * own * k0_ref[...]).astype(BF16)


def settle_kernel(shift_ref, k0_ref, k1_ref, k2_ref, s1_ref, s2_ref, moment_ref):
    width = moment_ref.shape[1]
    c = shift_ref[0:1, 0:1]
    k0, k1 = k0_ref[...], k1_ref[...]
    s1 = k1 - c * k0
    s2 = k2_ref[...] - 2 * c * k1 + c * c * k0
    s1_ref[...] = s1
    s2_ref[...] = s2
    for i, value in enumerate((k0 * s1, s1 * s1, s1 * s2, s2 * s2)):
        moment_ref[i : i + 1, :] = column_sums(value, width)


def cross_third_kernel(
    band_ref, ridge_ref, shift_ref, mean_ref, k_ref, local0_ref, local1_ref, local_ref,
    before0_ref, before1_ref, after0_ref, after1_ref, qn0_ref, qf0_ref,
    near_ref, far_ref, sum_ref, form_ref
):
    width = form_ref.shape[1]
    c = shift_ref[0:1, 0:1]
    own, mean_near, mean_far, mean_before, mean_after = (mean_ref[i : i + 1, 0:1] - c for i in range(5))
    before, after = neighbours(near_ref, far_ref, k_ref.shape[0])
    form = jnp.zeros((k_ref.shape[0], width), F32)

    def known(gap, zeroth_ref, first_ref, out):
        zeroth, first = zeroth_ref[:, out].astype(F32), first_ref[:, out].astype(F32)
        return 2 * gap * first + gap * gap * zeroth

    for j in range(0, band_ref.shape[0] // 3, 2):
        out, first, second = forward_products(band_ref, before, after, j)
        first = first + known(mean_before, before0_ref, before1_ref, out)
        second = second + known(mean_after, after0_ref, after1_ref, out)
        local = local_ref[:, out] + known(own, local0_ref, local1_ref, out)
        back = mean_near * mean_near * qn0_ref[:, out].astype(F32)
        back = back + mean_far * mean_far * qf0_ref[:, out].astype(F32)
        mine = (ridge_ref[:, out] - c) * k_ref[:, out] + 0.5 * local
        sum_ref[:, out] = mine + 0.5 * (first + second + back)
        part = k_ref[:, out] * (mine + first + second)
        form = form + part[:, :width] + part[:, width:]
    form_ref[...] = jnp.sum(form.T, axis=0, keepdims=True)


def finish_third_kernel(sum_ref, q_ref, next_ref):
    next_ref[...] = sum_ref[...] + 0.5 * q_ref[...].astype(F32)


def share(above, below):
    return jnp.where(below == 0, 0.0, above / below)


def scalars(m, shift, iters):
    zero = jnp.zeros_like(m[0])
    solution = [zero] * iters
    residual = [zero + 1.0] + [zero] * iters
    direction = [zero + 1.0] + [zero] * (iters - 1)

    def inner(a, b):
        total = zero
        for i, left in enumerate(a):
            for j, right in enumerate(b):
                if i + j < len(m):
                    total = total + left * right * m[i + j]
        return total

    now = m[0]
    for step in range(iters):
        used = direction[: step + 1]
        image = [shift * value for value in used] + [zero]
        for i, value in enumerate(used):
            image[i + 1] = image[i + 1] + value
        alpha = share(now, inner(used, image))
        for i, value in enumerate(used):
            solution[i] = solution[i] + alpha * value
        for i, value in enumerate(image):
            residual[i] = residual[i] - alpha * value
        if step + 1 < iters:
            left = residual[: step + 2]
            new = inner(left, left)
            beta = share(new, now)
            direction = [r + beta * d for r, d in zip(residual[:iters], direction, strict=True)]
            now = new
    return solution, residual


def combine_kernel(shift_ref, moment_ref, targets_ref, k1_ref, k2_ref, k3_ref, solution_ref, residual_ref):
    width = moment_ref.shape[1]
    m = [moment_ref[i : i + 1, :] for i in range(6)]
    x, r = scalars(m, shift_ref[...], 3)
    for at in range(0, targets_ref.shape[0], width):
        out = slice(at, at + width)
        k0 = targets_ref[out, :]
        k1, k2, k3 = k1_ref[:, out].T, k2_ref[:, out].T, k3_ref[:, out].T
        solution_ref[out, :] = x[0] * k0 + x[1] * k1 + x[2] * k2
        residual_ref[out, :] = r[0] * k0 + r[1] * k1 + r[2] * k2 + r[3] * k3


def near(value):
    count = lax.axis_size("asset")
    return lax.ppermute(value, "asset", [(i, i ^ 1) for i in range(count)])


def far(value):
    count = lax.axis_size("asset")
    return lax.ppermute(
        value, "asset", [(i, (i + 1 if i % 2 else i - 1) % count) for i in range(count)]
    )


def back(value):
    count = lax.axis_size("asset")
    return lax.ppermute(
        value, "asset", [(i, (i + 2 if i % 2 else i - 2) % count) for i in range(count)]
    )


def joined(to_near, to_far):
    return near((to_near.astype(F32) + back(to_far).astype(F32)).astype(BF16))


def sum_step(value, axis, distance):
    count = lax.axis_size(axis)
    return value + lax.ppermute(value, axis, [(i, i ^ distance) for i in range(count)])


def sum_over(value, axis):
    count = lax.axis_size(axis)
    step = 1
    while step < count:
        total = value
        for distance in (step, 2 * step, 3 * step) if 2 * step < count else (step,):
            route = [(i, i ^ distance) for i in range(count)]
            total = total + lax.ppermute(value, axis, route)
        value = total
        step *= 4
    return value


def together(*values):
    return lax.optimization_barrier(values)


def shards(targets, ridge, blocks, col_index, row_length):
    rows, slots, height, width = blocks.shape
    cols = targets.shape[1]
    assets = rows * width
    devices = lax.axis_size("asset")
    halves = lax.axis_size("rhs")
    ridge = ridge[None, :]

    def shape(kind, *dims):
        return jax.ShapeDtypeStruct(dims, kind)

    field, rounded, row = shape(F32, cols, assets), shape(BF16, cols, assets), shape(F32, 1, cols)
    band_shape = shape(BF16, 3 * rows + 1, assets, width)
    if halves == 2:
        part, other = blocks, lax.ppermute(blocks, "rhs", [(0, 1), (1, 0)])
    else:
        part, other = lax.all_gather(blocks, "rhs", axis=2, tiled=True), None

    k0, v0, m0 = call(prepare_kernel, (field, shape(BF16, cols + 16, assets), row), (targets, ridge))
    near0, far0 = near(v0), far(v0)
    band = call(spread_first_kernel, band_shape, (col_index, row_length, part), smem=2)
    if other is not None:
        band = call(
            spread_other_kernel, band_shape, (col_index, row_length, other, band), smem=2, aliases={3: 0}
        )
    distances = [1 << i for i in range(1, (devices - 1).bit_length())]
    pieces = (field,) * 3

    to_near, to_far = call(products_kernel, (rounded,) * 2, (band, v0))
    qf0, qn0 = far(to_far), near(to_near)
    local0 = call(local_kernel, field, (band, v0))
    partial, before0, after0, means = call(
        cross_first_kernel,
        (*pieces, shape(F32, 8, width)),
        (band, ridge, k0, local0, v0, near0, far0),
    )
    mean = sum_step(means[5:6], "asset", distances[0])
    mean, partial = together(mean, partial)
    k1, v1 = call(finish_first_kernel, (field, rounded), (k0, means, partial, qn0, qf0))

    to_near1, to_far1 = call(products_kernel, (rounded,) * 2, (band, v1))
    far1, near1 = far(v1), near(v1)
    q1 = joined(to_near1, to_far1)
    local1 = call(local_kernel, field, (band, v1))
    mean, _ = together(mean, v1)
    for distance in distances[1:-1]:
        mean = sum_step(mean, "asset", distance)
    partial, before1, after1 = call(
        cross_second_kernel,
        pieces,
        (band, ridge, means, k1, local0, local1, before0, after0, qn0, qf0, near1, far1),
    )
    mean, _ = together(mean, partial)
    shift = sum_step(mean, "asset", distances[-1]) / devices
    k2, v2 = call(finish_second_kernel, (field, rounded), (k0, k1, means, partial, q1))

    far2, near2 = far(v2), near(v2)
    to_near, to_far, _, _ = call(
        products_third_kernel, (rounded,) * 4, (band, shift, means, to_near1, to_far1, v2)
    )
    q2 = joined(to_near, to_far)
    local2 = call(local_kernel, field, (band, v2))
    s1, s2, pairs = call(settle_kernel, (field, field, shape(F32, 4, cols)), (shift, k0, k1, k2))
    partial, form = call(
        cross_third_kernel,
        (field, row),
        (
            band, ridge, shift, means, s2, local0, local1, local2, before0, before1, after0, after1,
            qn0, qf0, near2, far2,
        ),
    )
    moments = sum_over(jnp.concatenate([m0, pairs, form]), "asset")
    s3 = call(finish_third_kernel, field, (partial, q2))
    out = shape(F32, assets, cols)
    return call(combine_kernel, (out, out), (shift, moments, targets, s1, s2, s3))


def solution(mesh):
    return jax.shard_map(
        shards,
        mesh=mesh,
        in_specs=(
            P("asset", "rhs"),
            P("asset"),
            P("asset", None, "rhs", None),
            P("asset", None),
            P("asset"),
        ),
        out_specs=(P("asset", "rhs"), P("asset", "rhs")),
        check_vma=False,
    )
```

time: 112 us -> 87.3 us (0.78)
  blocking collectives: 14.4 us -> 0 us
  waiting for transfers between devices: 34 us -> 29.4 us
  starting transfers between devices: 39 us -> 36.6 us
  other arithmetic: 2.12 us -> 0.17 us
  Pallas kernels: 17.2 us -> 15.3 us
    all_to_all x1 -> x0, blocking collectives: 14.4 us -> none  [to_all(): lax.all_to_all(jnp.broadcast_to(value[None], (count,) + value.shape), axi...]
    all_to_all x1 -> x0, waiting for transfers between devices: 6.38 us -> none  [to_all(): lax.all_to_all(jnp.broadcast_to(value[None], (count,) + value.shape), axi...]
    all_to_all x1 -> x0, starting transfers between devices: 3.47 us -> none  [to_all(): lax.all_to_all(jnp.broadcast_to(value[None], (count,) + value.shape), axi...]
    pallas_call x12 -> x17, Pallas kernels: 17.2 us -> 15.3 us  [call(): pl.pallas_call(kernel, out_shape=out_shape, in_specs=specs, out_specs=jax...]
    ppermute x13 -> x22, waiting for transfers between devices: 27.6 us -> 29.4 us  [the longest x6 11.1 us: near(): return lax.ppermute(value, 'asset', [(i, i ^ 1) for i in range(count)])]
    unnamed x10 -> x14, local copies, waits for them, and re-layouts: 3.29 us -> 4.67 us
    reduce_sum x2 -> x0, other arithmetic: 1.31 us -> none  [the longest x1 1.29 us: shards(): sums = to_all(jnp.broadcast_to(jnp.sum(ridge), (1, 128)), 'asset')]
    another operation x1 -> x0, local copies, waits for them, and re-layouts: 1.25 us -> none  [to_all(): jnp.broadcast_to(value[None], (count,) + value.shape)]
  transfers between devices with their start and end apart: 14 -> 22, of which waited for: 9 -> 11; matrix products, arithmetic and copies ran while one was open for 3% -> 0% of each run, Pallas kernels for 10% -> 15%
where the time goes in v2:
time: 87.3 us; the launch traced here: 87 us
  starting transfers between devices  36.6 us (42%)
  waiting for transfers between devices  29.4 us (34%)
  Pallas kernels  15.3 us (18%)
  local copies, waits for them, and re-layouts  4.67 us (5%)
    pallas_call x17, Pallas kernels, call(): pl.pallas_call(kernel, out_shape=out_shape, in_specs=specs, out_specs=jax...  15.3 us
    ppermute x4, starting transfers between devices, far(): lax.ppermute(value, 'asset', [(i, (i + 1 if i % 2 else i - 1) % count) fo...  11.8 us
    ppermute x6, waiting for transfers between devices, near(): return lax.ppermute(value, 'asset', [(i, i ^ 1) for i in range(count)])  11.1 us
    ppermute x6, starting transfers between devices, sum_over(): total = total + lax.ppermute(value, axis, route)  9.58 us
    ppermute x6, starting transfers between devices, near(): return lax.ppermute(value, 'asset', [(i, i ^ 1) for i in range(count)])  7.14 us
    ppermute x2, starting transfers between devices, back(): lax.ppermute(value, 'asset', [(i, (i + 2 if i % 2 else i - 2) % count) fo...  6.98 us
    ppermute x3, waiting for transfers between devices, sum_step(): lax.ppermute(value, axis, [(i, i ^ distance) for i in range(count)])  5.96 us
    ppermute x2, waiting for transfers between devices, back(): lax.ppermute(value, 'asset', [(i, (i + 2 if i % 2 else i - 2) % count) fo...  4.99 us
  transfers between devices with their start and end apart: 22, of which 11 were waited for; matrix products, arithmetic and copies ran while one was open for 0% of the time, Pallas kernels for 15%

profile of v2, /device:TPU:0, one launch (start us, length us, event | category | flops | bytes accessed | tf_op | source)
XLA Modules:
  0.0 87.0 jit_solution(863678953713425053)
XLA Ops:
  0.6 0.5 collective-permute-start
  1.1 1.0 %copy-done = f32[1024,128]{1,0:T(8,128)S(1)} copy-done((f32[1024,128]{1,0:T(8,128)S(1)}, f32[1024,128]{1,0:T(8,128)}, u32[]{:S(2)}) %copy-start) | copy-done | bytes 524312
  2.2 0.7 copy-done.3
  2.9 0.2 shard_map.70
  3.1 2.6 %collective-permute-start.1 = (bf16[144,1024]{1,0:T(8,128)(2,1)S(1)}, bf16[144,1024]{1,0:T(8,128)(2,1)S(1)}, u32[]{:S(2)}, u32[]{:S(2)}) collective-permute-start(bf16[144,1024]{1,0:T(8,128)(2,1)S(1)} %get-tuple-element.32.v_ref.own_ref), channel_id=1, source_target_pairs={{0,2},{2,0},{4,6},{6,4},{8,10},{10,8},{12,14},{14,12},{16,18},{18,... | collective-permute-start | bytes 884744 | tf_op jit(solution)/shard_map/ppermute | solution.py:306
  5.7 4.5 %collective-permute-start.2 = (bf16[144,1024]{1,0:T(8,128)(2,1)S(1)}, bf16[144,1024]{1,0:T(8,128)(2,1)S(1)}, u32[]{:S(2)}, u32[]{:S(2)}) collective-permute-start(bf16[144,1024]{1,0:T(8,128)(2,1)S(1)} %get-tuple-element.32.v_ref.own_ref), channel_id=1, source_target_pairs={{0,30},{2,4},{4,2},{6,8},{8,6},{10,12},{12,10},{14,16},{16,14},{18... | collective-permute-start | bytes 884744 | tf_op jit(solution)/shard_map/ppermute | solution.py:311
  10.2 1.6 %copy-done.2 = bf16[8,16,64,128]{3,2,1,0:T(8,128)(2,1)S(1)} copy-done((bf16[8,16,64,128]{3,2,1,0:T(8,128)(2,1)S(1)}, bf16[8,16,64,128]{3,2,1,0:T(8,128)(2,1)}, u32[]{:S(2)}) %copy-start.2) | copy-done | bytes 2097176
  11.8 0.7 copy-done.5
  12.5 0.7 copy-done.6
  13.1 2.1 %shard_map.68._ = bf16[25,1024,128]{2,1,0:T(8,128)(2,1)S(1)} custom-call(s32[8,16]{1,0:T(8,128)S(1)} %copy-done.5, s32[8]{0:T(128)S(1)} %copy-done.6, bf16[8,16,64,128]{3,2,1,0:T(8,128)(2,1)S(1)} %copy-done.2), custom_call_target="tpu_custom_call" | custom-call | tf_op jit(solution)/shard_map/pallas_call | solution.py:22
  15.2 1.2 %shard_map.69.band_ref = bf16[25,1024,128]{2,1,0:T(8,128)(2,1)S(1)} custom-call(s32[8,16]{1,0:T(8,128)S(1)} %copy-done.5, s32[8]{0:T(128)S(1)} %copy-done.6, bf16[8,16,64,128]{3,2,1,0:T(8,128)(2,1)S(1)} %collective-permute-done.part_ref, bf16[25,1024,128]{2,1,0:T(8,128)(2,1)S(1)} %shard_map.68._), custom_call_target="tpu_custom_call", output_to_operand_aliasing={{}: (3, {})} | custom-call | tf_op jit(solution)/shard_map/pallas_call | solution.py:22
  16.5 0.6 shard_map.73
  17.1 0.1 collective-permute-start.4
  17.1 2.0 %collective-permute-start.5 = (bf16[128,1024]{1,0:T(8,128)(2,1)S(1)}, bf16[128,1024]{1,0:T(8,128)(2,1)S(1)}, u32[]{:S(2)}, u32[]{:S(2)}) collective-permute-start(bf16[128,1024]{1,0:T(8,128)(2,1)S(1)} %get-tuple-element.38), channel_id=1, source_target_pairs={{0,30},{2,4},{4,2},{6,8},{8,6},{10,12},{12,10},{14,16},{16,14},{18... | collective-permute-start | bytes 786440 | tf_op jit(solution)/shard_map/ppermute | solution.py:311
  19.1 1.1 %shard_map.71.local_ref.local0_ref = f32[128,1024]{1,0:T(8,128)S(1)} custom-call(bf16[25,1024,128]{2,1,0:T(8,128)(2,1)S(1)} %shard_map.69.band_ref, bf16[144,1024]{1,0:T(8,128)(2,1)S(1)} %get-tuple-element.32.v_ref.own_ref), custom_call_target="tpu_custom_call" | custom-call | tf_op jit(solution)/shard_map/pallas_call | solution.py:22
  20.2 4.7 %collective-permute-done.1.near_ref = bf16[144,1024]{1,0:T(8,128)(2,1)S(1)} collective-permute-done((bf16[144,1024]{1,0:T(8,128)(2,1)S(1)}, bf16[144,1024]{1,0:T(8,128)(2,1)S(1)}, u32[]{:S(2)}, u32[]{:S(2)}) %collective-permute-start.1) | collective-permute-done | bytes 294944 | tf_op jit(solution)/shard_map/ppermute | solution.py:306
  24.9 0.0 collective-permute-done.2.far_ref
  24.9 1.0 %shard_map.72 = (f32[128,1024]{1,0:T(8,128)S(1)}, f32[128,1024]{1,0:T(8,128)S(1)}, f32[128,1024]{1,0:T(8,128)S(1)}, f32[8,128]{1,0:T(8,128)S(1)}) custom-call(bf16[25,1024,128]{2,1,0:T(8,128)(2,1)S(1)} %shard_map.69.band_ref, f32[1,1024]{1,0:T(1,128)S(1)} %bitcast.2, f32[128,1024]{1,0:T(8,128)S(1)} %get-tuple-element.31.k_ref.k0_ref, ...), custom_call_target="tpu_custom_call" | custom-call | tf_op jit(solution)/shard_map/pallas_call | solution.py:22
  26.0 0.1 collective-permute-start.3
  26.0 3.5 %collective-permute-done.3 = f32[1,128]{1,0:T(1,128)S(1)} collective-permute-done((f32[1,128]{1,0:T(1,128)S(1)}, f32[1,128]{1,0:T(1,128)S(1)}, u32[]{:S(2)}, u32[]{:S(2)}) %collective-permute-start.3) | collective-permute-done | bytes 544 | tf_op jit(solution)/shard_map/ppermute | solution.py:329
  29.6 0.6 collective-permute-done.4.near_ref.qn0_ref
  30.2 0.3 shard_map.74
  30.4 0.0 copy-start.4
  30.4 0.5 shard_map.77
  31.0 5.6 %collective-permute-start.10 = (bf16[128,1024]{1,0:T(8,128)(2,1)S(1)}, bf16[128,1024]{1,0:T(8,128)(2,1)S(1)}, u32[]{:S(2)}, u32[]{:S(2)}) collective-permute-start(bf16[128,1024]{1,0:T(8,128)(2,1)S(1)} %get-tuple-element.48.far1_ref), channel_id=1, source_target_pairs={{0,28},{2,6},{4,0},{6,10},{8,4},{10,14},{12,8},{14,18},{16,12},{18... | collective-permute-start | bytes 786440 | tf_op jit(solution)/shard_map/ppermute | solution.py:318
  36.6 2.1 %collective-permute-start.8 = (bf16[128,1024]{1,0:T(8,128)(2,1)S(1)}, bf16[128,1024]{1,0:T(8,128)(2,1)S(1)}, u32[]{:S(2)}, u32[]{:S(2)}) collective-permute-start(bf16[128,1024]{1,0:T(8,128)(2,1)S(1)} %get-tuple-element.39.v_ref), channel_id=1, source_target_pairs={{0,30},{2,4},{4,2},{6,8},{8,6},{10,12},{12,10},{14,16},{16,14},{18... | collective-permute-start | bytes 786440 | tf_op jit(solution)/shard_map/ppermute | solution.py:311
  38.6 5.0 %collective-permute-done.10 = bf16[128,1024]{1,0:T(8,128)(2,1)S(1)} collective-permute-done((bf16[128,1024]{1,0:T(8,128)(2,1)S(1)}, bf16[128,1024]{1,0:T(8,128)(2,1)S(1)}, u32[]{:S(2)}, u32[]{:S(2)}) %collective-permute-start.10) | collective-permute-done | bytes 262176 | tf_op jit(solution)/shard_map/ppermute | solution.py:318
  43.6 0.1 add_convert_fusion.1
  43.7 3.3 %collective-permute-start.11 = (bf16[128,1024]{1,0:T(8,128)(2,1)S(1)}, bf16[128,1024]{1,0:T(8,128)(2,1)S(1)}, u32[]{:S(2)}, u32[]{:S(2)}) collective-permute-start(bf16[128,1024]{1,0:T(8,128)(2,1)S(1)} %add_convert_fusion.1), channel_id=1, source_target_pairs={{0,2},{2,0},{4,6},{6,4},{8,10},{10,8},{12,14},{14,12},{16,18},{18,... | collective-permute-start | bytes 786440 | tf_op jit(solution)/shard_map/ppermute | solution.py:306
  47.0 0.0 collective-permute-start.6
  47.0 1.1 %shard_map.75.local_ref.local1_ref = f32[128,1024]{1,0:T(8,128)S(1)} custom-call(bf16[25,1024,128]{2,1,0:T(8,128)(2,1)S(1)} %shard_map.69.band_ref, bf16[128,1024]{1,0:T(8,128)(2,1)S(1)} %get-tuple-element.39.v_ref), custom_call_target="tpu_custom_call" | custom-call | tf_op jit(solution)/shard_map/pallas_call | solution.py:22
  48.1 2.4 %collective-permute-done.6 = f32[1,128]{1,0:T(1,128)S(1)} collective-permute-done((f32[1,128]{1,0:T(1,128)S(1)}, f32[1,128]{1,0:T(1,128)S(1)}, u32[]{:S(2)}, u32[]{:S(2)}) %collective-permute-start.6) | collective-permute-done | bytes 544 | tf_op jit(solution)/shard_map/ppermute | solution.py:329
  50.6 0.0 collective-permute-done.7.near_ref
  50.6 0.0 collective-permute-done.8.far_ref
  50.6 1.1 %shard_map.76 = (f32[128,1024]{1,0:T(8,128)S(1)}, f32[128,1024]{1,0:T(8,128)S(1)}, f32[128,1024]{1,0:T(8,128)S(1)}) custom-call(bf16[25,1024,128]{2,1,0:T(8,128)(2,1)S(1)} %shard_map.69.band_ref, f32[1,1024]{1,0:T(1,128)S(1)} %bitcast.3, f32[8,128]{1,0:T(8,128)S(1)} %get-tuple-element.33.mean_ref, f32[128,1024]{1,0:T(8,128)S(1)} %get-tuple-element.41.k_ref.k1_ref, ...), custom_call_target="tpu_custom_call" | custom-call | tf_op jit(solution)/shard_map/pallas_call | solution.py:22
  51.7 0.5 collective-permute-start.9
  52.2 3.2 %collective-permute-done.11.q_ref = bf16[128,1024]{1,0:T(8,128)(2,1)S(1)} collective-permute-done((bf16[128,1024]{1,0:T(8,128)(2,1)S(1)}, bf16[128,1024]{1,0:T(8,128)(2,1)S(1)}, u32[]{:S(2)}, u32[]{:S(2)}) %collective-permute-start.11) | collective-permute-done | bytes 262176 | tf_op jit(solution)/shard_map/ppermute | solution.py:306
  55.5 0.3 shard_map.78
  55.8 0.3 collective-permute-start.12
  56.1 3.3 %collective-permute-start.13 = (bf16[128,1024]{1,0:T(8,128)(2,1)S(1)}, bf16[128,1024]{1,0:T(8,128)(2,1)S(1)}, u32[]{:S(2)}, u32[]{:S(2)}) collective-permute-start(bf16[128,1024]{1,0:T(8,128)(2,1)S(1)} %get-tuple-element.52.v_ref), channel_id=1, source_target_pairs={{0,30},{2,4},{4,2},{6,8},{8,6},{10,12},{12,10},{14,16},{16,14},{18... | collective-permute-start | bytes 786440 | tf_op jit(solution)/shard_map/ppermute | solution.py:311
  59.4 0.0 collective-permute-done.9
  59.4 1.4 %shard_map.82 = (bf16[128,1024]{1,0:T(8,128)(2,1)S(1)}, bf16[128,1024]{1,0:T(8,128)(2,1)S(1)}, bf16[128,1024]{1,0:T(8,128)(2,1)}, bf16[128,1024]{1,0:T(8,128)(2,1)}) custom-call(bf16[25,1024,128]{2,1,0:T(8,128)(2,1)S(1)} %shard_map.69.band_ref, f32[1,128]{1,0:T(1,128)S(1)} %add_multiply_fusion.shift_ref, f32[8,128]{1,0:T(8,128)S(1)} %get-tuple-element.33.mean_ref, ...), custom_call_target="tpu_custom_call" | custom-call | tf_op jit(solution)/shard_map/pallas_call | solution.py:22
  60.8 1.4 %collective-permute-start.20 = (bf16[128,1024]{1,0:T(8,128)(2,1)S(1)}, bf16[128,1024]{1,0:T(8,128)(2,1)S(1)}, u32[]{:S(2)}, u32[]{:S(2)}) collective-permute-start(bf16[128,1024]{1,0:T(8,128)(2,1)S(1)} %get-tuple-element.59), channel_id=1, source_target_pairs={{0,28},{2,6},{4,0},{6,10},{8,4},{10,14},{12,8},{14,18},{16,12},{18... | collective-permute-start | bytes 786440 | tf_op jit(solution)/shard_map/ppermute | solution.py:318
  62.2 1.1 %shard_map.80.local_ref = f32[128,1024]{1,0:T(8,128)S(1)} custom-call(bf16[25,1024,128]{2,1,0:T(8,128)(2,1)S(1)} %shard_map.69.band_ref, bf16[128,1024]{1,0:T(8,128)(2,1)S(1)} %get-tuple-element.52.v_ref), custom_call_target="tpu_custom_call" | custom-call | tf_op jit(solution)/shard_map/pallas_call | solution.py:22
  63.3 0.4 shard_map.79
  63.7 2.6 %collective-permute-done.12.near_ref = bf16[128,1024]{1,0:T(8,128)(2,1)S(1)} collective-permute-done((bf16[128,1024]{1,0:T(8,128)(2,1)S(1)}, bf16[128,1024]{1,0:T(8,128)(2,1)S(1)}, u32[]{:S(2)}, u32[]{:S(2)}) %collective-permute-start.12) | collective-permute-done | bytes 262176 | tf_op jit(solution)/shard_map/ppermute | solution.py:306
  66.3 2.7 %collective-permute-done.13.far_ref = bf16[128,1024]{1,0:T(8,128)(2,1)S(1)} collective-permute-done((bf16[128,1024]{1,0:T(8,128)(2,1)S(1)}, bf16[128,1024]{1,0:T(8,128)(2,1)S(1)}, u32[]{:S(2)}, u32[]{:S(2)}) %collective-permute-start.13) | collective-permute-done | bytes 262176 | tf_op jit(solution)/shard_map/ppermute | solution.py:311
  69.0 1.3 %shard_map.81 = (f32[128,1024]{1,0:T(8,128)S(1)}, f32[1,128]{1,0:T(1,128)S(1)}) custom-call(bf16[25,1024,128]{2,1,0:T(8,128)(2,1)S(1)} %shard_map.69.band_ref, f32[1,1024]{1,0:T(1,128)S(1)} %bitcast.4, f32[1,128]{1,0:T(1,128)S(1)} %add_multiply_fusion.shift_ref, f32[8,128]{1,0:T(8,128)S(1)} %get-tuple-element.33.mean_ref, ...), custom_call_target="tpu_custom_call" | custom-call | tf_op jit(solution)/shard_map/pallas_call | solution.py:22
  70.4 0.1 collective-permute-start.16
  70.4 3.8 %collective-permute-start.15 = (f32[6,128]{1,0:T(8,128)S(1)}, f32[6,128]{1,0:T(8,128)S(1)}, u32[]{:S(2)}, u32[]{:S(2)}) collective-permute-start(f32[6,128]{1,0:T(8,128)S(1)} %pad_maximum_fusion), channel_id=1, source_target_pairs={{0,4},{2,6},{4,0},{6,2},{8,12},{10,14},{12,8},{14,10},{16,20},{18,... | collective-permute-start | bytes 9224 | tf_op jit(solution)/shard_map/ppermute | solution.py:339
  74.2 1.3 %collective-permute-start.14 = (f32[6,128]{1,0:T(8,128)S(1)}, f32[6,128]{1,0:T(8,128)S(1)}, u32[]{:S(2)}, u32[]{:S(2)}) collective-permute-start(f32[6,128]{1,0:T(8,128)S(1)} %pad_maximum_fusion), channel_id=1, source_target_pairs={{0,2},{2,0},{4,6},{6,4},{8,10},{10,8},{12,14},{14,12},{16,18},{18,... | collective-permute-start | bytes 9224 | tf_op jit(solution)/shard_map/ppermute | solution.py:339
  75.5 0.0 collective-permute-done.20
  75.5 0.1 add_convert_fusion
  75.6 0.8 collective-permute-start.21
  76.4 0.0 collective-permute-done.16
  76.4 0.0 collective-permute-done.15
  76.4 1.4 %collective-permute-done.14 = f32[6,128]{1,0:T(8,128)S(1)} collective-permute-done((f32[6,128]{1,0:T(8,128)S(1)}, f32[6,128]{1,0:T(8,128)S(1)}, u32[]{:S(2)}, u32[]{:S(2)}) %collective-permute-start.14) | collective-permute-done | bytes 3104 | tf_op jit(solution)/shard_map/ppermute | solution.py:339
  77.9 3.1 %collective-permute-start.19 = (f32[6,128]{1,0:T(8,128)S(1)}, f32[6,128]{1,0:T(8,128)S(1)}, u32[]{:S(2)}, u32[]{:S(2)}) collective-permute-start(f32[6,128]{1,0:T(8,128)S(1)} %add_add_fusion.1), channel_id=1, source_target_pairs={{0,24},{2,26},{4,28},{6,30},{8,16},{10,18},{12,20},{14,22},{16,8},... | collective-permute-start | bytes 9224 | tf_op jit(solution)/shard_map/ppermute | solution.py:339
  81.0 1.4 %collective-permute-start.17 = (f32[6,128]{1,0:T(8,128)S(1)}, f32[6,128]{1,0:T(8,128)S(1)}, u32[]{:S(2)}, u32[]{:S(2)}) collective-permute-start(f32[6,128]{1,0:T(8,128)S(1)} %add_add_fusion.1), channel_id=1, source_target_pairs={{0,8},{2,10},{4,12},{6,14},{8,0},{10,2},{12,4},{14,6},{16,24},{18,... | collective-permute-start | bytes 9224 | tf_op jit(solution)/shard_map/ppermute | solution.py:339
  82.3 1.0 %collective-permute-done.19 = f32[6,128]{1,0:T(8,128)S(1)} collective-permute-done((f32[6,128]{1,0:T(8,128)S(1)}, f32[6,128]{1,0:T(8,128)S(1)}, u32[]{:S(2)}, u32[]{:S(2)}) %collective-permute-start.19) | collective-permute-done | bytes 3104 | tf_op jit(solution)/shard_map/ppermute | solution.py:339
  83.3 2.1 %collective-permute-done.18 = f32[6,128]{1,0:T(8,128)S(1)} collective-permute-done((f32[6,128]{1,0:T(8,128)S(1)}, f32[6,128]{1,0:T(8,128)S(1)}, u32[]{:S(2)}, u32[]{:S(2)}) %collective-permute-start.18) | collective-permute-done | bytes 3104 | tf_op jit(solution)/shard_map/ppermute | solution.py:339
  85.5 0.0 collective-permute-done.21.q_ref
  85.5 0.1 shard_map.83.k3_ref
  85.6 1.4 %shard_map.84 = (f32[1024,128]{1,0:T(8,128)}, f32[1024,128]{1,0:T(8,128)}) custom-call(f32[1,128]{1,0:T(1,128)S(1)} %add_multiply_fusion.shift_ref, f32[6,128]{1,0:T(8,128)S(1)} %add_add_fusion.moment_ref, f32[1024,128]{1,0:T(8,128)S(1)} %copy-done.1, f32[128,1024]{1,0:T(8,128)S(1)} %get-tuple-element.56.k1_ref, ...), custom_call_target="tpu_custom_call" | custom-call | tf_op jit(solution)/shard_map/pallas_call | solution.py:22
  (20 shorter events, 0.1 us)
Async XLA Ops:
  0.6 14.6 %collective-permute-start = (bf16[8,16,64,128]{3,2,1,0:T(8,128)(2,1)}, bf16[8,16,64,128]{3,2,1,0:T(8,128)(2,1)S(1)}, u32[]{:S(2)}, u32[]{:S(2)}) collective-permute-start(bf16[8,16,64,128]{3,2,1,0:T(8,128)(2,1)} %part_ref.1), channel_id=1, source_target_pairs={{0,1},{1,0},{2,3},{3,2},{4,5},{5,4},{6,7},{7,6},{8,9},{9,8},{10,11... | collective-permute-start | bytes 6291464 | tf_op jit(solution)/shard_map/ppermute | solution.py:363
  1.1 1.0 %copy-start = (f32[1024,128]{1,0:T(8,128)S(1)}, f32[1024,128]{1,0:T(8,128)}, u32[]{:S(2)}) copy-start(f32[1024,128]{1,0:T(8,128)} %targets_ref.3) | copy-start | bytes 1572868
  2.2 0.7 copy-start.3
  3.1 21.8 %collective-permute-start.1 = (bf16[144,1024]{1,0:T(8,128)(2,1)S(1)}, bf16[144,1024]{1,0:T(8,128)(2,1)S(1)}, u32[]{:S(2)}, u32[]{:S(2)}) collective-permute-start(bf16[144,1024]{1,0:T(8,128)(2,1)S(1)} %get-tuple-element.32.v_ref.own_ref), channel_id=1, source_target_pairs={{0,2},{2,0},{4,6},{6,4},{8,10},{10,8},{12,14},{14,12},{16,18},{18,... | collective-permute-start | bytes 884744 | tf_op jit(solution)/shard_map/ppermute | solution.py:306
  5.7 19.3 %collective-permute-start.2 = (bf16[144,1024]{1,0:T(8,128)(2,1)S(1)}, bf16[144,1024]{1,0:T(8,128)(2,1)S(1)}, u32[]{:S(2)}, u32[]{:S(2)}) collective-permute-start(bf16[144,1024]{1,0:T(8,128)(2,1)S(1)} %get-tuple-element.32.v_ref.own_ref), channel_id=1, source_target_pairs={{0,30},{2,4},{4,2},{6,8},{8,6},{10,12},{12,10},{14,16},{16,14},{18... | collective-permute-start | bytes 884744 | tf_op jit(solution)/shard_map/ppermute | solution.py:311
  10.2 1.6 %copy-start.2 = (bf16[8,16,64,128]{3,2,1,0:T(8,128)(2,1)S(1)}, bf16[8,16,64,128]{3,2,1,0:T(8,128)(2,1)}, u32[]{:S(2)}) copy-start(bf16[8,16,64,128]{3,2,1,0:T(8,128)(2,1)} %part_ref.1) | copy-start | bytes 6291460
  11.8 0.7 copy-start.5
  12.5 0.7 copy-start.6
  17.1 13.1 %collective-permute-start.4 = (bf16[128,1024]{1,0:T(8,128)(2,1)S(1)}, bf16[128,1024]{1,0:T(8,128)(2,1)S(1)}, u32[]{:S(2)}, u32[]{:S(2)}) collective-permute-start(bf16[128,1024]{1,0:T(8,128)(2,1)S(1)} %get-tuple-element.37), channel_id=1, source_target_pairs={{0,2},{2,0},{4,6},{6,4},{8,10},{10,8},{12,14},{14,12},{16,18},{18,... | collective-permute-start | bytes 786440 | tf_op jit(solution)/shard_map/ppermute | solution.py:306
  17.1 13.0 %collective-permute-start.5 = (bf16[128,1024]{1,0:T(8,128)(2,1)S(1)}, bf16[128,1024]{1,0:T(8,128)(2,1)S(1)}, u32[]{:S(2)}, u32[]{:S(2)}) collective-permute-start(bf16[128,1024]{1,0:T(8,128)(2,1)S(1)} %get-tuple-element.38), channel_id=1, source_target_pairs={{0,30},{2,4},{4,2},{6,8},{8,6},{10,12},{12,10},{14,16},{16,14},{18... | collective-permute-start | bytes 786440 | tf_op jit(solution)/shard_map/ppermute | solution.py:311
  26.0 3.6 %collective-permute-start.3 = (f32[1,128]{1,0:T(1,128)S(1)}, f32[1,128]{1,0:T(1,128)S(1)}, u32[]{:S(2)}, u32[]{:S(2)}) collective-permute-start(f32[1,128]{1,0:T(1,128)S(1)} %slice.3), channel_id=1, source_target_pairs={{0,4},{2,6},{4,0},{6,2},{8,12},{10,14},{12,8},{14,10},{16,20},{18,... | collective-permute-start | bytes 1544 | tf_op jit(solution)/shard_map/ppermute | solution.py:329
  30.4 20.2 %copy-start.4 = (f32[1024]{0:T(1024)S(1)}, f32[1024]{0:T(1024)}, u32[]{:S(2)}) copy-start(f32[1024]{0:T(1024)} %param.6) | copy-start | bytes 12292
  31.0 12.7 %collective-permute-start.10 = (bf16[128,1024]{1,0:T(8,128)(2,1)S(1)}, bf16[128,1024]{1,0:T(8,128)(2,1)S(1)}, u32[]{:S(2)}, u32[]{:S(2)}) collective-permute-start(bf16[128,1024]{1,0:T(8,128)(2,1)S(1)} %get-tuple-element.48.far1_ref), channel_id=1, source_target_pairs={{0,28},{2,6},{4,0},{6,10},{8,4},{10,14},{12,8},{14,18},{16,12},{18... | collective-permute-start | bytes 786440 | tf_op jit(solution)/shard_map/ppermute | solution.py:318
  36.6 14.0 %collective-permute-start.7 = (bf16[128,1024]{1,0:T(8,128)(2,1)S(1)}, bf16[128,1024]{1,0:T(8,128)(2,1)S(1)}, u32[]{:S(2)}, u32[]{:S(2)}) collective-permute-start(bf16[128,1024]{1,0:T(8,128)(2,1)S(1)} %get-tuple-element.39.v_ref), channel_id=1, source_target_pairs={{0,2},{2,0},{4,6},{6,4},{8,10},{10,8},{12,14},{14,12},{16,18},{18,... | collective-permute-start | bytes 786440 | tf_op jit(solution)/shard_map/ppermute | solution.py:306
  36.6 14.0 %collective-permute-start.8 = (bf16[128,1024]{1,0:T(8,128)(2,1)S(1)}, bf16[128,1024]{1,0:T(8,128)(2,1)S(1)}, u32[]{:S(2)}, u32[]{:S(2)}) collective-permute-start(bf16[128,1024]{1,0:T(8,128)(2,1)S(1)} %get-tuple-element.39.v_ref), channel_id=1, source_target_pairs={{0,30},{2,4},{4,2},{6,8},{8,6},{10,12},{12,10},{14,16},{16,14},{18... | collective-permute-start | bytes 786440 | tf_op jit(solution)/shard_map/ppermute | solution.py:311
  43.7 11.8 %collective-permute-start.11 = (bf16[128,1024]{1,0:T(8,128)(2,1)S(1)}, bf16[128,1024]{1,0:T(8,128)(2,1)S(1)}, u32[]{:S(2)}, u32[]{:S(2)}) collective-permute-start(bf16[128,1024]{1,0:T(8,128)(2,1)S(1)} %add_convert_fusion.1), channel_id=1, source_target_pairs={{0,2},{2,0},{4,6},{6,4},{8,10},{10,8},{12,14},{14,12},{16,18},{18,... | collective-permute-start | bytes 786440 | tf_op jit(solution)/shard_map/ppermute | solution.py:306
  47.0 3.5 %collective-permute-start.6 = (f32[1,128]{1,0:T(1,128)S(1)}, f32[1,128]{1,0:T(1,128)S(1)}, u32[]{:S(2)}, u32[]{:S(2)}) collective-permute-start(f32[1,128]{1,0:T(1,128)S(1)} %slice_add_fusion), channel_id=1, source_target_pairs={{0,8},{2,10},{4,12},{6,14},{8,0},{10,2},{12,4},{14,6},{16,24},{18,... | collective-permute-start | bytes 1544 | tf_op jit(solution)/shard_map/ppermute | solution.py:329
  51.7 7.7 %collective-permute-start.9 = (f32[1,128]{1,0:T(1,128)S(1)}, f32[1,128]{1,0:T(1,128)S(1)}, u32[]{:S(2)}, u32[]{:S(2)}) collective-permute-start(f32[1,128]{1,0:T(1,128)S(1)} %add.34), channel_id=1, source_target_pairs={{0,16},{2,18},{4,20},{6,22},{8,24},{10,26},{12,28},{14,30},{16,0},... | collective-permute-start | bytes 1544 | tf_op jit(solution)/shard_map/ppermute | solution.py:329
  55.8 10.5 %collective-permute-start.12 = (bf16[128,1024]{1,0:T(8,128)(2,1)S(1)}, bf16[128,1024]{1,0:T(8,128)(2,1)S(1)}, u32[]{:S(2)}, u32[]{:S(2)}) collective-permute-start(bf16[128,1024]{1,0:T(8,128)(2,1)S(1)} %get-tuple-element.52.v_ref), channel_id=1, source_target_pairs={{0,2},{2,0},{4,6},{6,4},{8,10},{10,8},{12,14},{14,12},{16,18},{18,... | collective-permute-start | bytes 786440 | tf_op jit(solution)/shard_map/ppermute | solution.py:306
  56.1 12.9 %collective-permute-start.13 = (bf16[128,1024]{1,0:T(8,128)(2,1)S(1)}, bf16[128,1024]{1,0:T(8,128)(2,1)S(1)}, u32[]{:S(2)}, u32[]{:S(2)}) collective-permute-start(bf16[128,1024]{1,0:T(8,128)(2,1)S(1)} %get-tuple-element.52.v_ref), channel_id=1, source_target_pairs={{0,30},{2,4},{4,2},{6,8},{8,6},{10,12},{12,10},{14,16},{16,14},{18... | collective-permute-start | bytes 786440 | tf_op jit(solution)/shard_map/ppermute | solution.py:311
  60.8 14.7 %collective-permute-start.20 = (bf16[128,1024]{1,0:T(8,128)(2,1)S(1)}, bf16[128,1024]{1,0:T(8,128)(2,1)S(1)}, u32[]{:S(2)}, u32[]{:S(2)}) collective-permute-start(bf16[128,1024]{1,0:T(8,128)(2,1)S(1)} %get-tuple-element.59), channel_id=1, source_target_pairs={{0,28},{2,6},{4,0},{6,10},{8,4},{10,14},{12,8},{14,18},{16,12},{18... | collective-permute-start | bytes 786440 | tf_op jit(solution)/shard_map/ppermute | solution.py:318
  69.0 16.5 %copy-start.1 = (f32[1024,128]{1,0:T(8,128)S(1)}, f32[1024,128]{1,0:T(8,128)}, u32[]{:S(2)}) copy-start(f32[1024,128]{1,0:T(8,128)} %targets_ref.3) | copy-start | bytes 1572868
  70.4 6.0 %collective-permute-start.16 = (f32[6,128]{1,0:T(8,128)S(1)}, f32[6,128]{1,0:T(8,128)S(1)}, u32[]{:S(2)}, u32[]{:S(2)}) collective-permute-start(f32[6,128]{1,0:T(8,128)S(1)} %pad_maximum_fusion), channel_id=1, source_target_pairs={{0,6},{2,4},{4,2},{6,0},{8,14},{10,12},{12,10},{14,8},{16,22},{18,... | collective-permute-start | bytes 9224 | tf_op jit(solution)/shard_map/ppermute | solution.py:339
  70.4 6.0 %collective-permute-start.15 = (f32[6,128]{1,0:T(8,128)S(1)}, f32[6,128]{1,0:T(8,128)S(1)}, u32[]{:S(2)}, u32[]{:S(2)}) collective-permute-start(f32[6,128]{1,0:T(8,128)S(1)} %pad_maximum_fusion), channel_id=1, source_target_pairs={{0,4},{2,6},{4,0},{6,2},{8,12},{10,14},{12,8},{14,10},{16,20},{18,... | collective-permute-start | bytes 9224 | tf_op jit(solution)/shard_map/ppermute | solution.py:339
  74.2 3.6 %collective-permute-start.14 = (f32[6,128]{1,0:T(8,128)S(1)}, f32[6,128]{1,0:T(8,128)S(1)}, u32[]{:S(2)}, u32[]{:S(2)}) collective-permute-start(f32[6,128]{1,0:T(8,128)S(1)} %pad_maximum_fusion), channel_id=1, source_target_pairs={{0,2},{2,0},{4,6},{6,4},{8,10},{10,8},{12,14},{14,12},{16,18},{18,... | collective-permute-start | bytes 9224 | tf_op jit(solution)/shard_map/ppermute | solution.py:339
  75.6 9.9 %collective-permute-start.21 = (bf16[128,1024]{1,0:T(8,128)(2,1)S(1)}, bf16[128,1024]{1,0:T(8,128)(2,1)S(1)}, u32[]{:S(2)}, u32[]{:S(2)}) collective-permute-start(bf16[128,1024]{1,0:T(8,128)(2,1)S(1)} %add_convert_fusion), channel_id=1, source_target_pairs={{0,2},{2,0},{4,6},{6,4},{8,10},{10,8},{12,14},{14,12},{16,18},{18,... | collective-permute-start | bytes 786440 | tf_op jit(solution)/shard_map/ppermute | solution.py:306
  77.9 5.5 %collective-permute-start.19 = (f32[6,128]{1,0:T(8,128)S(1)}, f32[6,128]{1,0:T(8,128)S(1)}, u32[]{:S(2)}, u32[]{:S(2)}) collective-permute-start(f32[6,128]{1,0:T(8,128)S(1)} %add_add_fusion.1), channel_id=1, source_target_pairs={{0,24},{2,26},{4,28},{6,30},{8,16},{10,18},{12,20},{14,22},{16,8},... | collective-permute-start | bytes 9224 | tf_op jit(solution)/shard_map/ppermute | solution.py:339
  81.0 4.5 %collective-permute-start.18 = (f32[6,128]{1,0:T(8,128)S(1)}, f32[6,128]{1,0:T(8,128)S(1)}, u32[]{:S(2)}, u32[]{:S(2)}) collective-permute-start(f32[6,128]{1,0:T(8,128)S(1)} %add_add_fusion.1), channel_id=1, source_target_pairs={{0,16},{2,18},{4,20},{6,22},{8,24},{10,26},{12,28},{14,30},{16,0},... | collective-permute-start | bytes 9224 | tf_op jit(solution)/shard_map/ppermute | solution.py:339
  81.0 4.5 %collective-permute-start.17 = (f32[6,128]{1,0:T(8,128)S(1)}, f32[6,128]{1,0:T(8,128)S(1)}, u32[]{:S(2)}, u32[]{:S(2)}) collective-permute-start(f32[6,128]{1,0:T(8,128)S(1)} %add_add_fusion.1), channel_id=1, source_target_pairs={{0,8},{2,10},{4,12},{6,14},{8,0},{10,2},{12,4},{14,6},{16,24},{18,... | collective-permute-start | bytes 9224 | tf_op jit(solution)/shard_map/ppermute | solution.py:339

commit v3 on v2

--- a/solution.py
+++ b/solution.py
@@ -15,7 +15,7 @@
 NT = (((1,), (1,)), ((), ()))
 
 
-def call(kernel, out_shape, args, smem=0, outside=(), scratch=(), aliases=None):
+def call(kernel, out_shape, args, smem=0, outside=(), scratch=(), aliases=None, flops=0):
     specs = [SMEM] * smem + [VMEM] * (len(args) - smem)
     for at in outside:
         specs[at] = HBM
@@ -26,6 +26,7 @@
         out_specs=jax.tree.map(lambda _: VMEM, out_shape),
         scratch_shapes=scratch,
         input_output_aliases=aliases or {},
+        cost_estimate=pl.CostEstimate(flops=flops, bytes_accessed=2**20, transcendentals=0) if flops else None,
         compiler_params=pltpu.CompilerParams(vmem_limit_bytes=LIMIT),
     )(*args)
 
@@ -37,18 +38,15 @@
     return jnp.sum(folded.T, axis=0, keepdims=True)
 
 
-def prepare_kernel(targets_ref, ridge_ref, base_ref, message_ref, moment_ref):
-    assets, cols = targets_ref.shape
+def prepare_kernel(targets_ref, base_ref, rounded_ref, moment_ref):
+    assets = targets_ref.shape[0]
     width = moment_ref.shape[1]
     for at in range(0, assets, width):
         tile = targets_ref[at : at + width, :].T
         base_ref[:, at : at + width] = tile
-        message_ref[:cols, at : at + width] = tile.astype(BF16)
+        rounded_ref[:, at : at + width] = tile.astype(BF16)
     values = targets_ref[...]
     moment_ref[...] = jnp.sum(values * values, axis=0, keepdims=True)
-    mean = jnp.sum(ridge_ref[...], axis=1, keepdims=True) / assets
-    rest = message_ref.shape[0] - cols
-    message_ref[cols:, :] = jnp.broadcast_to(mean, (rest, assets)).astype(BF16)
 
 
 def place_blocks(col_ref, length_ref, offset, part_ref, band_ref):
@@ -93,23 +91,32 @@
 def products_kernel(band_ref, v_ref, near_ref, far_ref):
     places, _, width = band_ref.shape
     rows = places // 3
-    cols = near_ref.shape[0]
+    cols = v_ref.shape[0]
     odd = is_odd((cols, 2 * width))
     for j in range(0, rows, 2):
         out = slice(j * width, (j + 2) * width)
         low = slice(0, (j + 2) * width)
         high = slice(j * width, rows * width)
         before = lax.dot_general(
-            v_ref[:cols, low], columns(band_ref, j, j + 2, low), NN, preferred_element_type=F32
+            v_ref[:, low], columns(band_ref, j, j + 2, low), NN, preferred_element_type=F32
         )
         after = lax.dot_general(
-            v_ref[:cols, high],
+            v_ref[:, high],
             columns(band_ref, 2 * rows + j, 2 * rows + j + 2, high),
             NN,
             preferred_element_type=F32,
         )
-        near_ref[:, out] = jnp.where(odd, before, after).astype(BF16)
-        far_ref[:, out] = jnp.where(odd, after, before).astype(BF16)
+        near_ref[:cols, out] = jnp.where(odd, before, after).astype(BF16)
+        far_ref[:cols, out] = jnp.where(odd, after, before).astype(BF16)
+
+
+def products_first_kernel(band_ref, v_ref, ridge_ref, near_ref, far_ref):
+    products_kernel(band_ref, v_ref, near_ref, far_ref)
+    cols, assets = v_ref.shape
+    mean = jnp.sum(ridge_ref[...], axis=1, keepdims=True) / assets
+    rest = jnp.broadcast_to(mean, (near_ref.shape[0] - cols, assets)).astype(BF16)
+    near_ref[cols:, :] = rest
+    far_ref[cols:, :] = rest
 
 
 def products_third_kernel(
@@ -158,29 +165,29 @@
     )
 
 
-def cross_first_kernel(
-    band_ref, ridge_ref, k_ref, local_ref, own_ref, near_ref, far_ref,
-    sum_ref, before_ref, after_ref, mean_ref
-):
+def gather_first_kernel(ridge_ref, k_ref, local_ref, own_ref, near_ref, far_ref, sum_ref, mean_ref):
     cols, width = k_ref.shape[0], mean_ref.shape[1]
-    before, after = neighbours(near_ref, far_ref, cols)
     means = [ref[cols : cols + 8, :width].astype(F32)[:1] for ref in (own_ref, near_ref, far_ref)]
     odd = is_odd(means[0].shape)
     means += [jnp.where(odd, means[1], means[2]), jnp.where(odd, means[2], means[1])]
     means.append(means[0] + means[1])
     for i, value in enumerate(means):
         mean_ref[i : i + 1, :] = value
+    both = local_ref[...] + near_ref[:cols, :].astype(F32) + far_ref[:cols, :].astype(F32)
+    sum_ref[...] = ridge_ref[...] * k_ref[...] + 0.5 * both
+
+
+def cross_first_kernel(
+    band_ref, sum_ref, k_ref, mean_ref, near_ref, far_ref, next_ref, rounded_ref, before_ref, after_ref
+):
+    before, after = neighbours(near_ref, far_ref, k_ref.shape[0])
     for j in range(0, band_ref.shape[0] // 3, 2):
         out, first, second = forward_products(band_ref, before, after, j)
         before_ref[:, out] = first
         after_ref[:, out] = second
-        sum_ref[:, out] = ridge_ref[:, out] * k_ref[:, out] + 0.5 * (local_ref[:, out] + first + second)
-
-
-def finish_first_kernel(k_ref, mean_ref, sum_ref, near_ref, far_ref, next_ref, rounded_ref):
-    value = sum_ref[...] + 0.5 * (near_ref[...].astype(F32) + far_ref[...].astype(F32))
-    next_ref[...] = value
-    rounded_ref[...] = (value - mean_ref[0:1, 0:1] * k_ref[...]).astype(BF16)
+        value = sum_ref[:, out] + 0.5 * (first + second)
+        next_ref[:, out] = value
+        rounded_ref[:, out] = (value - mean_ref[0:1, 0:1] * k_ref[:, out]).astype(BF16)
 
 
 def cross_second_kernel(
@@ -194,7 +201,7 @@
         before_ref[:, out] = first
         after_ref[:, out] = second
         known = own * local0_ref[:, out] + mean_before * before0_ref[:, out] + mean_after * after0_ref[:, out]
-        known = known + mean_near * qn0_ref[:, out].astype(F32) + mean_far * qf0_ref[:, out].astype(F32)
+        known = known + mean_near * qn0_ref[: k_ref.shape[0], out].astype(F32) + mean_far * qf0_ref[: k_ref.shape[0], out].astype(F32)
         both = local_ref[:, out] + first + second + known
         sum_ref[:, out] = ridge_ref[:, out] * k_ref[:, out] + 0.5 * both
 
@@ -206,14 +213,16 @@
     rounded_ref[...] = (value - 2 * own * k_ref[...] + own * own * k0_ref[...]).astype(BF16)
 
 
-def settle_kernel(shift_ref, k0_ref, k1_ref, k2_ref, s1_ref, s2_ref, moment_ref):
+def settle_kernel(shift_ref, k0_ref, k1_ref, k2_ref, s2_ref, rows1_ref, rows2_ref, moment_ref):
     width = moment_ref.shape[1]
     c = shift_ref[0:1, 0:1]
     k0, k1 = k0_ref[...], k1_ref[...]
     s1 = k1 - c * k0
     s2 = k2_ref[...] - 2 * c * k1 + c * c * k0
-    s1_ref[...] = s1
     s2_ref[...] = s2
+    for at in range(0, k0.shape[1], width):
+        rows1_ref[at : at + width, :] = s1[:, at : at + width].T
+        rows2_ref[at : at + width, :] = s2[:, at : at + width].T
     for i, value in enumerate((k0 * s1, s1 * s1, s1 * s2, s2 * s2)):
         moment_ref[i : i + 1, :] = column_sums(value, width)
 
@@ -238,8 +247,8 @@
         first = first + known(mean_before, before0_ref, before1_ref, out)
         second = second + known(mean_after, after0_ref, after1_ref, out)
         local = local_ref[:, out] + known(own, local0_ref, local1_ref, out)
-        back = mean_near * mean_near * qn0_ref[:, out].astype(F32)
-        back = back + mean_far * mean_far * qf0_ref[:, out].astype(F32)
+        back = mean_near * mean_near * qn0_ref[: k_ref.shape[0], out].astype(F32)
+        back = back + mean_far * mean_far * qf0_ref[: k_ref.shape[0], out].astype(F32)
         mine = (ridge_ref[:, out] - c) * k_ref[:, out] + 0.5 * local
         sum_ref[:, out] = mine + 0.5 * (first + second + back)
         part = k_ref[:, out] * (mine + first + second)
@@ -247,8 +256,11 @@
     form_ref[...] = jnp.sum(form.T, axis=0, keepdims=True)
 
 
-def finish_third_kernel(sum_ref, q_ref, next_ref):
-    next_ref[...] = sum_ref[...] + 0.5 * q_ref[...].astype(F32)
+def finish_third_kernel(sum_ref, q_ref, rows3_ref):
+    width = rows3_ref.shape[1]
+    for at in range(0, sum_ref.shape[1], width):
+        out = slice(at, at + width)
+        rows3_ref[out, :] = (sum_ref[:, out] + 0.5 * q_ref[:, out].astype(F32)).T
 
 
 def share(above, below):
@@ -296,7 +308,7 @@
     for at in range(0, targets_ref.shape[0], width):
         out = slice(at, at + width)
         k0 = targets_ref[out, :]
-        k1, k2, k3 = k1_ref[:, out].T, k2_ref[:, out].T, k3_ref[:, out].T
+        k1, k2, k3 = k1_ref[out, :], k2_ref[out, :], k3_ref[out, :]
         solution_ref[out, :] = x[0] * k0 + x[1] * k1 + x[2] * k2
         residual_ref[out, :] = r[0] * k0 + r[1] * k1 + r[2] * k2 + r[3] * k3
 
@@ -313,6 +325,13 @@
     )
 
 
+def forward(value):
+    count = lax.axis_size("asset")
+    return lax.ppermute(
+        value, "asset", [(i, (i - 2 if i % 2 else i + 2) % count) for i in range(count)]
+    )
+
+
 def back(value):
     count = lax.axis_size("asset")
     return lax.ppermute(
@@ -320,8 +339,8 @@
     )
 
 
-def joined(to_near, to_far):
-    return near((to_near.astype(F32) + back(to_far).astype(F32)).astype(BF16))
+def added(to_near, received):
+    return (to_near.astype(F32) + received.astype(F32)).astype(BF16)
 
 
 def sum_step(value, axis, distance):
@@ -364,34 +383,37 @@
     else:
         part, other = lax.all_gather(blocks, "rhs", axis=2, tiled=True), None
 
-    k0, v0, m0 = call(prepare_kernel, (field, shape(BF16, cols + 16, assets), row), (targets, ridge))
-    near0, far0 = near(v0), far(v0)
+    k0, v0, m0 = call(prepare_kernel, (field, rounded, row), (targets,), flops=5 * 10**9)
+    near0 = near(v0)
     band = call(spread_first_kernel, band_shape, (col_index, row_length, part), smem=2)
     if other is not None:
         band = call(
             spread_other_kernel, band_shape, (col_index, row_length, other, band), smem=2, aliases={3: 0}
         )
     distances = [1 << i for i in range(1, (devices - 1).bit_length())]
-    pieces = (field,) * 3
-
-    to_near, to_far = call(products_kernel, (rounded,) * 2, (band, v0))
+    pieces, message = (field,) * 3, shape(BF16, cols + 16, assets)
+
+    to_near, to_far = call(products_first_kernel, (message,) * 2, (band, v0, ridge))
     qf0, qn0 = far(to_far), near(to_near)
-    local0 = call(local_kernel, field, (band, v0))
-    partial, before0, after0, means = call(
-        cross_first_kernel,
-        (*pieces, shape(F32, 8, width)),
-        (band, ridge, k0, local0, v0, near0, far0),
-    )
-    mean = sum_step(means[5:6], "asset", distances[0])
-    mean, partial = together(mean, partial)
-    k1, v1 = call(finish_first_kernel, (field, rounded), (k0, means, partial, qn0, qf0))
+    local0 = call(local_kernel, field, (band, together(v0, to_near)[0]))
+    far0 = forward(together(near0, local0)[0])
+    partial, means = call(
+        gather_first_kernel, (field, shape(F32, 8, width)), (ridge, k0, local0, to_near, qn0, qf0)
+    )
+    k1, v1, before0, after0 = call(
+        cross_first_kernel, (field, rounded, field, field), (band, partial, k0, means, near0, far0)
+    )
 
     to_near1, to_far1 = call(products_kernel, (rounded,) * 2, (band, v1))
-    far1, near1 = far(v1), near(v1)
-    q1 = joined(to_near1, to_far1)
+    received, near1 = back(to_far1), near(v1)
+    far1 = forward(near1)
+    mean = together(means[5:6], to_near1)[0]
+    for distance in distances[:-2]:
+        mean = sum_step(mean, "asset", distance)
+    received, mean = together(received, mean)
+    q1 = near(added(to_near1, received))
     local1 = call(local_kernel, field, (band, v1))
-    mean, _ = together(mean, v1)
-    for distance in distances[1:-1]:
+    for distance in distances[-2:-1]:
         mean = sum_step(mean, "asset", distance)
     partial, before1, after1 = call(
         cross_second_kernel,
@@ -406,9 +428,12 @@
     to_near, to_far, _, _ = call(
         products_third_kernel, (rounded,) * 4, (band, shift, means, to_near1, to_far1, v2)
     )
-    q2 = joined(to_near, to_far)
+    q2 = near(added(to_near, back(to_far)))
     local2 = call(local_kernel, field, (band, v2))
-    s1, s2, pairs = call(settle_kernel, (field, field, shape(F32, 4, cols)), (shift, k0, k1, k2))
+    out = shape(F32, assets, cols)
+    s2, rows1, rows2, pairs = call(
+        settle_kernel, (field, out, out, shape(F32, 4, cols)), (shift, k0, k1, k2)
+    )
     partial, form = call(
         cross_third_kernel,
         (field, row),
@@ -418,9 +443,8 @@
         ),
     )
     moments = sum_over(jnp.concatenate([m0, pairs, form]), "asset")
-    s3 = call(finish_third_kernel, field, (partial, q2))
-    out = shape(F32, assets, cols)
-    return call(combine_kernel, (out, out), (shift, moments, targets, s1, s2, s3))
+    rows3 = call(finish_third_kernel, out, (partial, q2))
+    return call(combine_kernel, (out, out), (shift, moments, targets, rows1, rows2, rows3))
 
 
 def solution(mesh):

time: 87.3 us -> 80.1 us (0.918)
  starting transfers between devices: 36.6 us -> 30.7 us
  local copies, waits for them, and re-layouts: 4.67 us -> 1.17 us
  waiting for transfers between devices: 29.4 us -> 31.8 us
    ppermute x0 -> x2, waiting for transfers between devices: none -> 6.62 us  [forward(): lax.ppermute(value, 'asset', [(i, (i - 2 if i % 2 else i + 2) % count) fo...]
    ppermute x2, waiting for transfers between devices: 4.99 us -> 0.01 us  [back(): lax.ppermute(value, 'asset', [(i, (i + 2 if i % 2 else i - 2) % count) fo...]
    unnamed x14 -> x12, local copies, waits for them, and re-layouts: 4.67 us -> 1.17 us
    ppermute x6, waiting for transfers between devices: 11.1 us -> 8.15 us  [near(): return lax.ppermute(value, 'asset', [(i, i ^ 1) for i in range(count)])]
    ppermute x2, starting transfers between devices: 6.98 us -> 4.21 us  [back(): lax.ppermute(value, 'asset', [(i, (i + 2 if i % 2 else i - 2) % count) fo...]
    ppermute x4 -> x2, starting transfers between devices: 11.8 us -> 9.4 us  [far(): lax.ppermute(value, 'asset', [(i, (i + 1 if i % 2 else i - 1) % count) fo...]
    ppermute x0 -> x2, starting transfers between devices: none -> 1.97 us  [forward(): lax.ppermute(value, 'asset', [(i, (i - 2 if i % 2 else i + 2) % count) fo...]
    ppermute x3, waiting for transfers between devices: 5.96 us -> 7.78 us  [sum_step(): lax.ppermute(value, axis, [(i, i ^ distance) for i in range(count)])]
  transfers between devices with their start and end apart: 22 -> 22, of which waited for: 11 -> 10; matrix products, arithmetic and copies ran while one was open for 0% -> 0% of each run, Pallas kernels for 15% -> 15%
where the time goes in v3:
time: 80.1 us; the launch traced here: 80 us
  waiting for transfers between devices  31.8 us (40%)
  starting transfers between devices  30.7 us (38%)
  Pallas kernels  15.2 us (19%)
  local copies, waits for them, and re-layouts  1.17 us (1%)
  between operations  0.85 us (1%)
    pallas_call x17, Pallas kernels, call(): pl.pallas_call(kernel, out_shape=out_shape, in_specs=specs, out_specs=jax...  15.2 us
    ppermute x2, starting transfers between devices, far(): lax.ppermute(value, 'asset', [(i, (i + 1 if i % 2 else i - 1) % count) fo...  9.4 us
    ppermute x6, starting transfers between devices, sum_over(): total = total + lax.ppermute(value, axis, route)  8.25 us
    ppermute x6, waiting for transfers between devices, near(): return lax.ppermute(value, 'asset', [(i, i ^ 1) for i in range(count)])  8.15 us
    ppermute x3, waiting for transfers between devices, sum_step(): lax.ppermute(value, axis, [(i, i ^ distance) for i in range(count)])  7.78 us
    ppermute x2, waiting for transfers between devices, forward(): lax.ppermute(value, 'asset', [(i, (i - 2 if i % 2 else i + 2) % count) fo...  6.62 us
    ppermute x6, waiting for transfers between devices, sum_over(): total = total + lax.ppermute(value, axis, route)  6.1 us
    ppermute x6, starting transfers between devices, near(): return lax.ppermute(value, 'asset', [(i, i ^ 1) for i in range(count)])  5.99 us
  transfers between devices with their start and end apart: 22, of which 10 were waited for; matrix products, arithmetic and copies ran while one was open for 0% of the time, Pallas kernels for 15%

profile of v3, /device:TPU:0, one launch (start us, length us, event | category | flops | bytes accessed | tf_op | source)
XLA Modules:
  0.0 80.0 jit_solution(14649090534064398896)
XLA Ops:
  0.6 0.5 collective-permute-start
  1.2 1.1 %copy-done.1 = f32[1024,128]{1,0:T(8,128)S(1)} copy-done((f32[1024,128]{1,0:T(8,128)S(1)}, f32[1024,128]{1,0:T(8,128)}, u32[]{:S(2)}) %copy-start.1) | copy-done | bytes 524312
  2.3 0.2 shard_map.70
  2.5 2.6 %collective-permute-start.3 = (bf16[128,1024]{1,0:T(8,128)(2,1)S(1)}, bf16[128,1024]{1,0:T(8,128)(2,1)S(1)}, u32[]{:S(2)}, u32[]{:S(2)}) collective-permute-start(bf16[128,1024]{1,0:T(8,128)(2,1)S(1)} %get-tuple-element.37.v_ref), channel_id=1, source_target_pairs={{0,2},{2,0},{4,6},{6,4},{8,10},{10,8},{12,14},{14,12},{16,18},{18,... | collective-permute-start | bytes 786440 | tf_op jit(solution)/shard_map/ppermute | solution.py:318
  5.1 2.1 %shard_map.68._ = bf16[25,1024,128]{2,1,0:T(8,128)(2,1)S(1)} custom-call(s32[8,16]{1,0:T(8,128)S(1)} %copy-done.4, s32[8]{0:T(128)S(1)} %copy-done.5, bf16[8,16,64,128]{3,2,1,0:T(8,128)(2,1)S(1)} %copy-done), custom_call_target="tpu_custom_call" | custom-call | tf_op jit(solution)/shard_map/pallas_call | solution.py:22
  7.2 0.0 copy-start.3
  7.2 0.0 collective-permute-done.part_ref
  7.2 1.2 %shard_map.69.band_ref = bf16[25,1024,128]{2,1,0:T(8,128)(2,1)S(1)} custom-call(s32[8,16]{1,0:T(8,128)S(1)} %copy-done.4, s32[8]{0:T(128)S(1)} %copy-done.5, bf16[8,16,64,128]{3,2,1,0:T(8,128)(2,1)S(1)} %collective-permute-done.part_ref, bf16[25,1024,128]{2,1,0:T(8,128)(2,1)S(1)} %shard_map.68._), custom_call_target="tpu_custom_call", output_to_operand_aliasing={{}: (3, {})} | custom-call | tf_op jit(solution)/shard_map/pallas_call | solution.py:22
  8.5 0.6 shard_map.71
  9.1 0.8 %collective-permute-start.1 = (bf16[144,1024]{1,0:T(8,128)(2,1)S(1)}, bf16[144,1024]{1,0:T(8,128)(2,1)S(1)}, u32[]{:S(2)}, u32[]{:S(2)}) collective-permute-start(bf16[144,1024]{1,0:T(8,128)(2,1)S(1)} %get-tuple-element.36.own_ref), channel_id=1, source_target_pairs={{0,2},{2,0},{4,6},{6,4},{8,10},{10,8},{12,14},{14,12},{16,18},{18,... | collective-permute-start | bytes 884744 | tf_op jit(solution)/shard_map/ppermute | solution.py:318
  9.9 5.3 %collective-permute-start.2 = (bf16[144,1024]{1,0:T(8,128)(2,1)S(1)}, bf16[144,1024]{1,0:T(8,128)(2,1)S(1)}, u32[]{:S(2)}, u32[]{:S(2)}) collective-permute-start(bf16[144,1024]{1,0:T(8,128)(2,1)S(1)} %get-tuple-element.38), channel_id=1, source_target_pairs={{0,30},{2,4},{4,2},{6,8},{8,6},{10,12},{12,10},{14,16},{16,14},{18... | collective-permute-start | bytes 884744 | tf_op jit(solution)/shard_map/ppermute | solution.py:323
  15.2 1.1 %shard_map.72.local_ref.local0_ref = f32[128,1024]{1,0:T(8,128)S(1)} custom-call(bf16[25,1024,128]{2,1,0:T(8,128)(2,1)S(1)} %shard_map.69.band_ref, bf16[128,1024]{1,0:T(8,128)(2,1)S(1)} %get-tuple-element.37.v_ref), custom_call_target="tpu_custom_call" | custom-call | tf_op jit(solution)/shard_map/pallas_call | solution.py:22
  16.3 0.0 collective-permute-done.3.near_ref
  16.3 0.1 collective-permute-start.4
  16.4 7.5 %collective-permute-done.1.near_ref.qn0_ref = bf16[144,1024]{1,0:T(8,128)(2,1)S(1)} collective-permute-done((bf16[144,1024]{1,0:T(8,128)(2,1)S(1)}, bf16[144,1024]{1,0:T(8,128)(2,1)S(1)}, u32[]{:S(2)}, u32[]{:S(2)}) %collective-permute-start.1) | collective-permute-done | bytes 294944 | tf_op jit(solution)/shard_map/ppermute | solution.py:318
  23.8 0.0 collective-permute-done.2.far_ref.qf0_ref
  23.8 0.1 shard_map.73
  24.0 4.2 %collective-permute-done.4.far_ref = bf16[128,1024]{1,0:T(8,128)(2,1)S(1)} collective-permute-done((bf16[128,1024]{1,0:T(8,128)(2,1)S(1)}, bf16[128,1024]{1,0:T(8,128)(2,1)S(1)}, u32[]{:S(2)}, u32[]{:S(2)}) %collective-permute-start.4) | collective-permute-done | bytes 262176 | tf_op jit(solution)/shard_map/ppermute | solution.py:330
  28.2 1.0 %shard_map.74 = (f32[128,1024]{1,0:T(8,128)S(1)}, bf16[128,1024]{1,0:T(8,128)(2,1)S(1)}, f32[128,1024]{1,0:T(8,128)S(1)}, f32[128,1024]{1,0:T(8,128)S(1)}) custom-call(bf16[25,1024,128]{2,1,0:T(8,128)(2,1)S(1)} %shard_map.69.band_ref, f32[128,1024]{1,0:T(8,128)S(1)} %get-tuple-element.39.sum_ref, f32[128,1024]{1,0:T(8,128)S(1)} %get-tuple-element.34.k_ref.k0_ref, ...), custom_call_target="tpu_custom_call" | custom-call | tf_op jit(solution)/shard_map/pallas_call | solution.py:22
  29.2 0.5 shard_map.75
  29.8 2.7 %collective-permute-start.5 = (bf16[128,1024]{1,0:T(8,128)(2,1)S(1)}, bf16[128,1024]{1,0:T(8,128)(2,1)S(1)}, u32[]{:S(2)}, u32[]{:S(2)}) collective-permute-start(bf16[128,1024]{1,0:T(8,128)(2,1)S(1)} %get-tuple-element.43.far1_ref), channel_id=1, source_target_pairs={{0,28},{2,6},{4,0},{6,10},{8,4},{10,14},{12,8},{14,18},{16,12},{18... | collective-permute-start | bytes 786440 | tf_op jit(solution)/shard_map/ppermute | solution.py:337
  32.5 0.0 collective-permute-start.8
  32.5 0.3 collective-permute-start.6
  32.8 5.4 %collective-permute-done.6 = f32[1,128]{1,0:T(1,128)S(1)} collective-permute-done((f32[1,128]{1,0:T(1,128)S(1)}, f32[1,128]{1,0:T(1,128)S(1)}, u32[]{:S(2)}, u32[]{:S(2)}) %collective-permute-start.6) | collective-permute-done | bytes 544 | tf_op jit(solution)/shard_map/ppermute | solution.py:348
  38.2 0.0 collective-permute-done.5
  38.2 0.7 collective-permute-done.8.near_ref
  38.9 1.9 %collective-permute-start.9 = (bf16[128,1024]{1,0:T(8,128)(2,1)S(1)}, bf16[128,1024]{1,0:T(8,128)(2,1)S(1)}, u32[]{:S(2)}, u32[]{:S(2)}) collective-permute-start(bf16[128,1024]{1,0:T(8,128)(2,1)S(1)} %collective-permute-done.8.near_ref), channel_id=1, source_target_pairs={{0,4},{2,30},{4,8},{6,2},{8,12},{10,6},{12,16},{14,10},{16,20},{18... | collective-permute-start | bytes 786440 | tf_op jit(solution)/shard_map/ppermute | solution.py:330
  40.8 0.1 add_convert_fusion.1
  40.9 1.1 %collective-permute-start.11 = (bf16[128,1024]{1,0:T(8,128)(2,1)S(1)}, bf16[128,1024]{1,0:T(8,128)(2,1)S(1)}, u32[]{:S(2)}, u32[]{:S(2)}) collective-permute-start(bf16[128,1024]{1,0:T(8,128)(2,1)S(1)} %add_convert_fusion.1), channel_id=1, source_target_pairs={{0,2},{2,0},{4,6},{6,4},{8,10},{10,8},{12,14},{14,12},{16,18},{18,... | collective-permute-start | bytes 786440 | tf_op jit(solution)/shard_map/ppermute | solution.py:318
  42.0 0.0 collective-permute-start.7
  42.0 1.1 %shard_map.76.local_ref.local1_ref = f32[128,1024]{1,0:T(8,128)S(1)} custom-call(bf16[25,1024,128]{2,1,0:T(8,128)(2,1)S(1)} %shard_map.69.band_ref, bf16[128,1024]{1,0:T(8,128)(2,1)S(1)} %get-tuple-element.42.v_ref), custom_call_target="tpu_custom_call" | custom-call | tf_op jit(solution)/shard_map/pallas_call | solution.py:22
  43.1 2.4 %collective-permute-done.7 = f32[1,128]{1,0:T(1,128)S(1)} collective-permute-done((f32[1,128]{1,0:T(1,128)S(1)}, f32[1,128]{1,0:T(1,128)S(1)}, u32[]{:S(2)}, u32[]{:S(2)}) %collective-permute-start.7) | collective-permute-done | bytes 544 | tf_op jit(solution)/shard_map/ppermute | solution.py:348
  45.5 2.4 %collective-permute-done.9.far_ref = bf16[128,1024]{1,0:T(8,128)(2,1)S(1)} collective-permute-done((bf16[128,1024]{1,0:T(8,128)(2,1)S(1)}, bf16[128,1024]{1,0:T(8,128)(2,1)S(1)}, u32[]{:S(2)}, u32[]{:S(2)}) %collective-permute-start.9) | collective-permute-done | bytes 262176 | tf_op jit(solution)/shard_map/ppermute | solution.py:330
  48.0 1.1 %shard_map.77 = (f32[128,1024]{1,0:T(8,128)S(1)}, f32[128,1024]{1,0:T(8,128)S(1)}, f32[128,1024]{1,0:T(8,128)S(1)}) custom-call(bf16[25,1024,128]{2,1,0:T(8,128)(2,1)S(1)} %shard_map.69.band_ref, f32[1,1024]{1,0:T(1,128)S(1)} %bitcast.3, f32[8,128]{1,0:T(8,128)S(1)} %get-tuple-element.40.mean_ref, f32[128,1024]{1,0:T(8,128)S(1)} %get-tuple-element.47.k_ref.k1_ref, ...), custom_call_target="tpu_custom_call" | custom-call | tf_op jit(solution)/shard_map/pallas_call | solution.py:22
  49.1 0.1 collective-permute-start.10
  49.1 0.0 collective-permute-done.11.q_ref
  49.2 0.3 shard_map.78
  49.5 0.1 collective-permute-start.12
  49.6 4.1 %collective-permute-start.13 = (bf16[128,1024]{1,0:T(8,128)(2,1)S(1)}, bf16[128,1024]{1,0:T(8,128)(2,1)S(1)}, u32[]{:S(2)}, u32[]{:S(2)}) collective-permute-start(bf16[128,1024]{1,0:T(8,128)(2,1)S(1)} %get-tuple-element.57.v_ref), channel_id=1, source_target_pairs={{0,30},{2,4},{4,2},{6,8},{8,6},{10,12},{12,10},{14,16},{16,14},{18... | collective-permute-start | bytes 786440 | tf_op jit(solution)/shard_map/ppermute | solution.py:323
  53.7 0.0 collective-permute-done.10
  53.7 1.4 %shard_map.82 = (bf16[128,1024]{1,0:T(8,128)(2,1)S(1)}, bf16[128,1024]{1,0:T(8,128)(2,1)S(1)}, bf16[128,1024]{1,0:T(8,128)(2,1)}, bf16[128,1024]{1,0:T(8,128)(2,1)}) custom-call(bf16[25,1024,128]{2,1,0:T(8,128)(2,1)S(1)} %shard_map.69.band_ref, f32[1,128]{1,0:T(1,128)S(1)} %add_multiply_fusion.shift_ref, f32[8,128]{1,0:T(8,128)S(1)} %get-tuple-element.40.mean_ref, ...), custom_call_target="tpu_custom_call" | custom-call | tf_op jit(solution)/shard_map/pallas_call | solution.py:22
  55.1 1.5 %collective-permute-start.20 = (bf16[128,1024]{1,0:T(8,128)(2,1)S(1)}, bf16[128,1024]{1,0:T(8,128)(2,1)S(1)}, u32[]{:S(2)}, u32[]{:S(2)}) collective-permute-start(bf16[128,1024]{1,0:T(8,128)(2,1)S(1)} %get-tuple-element.65), channel_id=1, source_target_pairs={{0,28},{2,6},{4,0},{6,10},{8,4},{10,14},{12,8},{14,18},{16,12},{18... | collective-permute-start | bytes 786440 | tf_op jit(solution)/shard_map/ppermute | solution.py:337
  56.6 1.1 %shard_map.80.local_ref = f32[128,1024]{1,0:T(8,128)S(1)} custom-call(bf16[25,1024,128]{2,1,0:T(8,128)(2,1)S(1)} %shard_map.69.band_ref, bf16[128,1024]{1,0:T(8,128)(2,1)S(1)} %get-tuple-element.57.v_ref), custom_call_target="tpu_custom_call" | custom-call | tf_op jit(solution)/shard_map/pallas_call | solution.py:22
  57.7 0.6 shard_map.79
  58.3 0.0 collective-permute-done.12.near_ref
  58.3 3.1 %collective-permute-done.13.far_ref = bf16[128,1024]{1,0:T(8,128)(2,1)S(1)} collective-permute-done((bf16[128,1024]{1,0:T(8,128)(2,1)S(1)}, bf16[128,1024]{1,0:T(8,128)(2,1)S(1)}, u32[]{:S(2)}, u32[]{:S(2)}) %collective-permute-start.13) | collective-permute-done | bytes 262176 | tf_op jit(solution)/shard_map/ppermute | solution.py:323
  61.4 1.3 %shard_map.81 = (f32[128,1024]{1,0:T(8,128)S(1)}, f32[1,128]{1,0:T(1,128)S(1)}) custom-call(bf16[25,1024,128]{2,1,0:T(8,128)(2,1)S(1)} %shard_map.69.band_ref, f32[1,1024]{1,0:T(1,128)S(1)} %bitcast.4, f32[1,128]{1,0:T(1,128)S(1)} %add_multiply_fusion.shift_ref, f32[8,128]{1,0:T(8,128)S(1)} %get-tuple-element.40.mean_ref, ...), custom_call_target="tpu_custom_call" | custom-call | tf_op jit(solution)/shard_map/pallas_call | solution.py:22
  62.7 1.3 %collective-permute-start.14 = (f32[6,128]{1,0:T(8,128)S(1)}, f32[6,128]{1,0:T(8,128)S(1)}, u32[]{:S(2)}, u32[]{:S(2)}) collective-permute-start(f32[6,128]{1,0:T(8,128)S(1)} %pad_maximum_fusion), channel_id=1, source_target_pairs={{0,2},{2,0},{4,6},{6,4},{8,10},{10,8},{12,14},{14,12},{16,18},{18,... | collective-permute-start | bytes 9224 | tf_op jit(solution)/shard_map/ppermute | solution.py:358
  64.0 0.6 collective-permute-start.15
  64.6 1.7 %collective-permute-start.16 = (f32[6,128]{1,0:T(8,128)S(1)}, f32[6,128]{1,0:T(8,128)S(1)}, u32[]{:S(2)}, u32[]{:S(2)}) collective-permute-start(f32[6,128]{1,0:T(8,128)S(1)} %pad_maximum_fusion), channel_id=1, source_target_pairs={{0,6},{2,4},{4,2},{6,0},{8,14},{10,12},{12,10},{14,8},{16,22},{18,... | collective-permute-start | bytes 9224 | tf_op jit(solution)/shard_map/ppermute | solution.py:358
  66.3 0.0 collective-permute-done.20
  66.3 0.1 add_convert_fusion
  66.4 1.3 %collective-permute-start.21 = (bf16[128,1024]{1,0:T(8,128)(2,1)S(1)}, bf16[128,1024]{1,0:T(8,128)(2,1)S(1)}, u32[]{:S(2)}, u32[]{:S(2)}) collective-permute-start(bf16[128,1024]{1,0:T(8,128)(2,1)S(1)} %add_convert_fusion), channel_id=1, source_target_pairs={{0,2},{2,0},{4,6},{6,4},{8,10},{10,8},{12,14},{14,12},{16,18},{18,... | collective-permute-start | bytes 786440 | tf_op jit(solution)/shard_map/ppermute | solution.py:318
  67.7 0.0 collective-permute-done.14
  67.7 1.4 %collective-permute-done.16 = f32[6,128]{1,0:T(8,128)S(1)} collective-permute-done((f32[6,128]{1,0:T(8,128)S(1)}, f32[6,128]{1,0:T(8,128)S(1)}, u32[]{:S(2)}, u32[]{:S(2)}) %collective-permute-start.16) | collective-permute-done | bytes 3104 | tf_op jit(solution)/shard_map/ppermute | solution.py:358
  69.1 0.5 collective-permute-start.17
  69.7 3.4 %collective-permute-start.18 = (f32[6,128]{1,0:T(8,128)S(1)}, f32[6,128]{1,0:T(8,128)S(1)}, u32[]{:S(2)}, u32[]{:S(2)}) collective-permute-start(f32[6,128]{1,0:T(8,128)S(1)} %add_add_fusion.1), channel_id=1, source_target_pairs={{0,16},{2,18},{4,20},{6,22},{8,24},{10,26},{12,28},{14,30},{16,0},... | collective-permute-start | bytes 9224 | tf_op jit(solution)/shard_map/ppermute | solution.py:358
  73.1 0.8 collective-permute-start.19
  73.8 0.0 collective-permute-done.17
  73.8 0.8 %collective-permute-done.18 = f32[6,128]{1,0:T(8,128)S(1)} collective-permute-done((f32[6,128]{1,0:T(8,128)S(1)}, f32[6,128]{1,0:T(8,128)S(1)}, u32[]{:S(2)}, u32[]{:S(2)}) %collective-permute-start.18) | collective-permute-done | bytes 3104 | tf_op jit(solution)/shard_map/ppermute | solution.py:358
  74.7 3.8 %collective-permute-done.19 = f32[6,128]{1,0:T(8,128)S(1)} collective-permute-done((f32[6,128]{1,0:T(8,128)S(1)}, f32[6,128]{1,0:T(8,128)S(1)}, u32[]{:S(2)}, u32[]{:S(2)}) %collective-permute-start.19) | collective-permute-done | bytes 3104 | tf_op jit(solution)/shard_map/ppermute | solution.py:358
  78.5 0.0 collective-permute-done.21.q_ref
  78.5 0.2 shard_map.83.k3_ref
  78.7 1.3 %shard_map.84 = (f32[1024,128]{1,0:T(8,128)}, f32[1024,128]{1,0:T(8,128)}) custom-call(f32[1,128]{1,0:T(1,128)S(1)} %add_multiply_fusion.shift_ref, f32[6,128]{1,0:T(8,128)S(1)} %add_add_fusion.moment_ref, f32[1024,128]{1,0:T(8,128)S(1)} %copy-done.2, f32[1024,128]{1,0:T(8,128)S(1)} %get-tuple-element.61.k1_ref, f32[1024,128]{1,0:T(8,128)S(1)} %get-tuple-element.62.k2_ref, ...), custom_call_target="tpu_custom_call" | custom-call | tf_op jit(solution)/shard_map/pallas_call | solution.py:22
  (18 shorter events, 0.1 us)
Async XLA Ops:
  0.6 4.5 %copy-start = (bf16[8,16,64,128]{3,2,1,0:T(8,128)(2,1)S(1)}, bf16[8,16,64,128]{3,2,1,0:T(8,128)(2,1)}, u32[]{:S(2)}) copy-start(bf16[8,16,64,128]{3,2,1,0:T(8,128)(2,1)} %part_ref.1) | copy-start | bytes 6291460
  0.6 6.6 %collective-permute-start = (bf16[8,16,64,128]{3,2,1,0:T(8,128)(2,1)}, bf16[8,16,64,128]{3,2,1,0:T(8,128)(2,1)S(1)}, u32[]{:S(2)}, u32[]{:S(2)}) collective-permute-start(bf16[8,16,64,128]{3,2,1,0:T(8,128)(2,1)} %part_ref.1), channel_id=1, source_target_pairs={{0,1},{1,0},{2,3},{3,2},{4,5},{5,4},{6,7},{7,6},{8,9},{9,8},{10,11... | collective-permute-start | bytes 6291464 | tf_op jit(solution)/shard_map/ppermute | solution.py:382
  1.2 1.1 %copy-start.1 = (f32[1024,128]{1,0:T(8,128)S(1)}, f32[1024,128]{1,0:T(8,128)}, u32[]{:S(2)}) copy-start(f32[1024,128]{1,0:T(8,128)} %targets_ref.3) | copy-start | bytes 1572868
  2.3 2.8 %copy-start.4 = (s32[8,16]{1,0:T(8,128)S(1)}, s32[8,16]{1,0:T(8,128)}, u32[]{:S(2)}) copy-start(s32[8,16]{1,0:T(8,128)} %col_ref.3) | copy-start | bytes 1540
  2.3 2.8 %copy-start.5 = (s32[8]{0:T(128)S(1)}, s32[8]{0:T(128)}, u32[]{:S(2)}) copy-start(s32[8]{0:T(128)} %length_ref.3) | copy-start | bytes 100
  2.5 13.8 %collective-permute-start.3 = (bf16[128,1024]{1,0:T(8,128)(2,1)S(1)}, bf16[128,1024]{1,0:T(8,128)(2,1)S(1)}, u32[]{:S(2)}, u32[]{:S(2)}) collective-permute-start(bf16[128,1024]{1,0:T(8,128)(2,1)S(1)} %get-tuple-element.37.v_ref), channel_id=1, source_target_pairs={{0,2},{2,0},{4,6},{6,4},{8,10},{10,8},{12,14},{14,12},{16,18},{18,... | collective-permute-start | bytes 786440 | tf_op jit(solution)/shard_map/ppermute | solution.py:318
  7.2 1.3 %copy-start.3 = (f32[1024]{0:T(1024)S(1)}, f32[1024]{0:T(1024)}, u32[]{:S(2)}) copy-start(f32[1024]{0:T(1024)} %param.6) | copy-start | bytes 12292
  9.1 14.8 %collective-permute-start.1 = (bf16[144,1024]{1,0:T(8,128)(2,1)S(1)}, bf16[144,1024]{1,0:T(8,128)(2,1)S(1)}, u32[]{:S(2)}, u32[]{:S(2)}) collective-permute-start(bf16[144,1024]{1,0:T(8,128)(2,1)S(1)} %get-tuple-element.36.own_ref), channel_id=1, source_target_pairs={{0,2},{2,0},{4,6},{6,4},{8,10},{10,8},{12,14},{14,12},{16,18},{18,... | collective-permute-start | bytes 884744 | tf_op jit(solution)/shard_map/ppermute | solution.py:318
  9.9 13.9 %collective-permute-start.2 = (bf16[144,1024]{1,0:T(8,128)(2,1)S(1)}, bf16[144,1024]{1,0:T(8,128)(2,1)S(1)}, u32[]{:S(2)}, u32[]{:S(2)}) collective-permute-start(bf16[144,1024]{1,0:T(8,128)(2,1)S(1)} %get-tuple-element.38), channel_id=1, source_target_pairs={{0,30},{2,4},{4,2},{6,8},{8,6},{10,12},{12,10},{14,16},{16,14},{18... | collective-permute-start | bytes 884744 | tf_op jit(solution)/shard_map/ppermute | solution.py:323
  16.3 11.9 %collective-permute-start.4 = (bf16[128,1024]{1,0:T(8,128)(2,1)S(1)}, bf16[128,1024]{1,0:T(8,128)(2,1)S(1)}, u32[]{:S(2)}, u32[]{:S(2)}) collective-permute-start(bf16[128,1024]{1,0:T(8,128)(2,1)S(1)} %collective-permute-done.3.near_ref), channel_id=1, source_target_pairs={{0,4},{2,30},{4,8},{6,2},{8,12},{10,6},{12,16},{14,10},{16,20},{18... | collective-permute-start | bytes 786440 | tf_op jit(solution)/shard_map/ppermute | solution.py:330
  29.8 8.4 %collective-permute-start.5 = (bf16[128,1024]{1,0:T(8,128)(2,1)S(1)}, bf16[128,1024]{1,0:T(8,128)(2,1)S(1)}, u32[]{:S(2)}, u32[]{:S(2)}) collective-permute-start(bf16[128,1024]{1,0:T(8,128)(2,1)S(1)} %get-tuple-element.43.far1_ref), channel_id=1, source_target_pairs={{0,28},{2,6},{4,0},{6,10},{8,4},{10,14},{12,8},{14,18},{16,12},{18... | collective-permute-start | bytes 786440 | tf_op jit(solution)/shard_map/ppermute | solution.py:337
  32.5 6.4 %collective-permute-start.8 = (bf16[128,1024]{1,0:T(8,128)(2,1)S(1)}, bf16[128,1024]{1,0:T(8,128)(2,1)S(1)}, u32[]{:S(2)}, u32[]{:S(2)}) collective-permute-start(bf16[128,1024]{1,0:T(8,128)(2,1)S(1)} %get-tuple-element.42.v_ref), channel_id=1, source_target_pairs={{0,2},{2,0},{4,6},{6,4},{8,10},{10,8},{12,14},{14,12},{16,18},{18,... | collective-permute-start | bytes 786440 | tf_op jit(solution)/shard_map/ppermute | solution.py:318
  32.5 5.7 %collective-permute-start.6 = (f32[1,128]{1,0:T(1,128)S(1)}, f32[1,128]{1,0:T(1,128)S(1)}, u32[]{:S(2)}, u32[]{:S(2)}) collective-permute-start(f32[1,128]{1,0:T(1,128)S(1)} %slice.3), channel_id=1, source_target_pairs={{0,4},{2,6},{4,0},{6,2},{8,12},{10,14},{12,8},{14,10},{16,20},{18,... | collective-permute-start | bytes 1544 | tf_op jit(solution)/shard_map/ppermute | solution.py:348
  38.9 9.1 %collective-permute-start.9 = (bf16[128,1024]{1,0:T(8,128)(2,1)S(1)}, bf16[128,1024]{1,0:T(8,128)(2,1)S(1)}, u32[]{:S(2)}, u32[]{:S(2)}) collective-permute-start(bf16[128,1024]{1,0:T(8,128)(2,1)S(1)} %collective-permute-done.8.near_ref), channel_id=1, source_target_pairs={{0,4},{2,30},{4,8},{6,2},{8,12},{10,6},{12,16},{14,10},{16,20},{18... | collective-permute-start | bytes 786440 | tf_op jit(solution)/shard_map/ppermute | solution.py:330
  40.9 8.3 %collective-permute-start.11 = (bf16[128,1024]{1,0:T(8,128)(2,1)S(1)}, bf16[128,1024]{1,0:T(8,128)(2,1)S(1)}, u32[]{:S(2)}, u32[]{:S(2)}) collective-permute-start(bf16[128,1024]{1,0:T(8,128)(2,1)S(1)} %add_convert_fusion.1), channel_id=1, source_target_pairs={{0,2},{2,0},{4,6},{6,4},{8,10},{10,8},{12,14},{14,12},{16,18},{18,... | collective-permute-start | bytes 786440 | tf_op jit(solution)/shard_map/ppermute | solution.py:318
  42.0 3.5 %collective-permute-start.7 = (f32[1,128]{1,0:T(1,128)S(1)}, f32[1,128]{1,0:T(1,128)S(1)}, u32[]{:S(2)}, u32[]{:S(2)}) collective-permute-start(f32[1,128]{1,0:T(1,128)S(1)} %add.33), channel_id=1, source_target_pairs={{0,8},{2,10},{4,12},{6,14},{8,0},{10,2},{12,4},{14,6},{16,24},{18,... | collective-permute-start | bytes 1544 | tf_op jit(solution)/shard_map/ppermute | solution.py:348
  49.1 4.7 %collective-permute-start.10 = (f32[1,128]{1,0:T(1,128)S(1)}, f32[1,128]{1,0:T(1,128)S(1)}, u32[]{:S(2)}, u32[]{:S(2)}) collective-permute-start(f32[1,128]{1,0:T(1,128)S(1)} %add.34), channel_id=1, source_target_pairs={{0,16},{2,18},{4,20},{6,22},{8,24},{10,26},{12,28},{14,30},{16,0},... | collective-permute-start | bytes 1544 | tf_op jit(solution)/shard_map/ppermute | solution.py:348
  49.5 8.8 %collective-permute-start.12 = (bf16[128,1024]{1,0:T(8,128)(2,1)S(1)}, bf16[128,1024]{1,0:T(8,128)(2,1)S(1)}, u32[]{:S(2)}, u32[]{:S(2)}) collective-permute-start(bf16[128,1024]{1,0:T(8,128)(2,1)S(1)} %get-tuple-element.57.v_ref), channel_id=1, source_target_pairs={{0,2},{2,0},{4,6},{6,4},{8,10},{10,8},{12,14},{14,12},{16,18},{18,... | collective-permute-start | bytes 786440 | tf_op jit(solution)/shard_map/ppermute | solution.py:318
  49.6 11.8 %collective-permute-start.13 = (bf16[128,1024]{1,0:T(8,128)(2,1)S(1)}, bf16[128,1024]{1,0:T(8,128)(2,1)S(1)}, u32[]{:S(2)}, u32[]{:S(2)}) collective-permute-start(bf16[128,1024]{1,0:T(8,128)(2,1)S(1)} %get-tuple-element.57.v_ref), channel_id=1, source_target_pairs={{0,30},{2,4},{4,2},{6,8},{8,6},{10,12},{12,10},{14,16},{16,14},{18... | collective-permute-start | bytes 786440 | tf_op jit(solution)/shard_map/ppermute | solution.py:323
  55.1 11.2 %collective-permute-start.20 = (bf16[128,1024]{1,0:T(8,128)(2,1)S(1)}, bf16[128,1024]{1,0:T(8,128)(2,1)S(1)}, u32[]{:S(2)}, u32[]{:S(2)}) collective-permute-start(bf16[128,1024]{1,0:T(8,128)(2,1)S(1)} %get-tuple-element.65), channel_id=1, source_target_pairs={{0,28},{2,6},{4,0},{6,10},{8,4},{10,14},{12,8},{14,18},{16,12},{18... | collective-permute-start | bytes 786440 | tf_op jit(solution)/shard_map/ppermute | solution.py:337
  61.4 17.3 %copy-start.2 = (f32[1024,128]{1,0:T(8,128)S(1)}, f32[1024,128]{1,0:T(8,128)}, u32[]{:S(2)}) copy-start(f32[1024,128]{1,0:T(8,128)} %targets_ref.3) | copy-start | bytes 1572868
  62.7 4.9 %collective-permute-start.14 = (f32[6,128]{1,0:T(8,128)S(1)}, f32[6,128]{1,0:T(8,128)S(1)}, u32[]{:S(2)}, u32[]{:S(2)}) collective-permute-start(f32[6,128]{1,0:T(8,128)S(1)} %pad_maximum_fusion), channel_id=1, source_target_pairs={{0,2},{2,0},{4,6},{6,4},{8,10},{10,8},{12,14},{14,12},{16,18},{18,... | collective-permute-start | bytes 9224 | tf_op jit(solution)/shard_map/ppermute | solution.py:358
  64.0 3.6 %collective-permute-start.15 = (f32[6,128]{1,0:T(8,128)S(1)}, f32[6,128]{1,0:T(8,128)S(1)}, u32[]{:S(2)}, u32[]{:S(2)}) collective-permute-start(f32[6,128]{1,0:T(8,128)S(1)} %pad_maximum_fusion), channel_id=1, source_target_pairs={{0,4},{2,6},{4,0},{6,2},{8,12},{10,14},{12,8},{14,10},{16,20},{18,... | collective-permute-start | bytes 9224 | tf_op jit(solution)/shard_map/ppermute | solution.py:358
  64.6 4.5 %collective-permute-start.16 = (f32[6,128]{1,0:T(8,128)S(1)}, f32[6,128]{1,0:T(8,128)S(1)}, u32[]{:S(2)}, u32[]{:S(2)}) collective-permute-start(f32[6,128]{1,0:T(8,128)S(1)} %pad_maximum_fusion), channel_id=1, source_target_pairs={{0,6},{2,4},{4,2},{6,0},{8,14},{10,12},{12,10},{14,8},{16,22},{18,... | collective-permute-start | bytes 9224 | tf_op jit(solution)/shard_map/ppermute | solution.py:358
  66.4 12.1 %collective-permute-start.21 = (bf16[128,1024]{1,0:T(8,128)(2,1)S(1)}, bf16[128,1024]{1,0:T(8,128)(2,1)S(1)}, u32[]{:S(2)}, u32[]{:S(2)}) collective-permute-start(bf16[128,1024]{1,0:T(8,128)(2,1)S(1)} %add_convert_fusion), channel_id=1, source_target_pairs={{0,2},{2,0},{4,6},{6,4},{8,10},{10,8},{12,14},{14,12},{16,18},{18,... | collective-permute-start | bytes 786440 | tf_op jit(solution)/shard_map/ppermute | solution.py:318
  69.1 4.7 %collective-permute-start.17 = (f32[6,128]{1,0:T(8,128)S(1)}, f32[6,128]{1,0:T(8,128)S(1)}, u32[]{:S(2)}, u32[]{:S(2)}) collective-permute-start(f32[6,128]{1,0:T(8,128)S(1)} %add_add_fusion.1), channel_id=1, source_target_pairs={{0,8},{2,10},{4,12},{6,14},{8,0},{10,2},{12,4},{14,6},{16,24},{18,... | collective-permute-start | bytes 9224 | tf_op jit(solution)/shard_map/ppermute | solution.py:358
  69.7 5.0 %collective-permute-start.18 = (f32[6,128]{1,0:T(8,128)S(1)}, f32[6,128]{1,0:T(8,128)S(1)}, u32[]{:S(2)}, u32[]{:S(2)}) collective-permute-start(f32[6,128]{1,0:T(8,128)S(1)} %add_add_fusion.1), channel_id=1, source_target_pairs={{0,16},{2,18},{4,20},{6,22},{8,24},{10,26},{12,28},{14,30},{16,0},... | collective-permute-start | bytes 9224 | tf_op jit(solution)/shard_map/ppermute | solution.py:358
  73.1 5.4 %collective-permute-start.19 = (f32[6,128]{1,0:T(8,128)S(1)}, f32[6,128]{1,0:T(8,128)S(1)}, u32[]{:S(2)}, u32[]{:S(2)}) collective-permute-start(f32[6,128]{1,0:T(8,128)S(1)} %add_add_fusion.1), channel_id=1, source_target_pairs={{0,24},{2,26},{4,28},{6,30},{8,16},{10,18},{12,20},{14,22},{16,8},... | collective-permute-start | bytes 9224 | tf_op jit(solution)/shard_map/ppermute | solution.py:358

commit v4 on v3

--- a/solution.py
+++ b/solution.py
@@ -68,7 +68,9 @@
     lax.fori_loop(0, rows, one_row, 0)
 
 
-def spread_first_kernel(col_ref, length_ref, part_ref, band_ref):
+def spread_first_kernel(col_ref, length_ref, part_ref, ridge_ref, band_ref, mean_ref):
+    mean = jnp.sum(ridge_ref[...], axis=1, keepdims=True) / ridge_ref.shape[1]
+    mean_ref[...] = jnp.broadcast_to(mean, mean_ref.shape)
     band_ref[...] = jnp.zeros_like(band_ref)
     height = part_ref.shape[2]
     mine = 0 if height == part_ref.shape[3] else lax.axis_index("rhs") * height
@@ -119,13 +121,11 @@
     far_ref[cols:, :] = rest
 
 
-def products_third_kernel(
-    band_ref, shift_ref, mean_ref, near1_ref, far1_ref, v_ref, near_ref, far_ref, near2_ref, far2_ref
-):
-    products_kernel(band_ref, v_ref, near2_ref, far2_ref)
-    gap = 2 * (mean_ref[0:1, 0:1] - shift_ref[0:1, 0:1])
-    near_ref[...] = (near2_ref[...].astype(F32) + gap * near1_ref[...].astype(F32)).astype(BF16)
-    far_ref[...] = (far2_ref[...].astype(F32) + gap * far1_ref[...].astype(F32)).astype(BF16)
+def products_second_kernel(band_ref, v_ref, mean_ref, near_ref, far_ref):
+    products_kernel(band_ref, v_ref, near_ref, far_ref)
+    cols = v_ref.shape[0]
+    rest = (far_ref.shape[0] - cols, far_ref.shape[1])
+    far_ref[cols:, :] = jnp.broadcast_to(mean_ref[0:1, 0:1], rest).astype(BF16)
 
 
 def local_kernel(band_ref, v_ref, out_ref):
@@ -206,54 +206,76 @@
         sum_ref[:, out] = ridge_ref[:, out] * k_ref[:, out] + 0.5 * both
 
 
-def finish_second_kernel(k0_ref, k_ref, mean_ref, sum_ref, q_ref, next_ref, rounded_ref):
-    value = sum_ref[...] + 0.5 * q_ref[...].astype(F32)
+def finish_second_kernel(
+    k0_ref, k_ref, mean_ref, sum_ref, own_ref, q_ref, next_ref, rounded_ref, total_ref
+):
+    cols, width = k_ref.shape[0], total_ref.shape[1]
+    sums = [ref[cols : cols + 8, :width].astype(F32)[:1] for ref in (own_ref, q_ref)]
+    total_ref[...] = sums[0] + sums[1]
+    value = sum_ref[...] + 0.5 * q_ref[:cols, :].astype(F32)
     next_ref[...] = value
     own = mean_ref[0:1, 0:1]
     rounded_ref[...] = (value - 2 * own * k_ref[...] + own * own * k0_ref[...]).astype(BF16)
 
 
-def settle_kernel(shift_ref, k0_ref, k1_ref, k2_ref, s2_ref, rows1_ref, rows2_ref, moment_ref):
+def settle_kernel(
+    shift_ref, mean_ref, ridge_ref, k0_ref, k1_ref, k2_ref, local0_ref, local1_ref, local2_ref,
+    before0_ref, before1_ref, after0_ref, after1_ref, qn0_ref, qf0_ref,
+    sum_ref, rows1_ref, rows2_ref, moment_ref
+):
+    cols, width = k0_ref.shape[0], moment_ref.shape[1]
+    c = shift_ref[0:1, 0:1]
+    own, mean_near, mean_far, mean_before, mean_after = (mean_ref[i : i + 1, 0:1] - c for i in range(5))
+    totals = [jnp.zeros((cols, width), F32)] * 5
+    for at in range(0, k0_ref.shape[1], width):
+        out = slice(at, at + width)
+        k0, k1 = k0_ref[:, out], k1_ref[:, out]
+        s1 = k1 - c * k0
+        s2 = k2_ref[:, out] - 2 * c * k1 + c * c * k0
+        rows1_ref[out, :] = s1.T
+        rows2_ref[out, :] = s2.T
+        local = local2_ref[:, out] + 2 * own * local1_ref[:, out] + own * own * local0_ref[:, out]
+        mine = (ridge_ref[:, out] - c) * s2 + 0.5 * local
+        known = 2 * mean_before * before1_ref[:, out] + mean_before * mean_before * before0_ref[:, out]
+        known = known + 2 * mean_after * after1_ref[:, out] + mean_after * mean_after * after0_ref[:, out]
+        back = mean_near * mean_near * qn0_ref[:cols, out].astype(F32)
+        back = back + mean_far * mean_far * qf0_ref[:cols, out].astype(F32)
+        sum_ref[:, out] = mine + 0.5 * (known + back)
+        parts = (k0 * s1, s1 * s1, s1 * s2, s2 * s2, s2 * (mine + back))
+        totals = [total + part for total, part in zip(totals, parts, strict=True)]
+    for i, total in enumerate(totals):
+        moment_ref[i : i + 1, :] = jnp.sum(total.T, axis=0, keepdims=True)
+
+
+def form_kernel(
+    shift_ref, mean_ref, m0_ref, pairs_ref, to2_ref, to1_ref, r2_ref, r1_ref, near2_ref, near1_ref, near0_ref,
+    q_ref, moment_ref
+):
+    cols, assets = to2_ref.shape
     width = moment_ref.shape[1]
     c = shift_ref[0:1, 0:1]
-    k0, k1 = k0_ref[...], k1_ref[...]
-    s1 = k1 - c * k0
-    s2 = k2_ref[...] - 2 * c * k1 + c * c * k0
-    s2_ref[...] = s2
-    for at in range(0, k0.shape[1], width):
-        rows1_ref[at : at + width, :] = s1[:, at : at + width].T
-        rows2_ref[at : at + width, :] = s2[:, at : at + width].T
-    for i, value in enumerate((k0 * s1, s1 * s1, s1 * s2, s2 * s2)):
-        moment_ref[i : i + 1, :] = column_sums(value, width)
-
-
-def cross_third_kernel(
-    band_ref, ridge_ref, shift_ref, mean_ref, k_ref, local0_ref, local1_ref, local_ref,
-    before0_ref, before1_ref, after0_ref, after1_ref, qn0_ref, qf0_ref,
-    near_ref, far_ref, sum_ref, form_ref
-):
-    width = form_ref.shape[1]
-    c = shift_ref[0:1, 0:1]
-    own, mean_near, mean_far, mean_before, mean_after = (mean_ref[i : i + 1, 0:1] - c for i in range(5))
-    before, after = neighbours(near_ref, far_ref, k_ref.shape[0])
-    form = jnp.zeros((k_ref.shape[0], width), F32)
-
-    def known(gap, zeroth_ref, first_ref, out):
-        zeroth, first = zeroth_ref[:, out].astype(F32), first_ref[:, out].astype(F32)
-        return 2 * gap * first + gap * gap * zeroth
-
+    own, gap = mean_ref[0:1, 0:1] - c, mean_ref[1:2, 0:1] - c
+    other = r1_ref[cols : cols + 8, :width].astype(F32)[:1, :1] - c
+    total = jnp.zeros((cols, width), F32)
+    for at in range(0, assets, width):
+        out = slice(at, at + width)
+        both = to2_ref[:, out].astype(F32) + 2 * own * to1_ref[:, out].astype(F32)
+        both = both + r2_ref[:, out].astype(F32) + 2 * other * r1_ref[:cols, out].astype(F32)
+        field = near2_ref[:, out].astype(F32) + 2 * gap * near1_ref[:, out].astype(F32)
+        field = field + gap * gap * near0_ref[:, out].astype(F32)
+        q_ref[:, out] = both.astype(BF16)
+        total = total + both * field
+    moment_ref[0:1, :] = m0_ref[...]
+    moment_ref[1:5, :] = pairs_ref[0:4, :]
+    moment_ref[5:6, :] = pairs_ref[4:5, :] + jnp.sum(total.T, axis=0, keepdims=True)
+    moment_ref[6:8, :] = jnp.zeros((2, width), F32)
+
+
+def cross_third_kernel(band_ref, known_ref, near_ref, far_ref, sum_ref):
+    before, after = neighbours(near_ref, far_ref, known_ref.shape[0])
     for j in range(0, band_ref.shape[0] // 3, 2):
         out, first, second = forward_products(band_ref, before, after, j)
-        first = first + known(mean_before, before0_ref, before1_ref, out)
-        second = second + known(mean_after, after0_ref, after1_ref, out)
-        local = local_ref[:, out] + known(own, local0_ref, local1_ref, out)
-        back = mean_near * mean_near * qn0_ref[: k_ref.shape[0], out].astype(F32)
-        back = back + mean_far * mean_far * qf0_ref[: k_ref.shape[0], out].astype(F32)
-        mine = (ridge_ref[:, out] - c) * k_ref[:, out] + 0.5 * local
-        sum_ref[:, out] = mine + 0.5 * (first + second + back)
-        part = k_ref[:, out] * (mine + first + second)
-        form = form + part[:, :width] + part[:, width:]
-    form_ref[...] = jnp.sum(form.T, axis=0, keepdims=True)
+        sum_ref[:, out] = known_ref[:, out] + 0.5 * (first + second)
 
 
 def finish_third_kernel(sum_ref, q_ref, rows3_ref):
@@ -339,13 +361,24 @@
     )
 
 
-def added(to_near, received):
-    return (to_near.astype(F32) + received.astype(F32)).astype(BF16)
+def add_kernel(near_ref, received_ref, mean_ref, out_ref):
+    cols = near_ref.shape[0]
+    out_ref[:cols, :] = (near_ref[...].astype(F32) + received_ref[:cols, :].astype(F32)).astype(BF16)
+    rest = (out_ref.shape[0] - cols, out_ref.shape[1])
+    out_ref[cols:, :] = jnp.broadcast_to(mean_ref[0:1, 0:1], rest).astype(BF16)
 
 
 def sum_step(value, axis, distance):
     count = lax.axis_size(axis)
     return value + lax.ppermute(value, axis, [(i, i ^ distance) for i in range(count)])
+
+
+def sum_four(value, axis, first, second):
+    count = lax.axis_size(axis)
+    total = value
+    for distance in (first, second, first + second):
+        total = total + lax.ppermute(value, axis, [(i, i ^ distance) for i in range(count)])
+    return total
 
 
 def sum_over(value, axis):
@@ -385,7 +418,12 @@
 
     k0, v0, m0 = call(prepare_kernel, (field, rounded, row), (targets,), flops=5 * 10**9)
     near0 = near(v0)
-    band = call(spread_first_kernel, band_shape, (col_index, row_length, part), smem=2)
+    band, mean = call(
+        spread_first_kernel,
+        (band_shape, shape(F32, 1, width)),
+        (col_index, row_length, part, ridge),
+        smem=2,
+    )
     if other is not None:
         band = call(
             spread_other_kernel, band_shape, (col_index, row_length, other, band), smem=2, aliases={3: 0}
@@ -397,6 +435,10 @@
     qf0, qn0 = far(to_far), near(to_near)
     local0 = call(local_kernel, field, (band, together(v0, to_near)[0]))
     far0 = forward(together(near0, local0)[0])
+    mean = together(mean, local0)[0]
+    for distance in distances[1:-1]:
+        mean = sum_step(mean, "asset", distance)
+    mean, local0 = together(mean, local0)
     partial, means = call(
         gather_first_kernel, (field, shape(F32, 8, width)), (ridge, k0, local0, to_near, qn0, qf0)
     )
@@ -404,45 +446,47 @@
         cross_first_kernel, (field, rounded, field, field), (band, partial, k0, means, near0, far0)
     )
 
-    to_near1, to_far1 = call(products_kernel, (rounded,) * 2, (band, v1))
+    to_near1, to_far1 = call(products_second_kernel, (rounded, message), (band, v1, means))
     received, near1 = back(to_far1), near(v1)
     far1 = forward(near1)
-    mean = together(means[5:6], to_near1)[0]
-    for distance in distances[:-2]:
-        mean = sum_step(mean, "asset", distance)
-    received, mean = together(received, mean)
-    q1 = near(added(to_near1, received))
+    mean = sum_four(together(mean, to_near1)[0], "asset", distances[0], distances[-1])
+    joined = call(add_kernel, message, (to_near1, received, mean))
+    q1 = near(joined)
     local1 = call(local_kernel, field, (band, v1))
-    for distance in distances[-2:-1]:
-        mean = sum_step(mean, "asset", distance)
     partial, before1, after1 = call(
         cross_second_kernel,
         pieces,
         (band, ridge, means, k1, local0, local1, before0, after0, qn0, qf0, near1, far1),
     )
-    mean, _ = together(mean, partial)
-    shift = sum_step(mean, "asset", distances[-1]) / devices
-    k2, v2 = call(finish_second_kernel, (field, rounded), (k0, k1, means, partial, q1))
-
-    far2, near2 = far(v2), near(v2)
-    to_near, to_far, _, _ = call(
-        products_third_kernel, (rounded,) * 4, (band, shift, means, to_near1, to_far1, v2)
-    )
-    q2 = near(added(to_near, back(to_far)))
+    k2, v2, mean = call(
+        finish_second_kernel,
+        (field, rounded, shape(F32, 1, width)),
+        (k0, k1, means, partial, joined, q1),
+    )
+
+    to_near2, to_far2 = call(products_kernel, (rounded,) * 2, (band, v2))
+    near2 = near(together(v2, to_near2)[0])
+    far2 = forward(near2)
+    received2 = back(to_far2)
     local2 = call(local_kernel, field, (band, v2))
+    shift = mean / devices
     out = shape(F32, assets, cols)
-    s2, rows1, rows2, pairs = call(
-        settle_kernel, (field, out, out, shape(F32, 4, cols)), (shift, k0, k1, k2)
-    )
-    partial, form = call(
-        cross_third_kernel,
-        (field, row),
+    known, rows1, rows2, pairs = call(
+        settle_kernel,
+        (field, out, out, shape(F32, 8, cols)),
         (
-            band, ridge, shift, means, s2, local0, local1, local2, before0, before1, after0, after1,
-            qn0, qf0, near2, far2,
+            shift, means, ridge, k0, k1, k2, local0, local1, local2,
+            before0, before1, after0, after1, qn0, qf0,
         ),
     )
-    moments = sum_over(jnp.concatenate([m0, pairs, form]), "asset")
+    joined, moments = call(
+        form_kernel,
+        (rounded, shape(F32, 8, cols)),
+        (shift, means, m0, pairs, to_near2, to_near1, received2, received, near2, near1, near0),
+    )
+    moments = sum_over(moments, "asset")
+    q2 = near(joined)
+    partial = call(cross_third_kernel, field, (band, known, near2, far2))
     rows3 = call(finish_third_kernel, out, (partial, q2))
     return call(combine_kernel, (out, out), (shift, moments, targets, rows1, rows2, rows3))
 

time: 80.1 us -> 77.1 us (0.963)
  waiting for transfers between devices: 31.8 us -> 28.1 us
    ppermute x6, waiting for transfers between devices: 8.15 us -> 1.7 us  [near(): return lax.ppermute(value, 'asset', [(i, i ^ 1) for i in range(count)])]
    ppermute x0 -> x3, starting transfers between devices: none -> 4.39 us  [sum_four(): lax.ppermute(value, axis, [(i, i ^ distance) for i in range(count)])]
    ppermute x2 -> x1, starting transfers between devices: 9.4 us -> 5.25 us  [far(): lax.ppermute(value, 'asset', [(i, (i + 1 if i % 2 else i - 1) % count) fo...]
    ppermute x2 -> x3, waiting for transfers between devices: 6.62 us -> 10.4 us  [forward(): lax.ppermute(value, 'asset', [(i, (i - 2 if i % 2 else i + 2) % count) fo...]
    ppermute x2 -> x1, waiting for transfers between devices: 3.15 us -> 0.01 us  [far(): lax.ppermute(value, 'asset', [(i, (i + 1 if i % 2 else i - 1) % count) fo...]
    ppermute x2, waiting for transfers between devices: 0.01 us -> 3.06 us  [back(): lax.ppermute(value, 'asset', [(i, (i + 2 if i % 2 else i - 2) % count) fo...]
    ppermute x0 -> x3, waiting for transfers between devices: none -> 2.41 us  [sum_four(): lax.ppermute(value, axis, [(i, i ^ distance) for i in range(count)])]
    ppermute x6, waiting for transfers between devices: 6.1 us -> 4.38 us  [sum_over(): total = total + lax.ppermute(value, axis, route)]
  transfers between devices with their start and end apart: 22 -> 23, of which waited for: 10 -> 12; matrix products, arithmetic and copies ran while one was open for 0% -> 0% of each run, Pallas kernels for 15% -> 14%
where the time goes in v4:
time: 77.1 us; the launch traced here: 77 us
  starting transfers between devices  31.5 us (41%)
  waiting for transfers between devices  28.1 us (36%)
  Pallas kernels  15.3 us (20%)
  local copies, waits for them, and re-layouts  1.17 us (2%)
  between operations  0.87 us (1%)
    pallas_call x19, Pallas kernels, call(): pl.pallas_call(kernel, out_shape=out_shape, in_specs=specs, out_specs=jax...  15.3 us
    ppermute x3, waiting for transfers between devices, forward(): lax.ppermute(value, 'asset', [(i, (i - 2 if i % 2 else i + 2) % count) fo...  10.4 us
    ppermute x6, starting transfers between devices, sum_over(): total = total + lax.ppermute(value, axis, route)  8.5 us
    ppermute x6, starting transfers between devices, near(): return lax.ppermute(value, 'asset', [(i, i ^ 1) for i in range(count)])  7.56 us
    ppermute x1, waiting for transfers between devices, sum_step(): lax.ppermute(value, axis, [(i, i ^ distance) for i in range(count)])  6.11 us
    ppermute x1, starting transfers between devices, far(): lax.ppermute(value, 'asset', [(i, (i + 1 if i % 2 else i - 1) % count) fo...  5.25 us
    ppermute x3, starting transfers between devices, sum_four(): lax.ppermute(value, axis, [(i, i ^ distance) for i in range(count)])  4.39 us
    ppermute x6, waiting for transfers between devices, sum_over(): total = total + lax.ppermute(value, axis, route)  4.38 us
  transfers between devices with their start and end apart: 23, of which 12 were waited for; matrix products, arithmetic and copies ran while one was open for 0% of the time, Pallas kernels for 14%

profile of v4, /device:TPU:0, one launch (start us, length us, event | category | flops | bytes accessed | tf_op | source)
XLA Modules:
  0.0 77.0 jit_solution(13838324599730984820)
XLA Ops:
  0.6 0.5 collective-permute-start
  1.2 1.1 %copy-done.1 = f32[1024,128]{1,0:T(8,128)S(1)} copy-done((f32[1024,128]{1,0:T(8,128)S(1)}, f32[1024,128]{1,0:T(8,128)}, u32[]{:S(2)}) %copy-start.1) | copy-done | bytes 524312
  2.3 0.2 shard_map.68
  2.5 2.6 %collective-permute-start.4 = (bf16[128,1024]{1,0:T(8,128)(2,1)S(1)}, bf16[128,1024]{1,0:T(8,128)(2,1)S(1)}, u32[]{:S(2)}, u32[]{:S(2)}) collective-permute-start(bf16[128,1024]{1,0:T(8,128)(2,1)S(1)} %get-tuple-element.43.v_ref), channel_id=1, source_target_pairs={{0,2},{2,0},{4,6},{6,4},{8,10},{10,8},{12,14},{14,12},{16,18},{18,... | collective-permute-start | bytes 786440 | tf_op jit(solution)/shard_map/ppermute | solution.py:340
  5.1 2.1 %shard_map.69 = (bf16[25,1024,128]{2,1,0:T(8,128)(2,1)S(1)}, f32[1,128]{1,0:T(1,128)S(1)}) custom-call(s32[8,16]{1,0:T(8,128)S(1)} %copy-done.4, s32[8]{0:T(128)S(1)} %copy-done.5, bf16[8,16,64,128]{3,2,1,0:T(8,128)(2,1)S(1)} %copy-done, f32[1,1024]{1,0:T(1,128)S(1)} %bitcast.1), custom_call_target="tpu_custom_call" | custom-call | tf_op jit(solution)/shard_map/pallas_call | solution.py:22
  7.2 0.0 collective-permute-done.part_ref
  7.2 1.2 %shard_map.70.band_ref = bf16[25,1024,128]{2,1,0:T(8,128)(2,1)S(1)} custom-call(s32[8,16]{1,0:T(8,128)S(1)} %copy-done.4, s32[8]{0:T(128)S(1)} %copy-done.5, bf16[8,16,64,128]{3,2,1,0:T(8,128)(2,1)S(1)} %collective-permute-done.part_ref, bf16[25,1024,128]{2,1,0:T(8,128)(2,1)S(1)} %get-tuple-element.39._), custom_call_target="tpu_custom_call", output_to_operand_aliasing={{}: (3, {})} | custom-call | tf_op jit(solution)/shard_map/pallas_call | solution.py:22
  8.5 0.5 shard_map.71
  9.1 0.8 %collective-permute-start.2 = (bf16[144,1024]{1,0:T(8,128)(2,1)S(1)}, bf16[144,1024]{1,0:T(8,128)(2,1)S(1)}, u32[]{:S(2)}, u32[]{:S(2)}) collective-permute-start(bf16[144,1024]{1,0:T(8,128)(2,1)S(1)} %get-tuple-element.42.own_ref), channel_id=1, source_target_pairs={{0,2},{2,0},{4,6},{6,4},{8,10},{10,8},{12,14},{14,12},{16,18},{18,... | collective-permute-start | bytes 884744 | tf_op jit(solution)/shard_map/ppermute | solution.py:340
  9.9 5.3 %collective-permute-start.3 = (bf16[144,1024]{1,0:T(8,128)(2,1)S(1)}, bf16[144,1024]{1,0:T(8,128)(2,1)S(1)}, u32[]{:S(2)}, u32[]{:S(2)}) collective-permute-start(bf16[144,1024]{1,0:T(8,128)(2,1)S(1)} %get-tuple-element.46), channel_id=1, source_target_pairs={{0,30},{2,4},{4,2},{6,8},{8,6},{10,12},{12,10},{14,16},{16,14},{18... | collective-permute-start | bytes 884744 | tf_op jit(solution)/shard_map/ppermute | solution.py:345
  15.1 1.1 %shard_map.72.local_ref.local0_ref = f32[128,1024]{1,0:T(8,128)S(1)} custom-call(bf16[25,1024,128]{2,1,0:T(8,128)(2,1)S(1)} %shard_map.70.band_ref, bf16[128,1024]{1,0:T(8,128)(2,1)S(1)} %get-tuple-element.43.v_ref), custom_call_target="tpu_custom_call" | custom-call | tf_op jit(solution)/shard_map/pallas_call | solution.py:22
  16.3 0.0 collective-permute-done.4.near_ref.near0_ref
  16.3 0.1 collective-permute-start.5
  16.3 0.1 collective-permute-start.1
  16.4 6.1 %collective-permute-done.1 = f32[1,128]{1,0:T(1,128)S(1)} collective-permute-done((f32[1,128]{1,0:T(1,128)S(1)}, f32[1,128]{1,0:T(1,128)S(1)}, u32[]{:S(2)}, u32[]{:S(2)}) %collective-permute-start.1) | collective-permute-done | bytes 544 | tf_op jit(solution)/shard_map/ppermute | solution.py:373
  22.5 1.3 %collective-permute-done.2.near_ref.qn0_ref = bf16[144,1024]{1,0:T(8,128)(2,1)S(1)} collective-permute-done((bf16[144,1024]{1,0:T(8,128)(2,1)S(1)}, bf16[144,1024]{1,0:T(8,128)(2,1)S(1)}, u32[]{:S(2)}, u32[]{:S(2)}) %collective-permute-start.2) | collective-permute-done | bytes 294944 | tf_op jit(solution)/shard_map/ppermute | solution.py:340
  23.8 0.0 collective-permute-done.3.far_ref.qf0_ref
  23.8 0.1 shard_map.73
  24.0 4.2 %collective-permute-done.5.far_ref = bf16[128,1024]{1,0:T(8,128)(2,1)S(1)} collective-permute-done((bf16[128,1024]{1,0:T(8,128)(2,1)S(1)}, bf16[128,1024]{1,0:T(8,128)(2,1)S(1)}, u32[]{:S(2)}, u32[]{:S(2)}) %collective-permute-start.5) | collective-permute-done | bytes 262176 | tf_op jit(solution)/shard_map/ppermute | solution.py:352
  28.2 1.0 %shard_map.74 = (f32[128,1024]{1,0:T(8,128)S(1)}, bf16[128,1024]{1,0:T(8,128)(2,1)S(1)}, f32[128,1024]{1,0:T(8,128)S(1)}, f32[128,1024]{1,0:T(8,128)S(1)}) custom-call(bf16[25,1024,128]{2,1,0:T(8,128)(2,1)S(1)} %shard_map.70.band_ref, f32[128,1024]{1,0:T(8,128)S(1)} %get-tuple-element.47.sum_ref, f32[128,1024]{1,0:T(8,128)S(1)} %get-tuple-element.38.k_ref.k0_ref, ...), custom_call_target="tpu_custom_call" | custom-call | tf_op jit(solution)/shard_map/pallas_call | solution.py:22
  29.2 0.6 shard_map.77
  29.8 2.7 %collective-permute-start.8 = (bf16[144,1024]{1,0:T(8,128)(2,1)S(1)}, bf16[144,1024]{1,0:T(8,128)(2,1)S(1)}, u32[]{:S(2)}, u32[]{:S(2)}) collective-permute-start(bf16[144,1024]{1,0:T(8,128)(2,1)S(1)} %get-tuple-element.56), channel_id=1, source_target_pairs={{0,28},{2,6},{4,0},{6,10},{8,4},{10,14},{12,8},{14,18},{16,12},{18... | collective-permute-start | bytes 884744 | tf_op jit(solution)/shard_map/ppermute | solution.py:359
  32.5 2.4 %collective-permute-start.11 = (f32[1,128]{1,0:T(1,128)S(1)}, f32[1,128]{1,0:T(1,128)S(1)}, u32[]{:S(2)}, u32[]{:S(2)}) collective-permute-start(f32[1,128]{1,0:T(1,128)S(1)} %add.30), channel_id=1, source_target_pairs={{0,20},{2,22},{4,16},{6,18},{8,28},{10,30},{12,24},{14,26},{16,4},... | collective-permute-start | bytes 1544 | tf_op jit(solution)/shard_map/ppermute | solution.py:380
  34.8 0.3 collective-permute-start.10
  35.2 1.7 %collective-permute-start.9 = (f32[1,128]{1,0:T(1,128)S(1)}, f32[1,128]{1,0:T(1,128)S(1)}, u32[]{:S(2)}, u32[]{:S(2)}) collective-permute-start(f32[1,128]{1,0:T(1,128)S(1)} %add.30), channel_id=1, source_target_pairs={{0,4},{2,6},{4,0},{6,2},{8,12},{10,14},{12,8},{14,10},{16,20},{18,... | collective-permute-start | bytes 1544 | tf_op jit(solution)/shard_map/ppermute | solution.py:380
  36.9 1.0 %collective-permute-done.11 = f32[1,128]{1,0:T(1,128)S(1)} collective-permute-done((f32[1,128]{1,0:T(1,128)S(1)}, f32[1,128]{1,0:T(1,128)S(1)}, u32[]{:S(2)}, u32[]{:S(2)}) %collective-permute-start.11) | collective-permute-done | bytes 544 | tf_op jit(solution)/shard_map/ppermute | solution.py:380
  37.8 1.5 %collective-permute-done.10 = f32[1,128]{1,0:T(1,128)S(1)} collective-permute-done((f32[1,128]{1,0:T(1,128)S(1)}, f32[1,128]{1,0:T(1,128)S(1)}, u32[]{:S(2)}, u32[]{:S(2)}) %collective-permute-start.10) | collective-permute-done | bytes 544 | tf_op jit(solution)/shard_map/ppermute | solution.py:380
  39.3 0.0 collective-permute-done.9
  39.3 0.1 shard_map.78.own_ref
  39.4 1.2 %collective-permute-start.12 = (bf16[144,1024]{1,0:T(8,128)(2,1)S(1)}, bf16[144,1024]{1,0:T(8,128)(2,1)S(1)}, u32[]{:S(2)}, u32[]{:S(2)}) collective-permute-start(bf16[144,1024]{1,0:T(8,128)(2,1)S(1)} %shard_map.78.own_ref), channel_id=1, source_target_pairs={{0,2},{2,0},{4,6},{6,4},{8,10},{10,8},{12,14},{14,12},{16,18},{18,... | collective-permute-start | bytes 884744 | tf_op jit(solution)/shard_map/ppermute | solution.py:340
  40.6 0.0 collective-permute-done.6.near_ref.near1_ref
  40.6 2.0 %collective-permute-start.7 = (bf16[128,1024]{1,0:T(8,128)(2,1)S(1)}, bf16[128,1024]{1,0:T(8,128)(2,1)S(1)}, u32[]{:S(2)}, u32[]{:S(2)}) collective-permute-start(bf16[128,1024]{1,0:T(8,128)(2,1)S(1)} %collective-permute-done.6.near_ref.near1_ref), channel_id=1, source_target_pairs={{0,4},{2,30},{4,8},{6,2},{8,12},{10,6},{12,16},{14,10},{16,20},{18... | collective-permute-start | bytes 786440 | tf_op jit(solution)/shard_map/ppermute | solution.py:352
  42.7 1.1 %shard_map.75.local_ref.local1_ref = f32[128,1024]{1,0:T(8,128)S(1)} custom-call(bf16[25,1024,128]{2,1,0:T(8,128)(2,1)S(1)} %shard_map.70.band_ref, bf16[128,1024]{1,0:T(8,128)(2,1)S(1)} %get-tuple-element.51.v_ref), custom_call_target="tpu_custom_call" | custom-call | tf_op jit(solution)/shard_map/pallas_call | solution.py:22
  43.8 5.9 %collective-permute-done.7.far_ref = bf16[128,1024]{1,0:T(8,128)(2,1)S(1)} collective-permute-done((bf16[128,1024]{1,0:T(8,128)(2,1)S(1)}, bf16[128,1024]{1,0:T(8,128)(2,1)S(1)}, u32[]{:S(2)}, u32[]{:S(2)}) %collective-permute-start.7) | collective-permute-done | bytes 262176 | tf_op jit(solution)/shard_map/ppermute | solution.py:352
  49.7 1.1 %shard_map.76 = (f32[128,1024]{1,0:T(8,128)S(1)}, f32[128,1024]{1,0:T(8,128)S(1)}, f32[128,1024]{1,0:T(8,128)S(1)}) custom-call(bf16[25,1024,128]{2,1,0:T(8,128)(2,1)S(1)} %shard_map.70.band_ref, f32[1,1024]{1,0:T(1,128)S(1)} %bitcast.4, f32[8,128]{1,0:T(8,128)S(1)} %get-tuple-element.48.mean_ref, f32[128,1024]{1,0:T(8,128)S(1)} %get-tuple-element.50.k_ref.k1_ref, ...), custom_call_target="tpu_custom_call" | custom-call | tf_op jit(solution)/shard_map/pallas_call | solution.py:22
  50.8 0.0 collective-permute-done.12.q_ref
  50.8 0.3 shard_map.79
  51.1 0.5 shard_map.82
  51.7 0.4 collective-permute-start.13
  52.1 0.9 %collective-permute-start.14 = (bf16[128,1024]{1,0:T(8,128)(2,1)S(1)}, bf16[128,1024]{1,0:T(8,128)(2,1)S(1)}, u32[]{:S(2)}, u32[]{:S(2)}) collective-permute-start(bf16[128,1024]{1,0:T(8,128)(2,1)S(1)} %get-tuple-element.68.v_ref), channel_id=1, source_target_pairs={{0,2},{2,0},{4,6},{6,4},{8,10},{10,8},{12,14},{14,12},{16,18},{18,... | collective-permute-start | bytes 786440 | tf_op jit(solution)/shard_map/ppermute | solution.py:340
  53.0 1.1 %shard_map.80.local2_ref = f32[128,1024]{1,0:T(8,128)S(1)} custom-call(bf16[25,1024,128]{2,1,0:T(8,128)(2,1)S(1)} %shard_map.70.band_ref, bf16[128,1024]{1,0:T(8,128)(2,1)S(1)} %get-tuple-element.68.v_ref), custom_call_target="tpu_custom_call" | custom-call | tf_op jit(solution)/shard_map/pallas_call | solution.py:22
  54.2 0.9 %shard_map.81 = (f32[128,1024]{1,0:T(8,128)S(1)}, f32[1024,128]{1,0:T(8,128)S(1)}, f32[1024,128]{1,0:T(8,128)S(1)}, f32[8,128]{1,0:T(8,128)S(1)}) custom-call(f32[1,128]{1,0:T(1,128)S(1)} %broadcast_multiply_fusion.shift_ref, f32[8,128]{1,0:T(8,128)S(1)} %get-tuple-element.48.mean_ref, f32[1,1024]{1,0:T(1,128)S(1)} %bitcast.5, ...), custom_call_target="tpu_custom_call" | custom-call | tf_op jit(solution)/shard_map/pallas_call | solution.py:22
  55.1 0.0 copy-start.2
  55.1 3.1 %collective-permute-done.13.r2_ref = bf16[128,1024]{1,0:T(8,128)(2,1)S(1)} collective-permute-done((bf16[128,1024]{1,0:T(8,128)(2,1)S(1)}, bf16[128,1024]{1,0:T(8,128)(2,1)S(1)}, u32[]{:S(2)}, u32[]{:S(2)}) %collective-permute-start.13) | collective-permute-done | bytes 262176 | tf_op jit(solution)/shard_map/ppermute | solution.py:359
  58.2 0.4 collective-permute-done.14.near2_ref.near_ref
  58.5 0.7 shard_map.83
  59.2 1.1 %collective-permute-start.17 = (f32[8,128]{1,0:T(8,128)S(1)}, f32[8,128]{1,0:T(8,128)S(1)}, u32[]{:S(2)}, u32[]{:S(2)}) collective-permute-start(f32[8,128]{1,0:T(8,128)S(1)} %get-tuple-element.69), channel_id=1, source_target_pairs={{0,6},{2,4},{4,2},{6,0},{8,14},{10,12},{12,10},{14,8},{16,22},{18,... | collective-permute-start | bytes 12296 | tf_op jit(solution)/shard_map/ppermute | solution.py:391
  60.3 3.0 %collective-permute-start.16 = (f32[8,128]{1,0:T(8,128)S(1)}, f32[8,128]{1,0:T(8,128)S(1)}, u32[]{:S(2)}, u32[]{:S(2)}) collective-permute-start(f32[8,128]{1,0:T(8,128)S(1)} %get-tuple-element.69), channel_id=1, source_target_pairs={{0,4},{2,6},{4,0},{6,2},{8,12},{10,14},{12,8},{14,10},{16,20},{18,... | collective-permute-start | bytes 12296 | tf_op jit(solution)/shard_map/ppermute | solution.py:391
  63.3 0.0 collective-permute-start.15
  63.3 2.0 %collective-permute-start.22 = (bf16[128,1024]{1,0:T(8,128)(2,1)S(1)}, bf16[128,1024]{1,0:T(8,128)(2,1)S(1)}, u32[]{:S(2)}, u32[]{:S(2)}) collective-permute-start(bf16[128,1024]{1,0:T(8,128)(2,1)S(1)} %get-tuple-element.73), channel_id=1, source_target_pairs={{0,2},{2,0},{4,6},{6,4},{8,10},{10,8},{12,14},{14,12},{16,18},{18,... | collective-permute-start | bytes 786440 | tf_op jit(solution)/shard_map/ppermute | solution.py:340
  65.3 0.0 collective-permute-done.17
  65.3 0.0 collective-permute-done.16
  65.4 1.6 %collective-permute-done.15 = f32[8,128]{1,0:T(8,128)S(1)} collective-permute-done((f32[8,128]{1,0:T(8,128)S(1)}, f32[8,128]{1,0:T(8,128)S(1)}, u32[]{:S(2)}, u32[]{:S(2)}) %collective-permute-start.15) | collective-permute-done | bytes 4128 | tf_op jit(solution)/shard_map/ppermute | solution.py:391
  66.9 2.7 %collective-permute-start.20 = (f32[8,128]{1,0:T(8,128)S(1)}, f32[8,128]{1,0:T(8,128)S(1)}, u32[]{:S(2)}, u32[]{:S(2)}) collective-permute-start(f32[8,128]{1,0:T(8,128)S(1)} %add_add_fusion.1), channel_id=1, source_target_pairs={{0,24},{2,26},{4,28},{6,30},{8,16},{10,18},{12,20},{14,22},{16,8},... | collective-permute-start | bytes 12296 | tf_op jit(solution)/shard_map/ppermute | solution.py:391
  69.6 0.0 collective-permute-start.19
  69.6 1.7 %collective-permute-start.18 = (f32[8,128]{1,0:T(8,128)S(1)}, f32[8,128]{1,0:T(8,128)S(1)}, u32[]{:S(2)}, u32[]{:S(2)}) collective-permute-start(f32[8,128]{1,0:T(8,128)S(1)} %add_add_fusion.1), channel_id=1, source_target_pairs={{0,8},{2,10},{4,12},{6,14},{8,0},{10,2},{12,4},{14,6},{16,24},{18,... | collective-permute-start | bytes 12296 | tf_op jit(solution)/shard_map/ppermute | solution.py:391
  71.3 1.0 %collective-permute-done.20 = f32[8,128]{1,0:T(8,128)S(1)} collective-permute-done((f32[8,128]{1,0:T(8,128)S(1)}, f32[8,128]{1,0:T(8,128)S(1)}, u32[]{:S(2)}, u32[]{:S(2)}) %collective-permute-start.20) | collective-permute-done | bytes 4128 | tf_op jit(solution)/shard_map/ppermute | solution.py:391
  72.3 1.8 %collective-permute-done.19 = f32[8,128]{1,0:T(8,128)S(1)} collective-permute-done((f32[8,128]{1,0:T(8,128)S(1)}, f32[8,128]{1,0:T(8,128)S(1)}, u32[]{:S(2)}, u32[]{:S(2)}) %collective-permute-start.19) | collective-permute-done | bytes 4128 | tf_op jit(solution)/shard_map/ppermute | solution.py:391
  74.1 0.0 collective-permute-done.18
  74.1 0.3 collective-permute-done.21.far_ref
  74.5 1.0 %shard_map.84.sum_ref = f32[128,1024]{1,0:T(8,128)S(1)} custom-call(bf16[25,1024,128]{2,1,0:T(8,128)(2,1)S(1)} %shard_map.70.band_ref, f32[128,1024]{1,0:T(8,128)S(1)} %get-tuple-element.72.known_ref, bf16[128,1024]{1,0:T(8,128)(2,1)S(1)} %collective-permute-done.14.near2_ref.near_ref, bf16[128,1024]{1,0:T(8,128)(2,1)S(1)} %collective-permute-done.21.far_ref), custom_call_target="tpu_custom_call" | custom-call | tf_op jit(solution)/shard_map/pallas_call | solution.py:22
  75.4 0.0 collective-permute-done.22.q_ref
  75.5 0.2 shard_map.85.k3_ref
  75.7 1.3 %shard_map.86 = (f32[1024,128]{1,0:T(8,128)}, f32[1024,128]{1,0:T(8,128)}) custom-call(f32[1,128]{1,0:T(1,128)S(1)} %broadcast_multiply_fusion.shift_ref, f32[8,128]{1,0:T(8,128)S(1)} %add_add_fusion.moment_ref, f32[1024,128]{1,0:T(8,128)S(1)} %copy-done.2, f32[1024,128]{1,0:T(8,128)S(1)} %get-tuple-element.70.k1_ref, ...), custom_call_target="tpu_custom_call" | custom-call | tf_op jit(solution)/shard_map/pallas_call | solution.py:22
  (18 shorter events, 0.0 us)
Async XLA Ops:
  0.6 4.5 %copy-start = (bf16[8,16,64,128]{3,2,1,0:T(8,128)(2,1)S(1)}, bf16[8,16,64,128]{3,2,1,0:T(8,128)(2,1)}, u32[]{:S(2)}) copy-start(bf16[8,16,64,128]{3,2,1,0:T(8,128)(2,1)} %part_ref.1) | copy-start | bytes 6291460
  0.6 6.6 %collective-permute-start = (bf16[8,16,64,128]{3,2,1,0:T(8,128)(2,1)}, bf16[8,16,64,128]{3,2,1,0:T(8,128)(2,1)S(1)}, u32[]{:S(2)}, u32[]{:S(2)}) collective-permute-start(bf16[8,16,64,128]{3,2,1,0:T(8,128)(2,1)} %part_ref.1), channel_id=1, source_target_pairs={{0,1},{1,0},{2,3},{3,2},{4,5},{5,4},{6,7},{7,6},{8,9},{9,8},{10,11... | collective-permute-start | bytes 6291464 | tf_op jit(solution)/shard_map/ppermute | solution.py:415
  1.2 1.1 %copy-start.1 = (f32[1024,128]{1,0:T(8,128)S(1)}, f32[1024,128]{1,0:T(8,128)}, u32[]{:S(2)}) copy-start(f32[1024,128]{1,0:T(8,128)} %targets_ref.3) | copy-start | bytes 1572868
  2.3 2.8 %copy-start.3 = (f32[1024]{0:T(1024)S(1)}, f32[1024]{0:T(1024)}, u32[]{:S(2)}) copy-start(f32[1024]{0:T(1024)} %param.6) | copy-start | bytes 12292
  2.3 2.8 %copy-start.4 = (s32[8,16]{1,0:T(8,128)S(1)}, s32[8,16]{1,0:T(8,128)}, u32[]{:S(2)}) copy-start(s32[8,16]{1,0:T(8,128)} %col_ref.3) | copy-start | bytes 1540
  2.3 2.8 %copy-start.5 = (s32[8]{0:T(128)S(1)}, s32[8]{0:T(128)}, u32[]{:S(2)}) copy-start(s32[8]{0:T(128)} %length_ref.3) | copy-start | bytes 100
  2.5 13.7 %collective-permute-start.4 = (bf16[128,1024]{1,0:T(8,128)(2,1)S(1)}, bf16[128,1024]{1,0:T(8,128)(2,1)S(1)}, u32[]{:S(2)}, u32[]{:S(2)}) collective-permute-start(bf16[128,1024]{1,0:T(8,128)(2,1)S(1)} %get-tuple-element.43.v_ref), channel_id=1, source_target_pairs={{0,2},{2,0},{4,6},{6,4},{8,10},{10,8},{12,14},{14,12},{16,18},{18,... | collective-permute-start | bytes 786440 | tf_op jit(solution)/shard_map/ppermute | solution.py:340
  9.1 14.8 %collective-permute-start.2 = (bf16[144,1024]{1,0:T(8,128)(2,1)S(1)}, bf16[144,1024]{1,0:T(8,128)(2,1)S(1)}, u32[]{:S(2)}, u32[]{:S(2)}) collective-permute-start(bf16[144,1024]{1,0:T(8,128)(2,1)S(1)} %get-tuple-element.42.own_ref), channel_id=1, source_target_pairs={{0,2},{2,0},{4,6},{6,4},{8,10},{10,8},{12,14},{14,12},{16,18},{18,... | collective-permute-start | bytes 884744 | tf_op jit(solution)/shard_map/ppermute | solution.py:340
  9.9 14.0 %collective-permute-start.3 = (bf16[144,1024]{1,0:T(8,128)(2,1)S(1)}, bf16[144,1024]{1,0:T(8,128)(2,1)S(1)}, u32[]{:S(2)}, u32[]{:S(2)}) collective-permute-start(bf16[144,1024]{1,0:T(8,128)(2,1)S(1)} %get-tuple-element.46), channel_id=1, source_target_pairs={{0,30},{2,4},{4,2},{6,8},{8,6},{10,12},{12,10},{14,16},{16,14},{18... | collective-permute-start | bytes 884744 | tf_op jit(solution)/shard_map/ppermute | solution.py:345
  16.3 11.9 %collective-permute-start.5 = (bf16[128,1024]{1,0:T(8,128)(2,1)S(1)}, bf16[128,1024]{1,0:T(8,128)(2,1)S(1)}, u32[]{:S(2)}, u32[]{:S(2)}) collective-permute-start(bf16[128,1024]{1,0:T(8,128)(2,1)S(1)} %collective-permute-done.4.near_ref.near0_ref), channel_id=1, source_target_pairs={{0,4},{2,30},{4,8},{6,2},{8,12},{10,6},{12,16},{14,10},{16,20},{18... | collective-permute-start | bytes 786440 | tf_op jit(solution)/shard_map/ppermute | solution.py:352
  16.3 6.2 %collective-permute-start.1 = (f32[1,128]{1,0:T(1,128)S(1)}, f32[1,128]{1,0:T(1,128)S(1)}, u32[]{:S(2)}, u32[]{:S(2)}) collective-permute-start(f32[1,128]{1,0:T(1,128)S(1)} %get-tuple-element.44), channel_id=1, source_target_pairs={{0,8},{2,10},{4,12},{6,14},{8,0},{10,2},{12,4},{14,6},{16,24},{18,... | collective-permute-start | bytes 1544 | tf_op jit(solution)/shard_map/ppermute | solution.py:373
  29.8 9.5 %collective-permute-start.8 = (bf16[144,1024]{1,0:T(8,128)(2,1)S(1)}, bf16[144,1024]{1,0:T(8,128)(2,1)S(1)}, u32[]{:S(2)}, u32[]{:S(2)}) collective-permute-start(bf16[144,1024]{1,0:T(8,128)(2,1)S(1)} %get-tuple-element.56), channel_id=1, source_target_pairs={{0,28},{2,6},{4,0},{6,10},{8,4},{10,14},{12,8},{14,18},{16,12},{18... | collective-permute-start | bytes 884744 | tf_op jit(solution)/shard_map/ppermute | solution.py:359
  32.5 8.1 %collective-permute-start.6 = (bf16[128,1024]{1,0:T(8,128)(2,1)S(1)}, bf16[128,1024]{1,0:T(8,128)(2,1)S(1)}, u32[]{:S(2)}, u32[]{:S(2)}) collective-permute-start(bf16[128,1024]{1,0:T(8,128)(2,1)S(1)} %get-tuple-element.51.v_ref), channel_id=1, source_target_pairs={{0,2},{2,0},{4,6},{6,4},{8,10},{10,8},{12,14},{14,12},{16,18},{18,... | collective-permute-start | bytes 786440 | tf_op jit(solution)/shard_map/ppermute | solution.py:340
  32.5 5.3 %collective-permute-start.11 = (f32[1,128]{1,0:T(1,128)S(1)}, f32[1,128]{1,0:T(1,128)S(1)}, u32[]{:S(2)}, u32[]{:S(2)}) collective-permute-start(f32[1,128]{1,0:T(1,128)S(1)} %add.30), channel_id=1, source_target_pairs={{0,20},{2,22},{4,16},{6,18},{8,28},{10,30},{12,24},{14,26},{16,4},... | collective-permute-start | bytes 1544 | tf_op jit(solution)/shard_map/ppermute | solution.py:380
  34.8 4.4 %collective-permute-start.10 = (f32[1,128]{1,0:T(1,128)S(1)}, f32[1,128]{1,0:T(1,128)S(1)}, u32[]{:S(2)}, u32[]{:S(2)}) collective-permute-start(f32[1,128]{1,0:T(1,128)S(1)} %add.30), channel_id=1, source_target_pairs={{0,16},{2,18},{4,20},{6,22},{8,24},{10,26},{12,28},{14,30},{16,0},... | collective-permute-start | bytes 1544 | tf_op jit(solution)/shard_map/ppermute | solution.py:380
  35.2 4.1 %collective-permute-start.9 = (f32[1,128]{1,0:T(1,128)S(1)}, f32[1,128]{1,0:T(1,128)S(1)}, u32[]{:S(2)}, u32[]{:S(2)}) collective-permute-start(f32[1,128]{1,0:T(1,128)S(1)} %add.30), channel_id=1, source_target_pairs={{0,4},{2,6},{4,0},{6,2},{8,12},{10,14},{12,8},{14,10},{16,20},{18,... | collective-permute-start | bytes 1544 | tf_op jit(solution)/shard_map/ppermute | solution.py:380
  39.4 11.4 %collective-permute-start.12 = (bf16[144,1024]{1,0:T(8,128)(2,1)S(1)}, bf16[144,1024]{1,0:T(8,128)(2,1)S(1)}, u32[]{:S(2)}, u32[]{:S(2)}) collective-permute-start(bf16[144,1024]{1,0:T(8,128)(2,1)S(1)} %shard_map.78.own_ref), channel_id=1, source_target_pairs={{0,2},{2,0},{4,6},{6,4},{8,10},{10,8},{12,14},{14,12},{16,18},{18,... | collective-permute-start | bytes 884744 | tf_op jit(solution)/shard_map/ppermute | solution.py:340
  40.6 9.1 %collective-permute-start.7 = (bf16[128,1024]{1,0:T(8,128)(2,1)S(1)}, bf16[128,1024]{1,0:T(8,128)(2,1)S(1)}, u32[]{:S(2)}, u32[]{:S(2)}) collective-permute-start(bf16[128,1024]{1,0:T(8,128)(2,1)S(1)} %collective-permute-done.6.near_ref.near1_ref), channel_id=1, source_target_pairs={{0,4},{2,30},{4,8},{6,2},{8,12},{10,6},{12,16},{14,10},{16,20},{18... | collective-permute-start | bytes 786440 | tf_op jit(solution)/shard_map/ppermute | solution.py:352
  51.7 6.5 %collective-permute-start.13 = (bf16[128,1024]{1,0:T(8,128)(2,1)S(1)}, bf16[128,1024]{1,0:T(8,128)(2,1)S(1)}, u32[]{:S(2)}, u32[]{:S(2)}) collective-permute-start(bf16[128,1024]{1,0:T(8,128)(2,1)S(1)} %get-tuple-element.67), channel_id=1, source_target_pairs={{0,28},{2,6},{4,0},{6,10},{8,4},{10,14},{12,8},{14,18},{16,12},{18... | collective-permute-start | bytes 786440 | tf_op jit(solution)/shard_map/ppermute | solution.py:359
  52.1 6.4 %collective-permute-start.14 = (bf16[128,1024]{1,0:T(8,128)(2,1)S(1)}, bf16[128,1024]{1,0:T(8,128)(2,1)S(1)}, u32[]{:S(2)}, u32[]{:S(2)}) collective-permute-start(bf16[128,1024]{1,0:T(8,128)(2,1)S(1)} %get-tuple-element.68.v_ref), channel_id=1, source_target_pairs={{0,2},{2,0},{4,6},{6,4},{8,10},{10,8},{12,14},{14,12},{16,18},{18,... | collective-permute-start | bytes 786440 | tf_op jit(solution)/shard_map/ppermute | solution.py:340
  55.1 20.6 %copy-start.2 = (f32[1024,128]{1,0:T(8,128)S(1)}, f32[1024,128]{1,0:T(8,128)}, u32[]{:S(2)}) copy-start(f32[1024,128]{1,0:T(8,128)} %targets_ref.3) | copy-start | bytes 1572868
  59.2 6.1 %collective-permute-start.17 = (f32[8,128]{1,0:T(8,128)S(1)}, f32[8,128]{1,0:T(8,128)S(1)}, u32[]{:S(2)}, u32[]{:S(2)}) collective-permute-start(f32[8,128]{1,0:T(8,128)S(1)} %get-tuple-element.69), channel_id=1, source_target_pairs={{0,6},{2,4},{4,2},{6,0},{8,14},{10,12},{12,10},{14,8},{16,22},{18,... | collective-permute-start | bytes 12296 | tf_op jit(solution)/shard_map/ppermute | solution.py:391
  60.3 5.0 %collective-permute-start.16 = (f32[8,128]{1,0:T(8,128)S(1)}, f32[8,128]{1,0:T(8,128)S(1)}, u32[]{:S(2)}, u32[]{:S(2)}) collective-permute-start(f32[8,128]{1,0:T(8,128)S(1)} %get-tuple-element.69), channel_id=1, source_target_pairs={{0,4},{2,6},{4,0},{6,2},{8,12},{10,14},{12,8},{14,10},{16,20},{18,... | collective-permute-start | bytes 12296 | tf_op jit(solution)/shard_map/ppermute | solution.py:391
  63.3 3.6 %collective-permute-start.15 = (f32[8,128]{1,0:T(8,128)S(1)}, f32[8,128]{1,0:T(8,128)S(1)}, u32[]{:S(2)}, u32[]{:S(2)}) collective-permute-start(f32[8,128]{1,0:T(8,128)S(1)} %get-tuple-element.69), channel_id=1, source_target_pairs={{0,2},{2,0},{4,6},{6,4},{8,10},{10,8},{12,14},{14,12},{16,18},{18,... | collective-permute-start | bytes 12296 | tf_op jit(solution)/shard_map/ppermute | solution.py:391
  63.3 12.1 %collective-permute-start.22 = (bf16[128,1024]{1,0:T(8,128)(2,1)S(1)}, bf16[128,1024]{1,0:T(8,128)(2,1)S(1)}, u32[]{:S(2)}, u32[]{:S(2)}) collective-permute-start(bf16[128,1024]{1,0:T(8,128)(2,1)S(1)} %get-tuple-element.73), channel_id=1, source_target_pairs={{0,2},{2,0},{4,6},{6,4},{8,10},{10,8},{12,14},{14,12},{16,18},{18,... | collective-permute-start | bytes 786440 | tf_op jit(solution)/shard_map/ppermute | solution.py:340
  65.3 9.1 %collective-permute-start.21 = (bf16[128,1024]{1,0:T(8,128)(2,1)S(1)}, bf16[128,1024]{1,0:T(8,128)(2,1)S(1)}, u32[]{:S(2)}, u32[]{:S(2)}) collective-permute-start(bf16[128,1024]{1,0:T(8,128)(2,1)S(1)} %collective-permute-done.14.near2_ref.near_ref), channel_id=1, source_target_pairs={{0,4},{2,30},{4,8},{6,2},{8,12},{10,6},{12,16},{14,10},{16,20},{18... | collective-permute-start | bytes 786440 | tf_op jit(solution)/shard_map/ppermute | solution.py:352
  66.9 5.4 %collective-permute-start.20 = (f32[8,128]{1,0:T(8,128)S(1)}, f32[8,128]{1,0:T(8,128)S(1)}, u32[]{:S(2)}, u32[]{:S(2)}) collective-permute-start(f32[8,128]{1,0:T(8,128)S(1)} %add_add_fusion.1), channel_id=1, source_target_pairs={{0,24},{2,26},{4,28},{6,30},{8,16},{10,18},{12,20},{14,22},{16,8},... | collective-permute-start | bytes 12296 | tf_op jit(solution)/shard_map/ppermute | solution.py:391
  69.6 4.5 %collective-permute-start.19 = (f32[8,128]{1,0:T(8,128)S(1)}, f32[8,128]{1,0:T(8,128)S(1)}, u32[]{:S(2)}, u32[]{:S(2)}) collective-permute-start(f32[8,128]{1,0:T(8,128)S(1)} %add_add_fusion.1), channel_id=1, source_target_pairs={{0,16},{2,18},{4,20},{6,22},{8,24},{10,26},{12,28},{14,30},{16,0},... | collective-permute-start | bytes 12296 | tf_op jit(solution)/shard_map/ppermute | solution.py:391
  69.6 4.5 %collective-permute-start.18 = (f32[8,128]{1,0:T(8,128)S(1)}, f32[8,128]{1,0:T(8,128)S(1)}, u32[]{:S(2)}, u32[]{:S(2)}) collective-permute-start(f32[8,128]{1,0:T(8,128)S(1)} %add_add_fusion.1), channel_id=1, source_target_pairs={{0,8},{2,10},{4,12},{6,14},{8,0},{10,2},{12,4},{14,6},{16,24},{18,... | collective-permute-start | bytes 12296 | tf_op jit(solution)/shard_map/ppermute | solution.py:391

commit v5 on v4

--- a/solution.py
+++ b/solution.py
@@ -15,7 +15,7 @@
 NT = (((1,), (1,)), ((), ()))
 
 
-def call(kernel, out_shape, args, smem=0, outside=(), scratch=(), aliases=None, flops=0):
+def call(kernel, out_shape, args, smem=0, outside=(), scratch=(), aliases=None, flops=0, results=VMEM):
     specs = [SMEM] * smem + [VMEM] * (len(args) - smem)
     for at in outside:
         specs[at] = HBM
@@ -23,7 +23,7 @@
         kernel,
         out_shape=out_shape,
         in_specs=specs,
-        out_specs=jax.tree.map(lambda _: VMEM, out_shape),
+        out_specs=jax.tree.map(lambda _: results, out_shape),
         scratch_shapes=scratch,
         input_output_aliases=aliases or {},
         cost_estimate=pl.CostEstimate(flops=flops, bytes_accessed=2**20, transcendentals=0) if flops else None,
@@ -221,11 +221,13 @@
 def settle_kernel(
     shift_ref, mean_ref, ridge_ref, k0_ref, k1_ref, k2_ref, local0_ref, local1_ref, local2_ref,
     before0_ref, before1_ref, after0_ref, after1_ref, qn0_ref, qf0_ref,
-    sum_ref, rows1_ref, rows2_ref, moment_ref
+    m0_ref, to2_ref, to1_ref, r1_ref, near1_ref, near0_ref,
+    sum_ref, rows1_ref, rows2_ref, moment_ref, both_ref, field_ref
 ):
     cols, width = k0_ref.shape[0], moment_ref.shape[1]
     c = shift_ref[0:1, 0:1]
     own, mean_near, mean_far, mean_before, mean_after = (mean_ref[i : i + 1, 0:1] - c for i in range(5))
+    other = r1_ref[cols : cols + 8, :width].astype(F32)[:1, :1] - c
     totals = [jnp.zeros((cols, width), F32)] * 5
     for at in range(0, k0_ref.shape[1], width):
         out = slice(at, at + width)
@@ -241,34 +243,29 @@
         back = mean_near * mean_near * qn0_ref[:cols, out].astype(F32)
         back = back + mean_far * mean_far * qf0_ref[:cols, out].astype(F32)
         sum_ref[:, out] = mine + 0.5 * (known + back)
+        both = to2_ref[:, out].astype(F32) + 2 * own * to1_ref[:, out].astype(F32)
+        both_ref[:, out] = both + 2 * other * r1_ref[:cols, out].astype(F32)
+        field = 2 * mean_near * near1_ref[:, out].astype(F32)
+        field_ref[:, out] = field + mean_near * mean_near * near0_ref[:, out].astype(F32)
         parts = (k0 * s1, s1 * s1, s1 * s2, s2 * s2, s2 * (mine + back))
         totals = [total + part for total, part in zip(totals, parts, strict=True)]
+    moment_ref[0:1, :] = m0_ref[...]
     for i, total in enumerate(totals):
-        moment_ref[i : i + 1, :] = jnp.sum(total.T, axis=0, keepdims=True)
-
-
-def form_kernel(
-    shift_ref, mean_ref, m0_ref, pairs_ref, to2_ref, to1_ref, r2_ref, r1_ref, near2_ref, near1_ref, near0_ref,
-    q_ref, moment_ref
-):
-    cols, assets = to2_ref.shape
+        moment_ref[i + 1 : i + 2, :] = jnp.sum(total.T, axis=0, keepdims=True)
+    moment_ref[6:8, :] = jnp.zeros((2, width), F32)
+
+
+def form_kernel(share_ref, both_ref, field_ref, received_ref, near_ref, q_ref, moment_ref):
+    cols, assets = both_ref.shape
     width = moment_ref.shape[1]
-    c = shift_ref[0:1, 0:1]
-    own, gap = mean_ref[0:1, 0:1] - c, mean_ref[1:2, 0:1] - c
-    other = r1_ref[cols : cols + 8, :width].astype(F32)[:1, :1] - c
     total = jnp.zeros((cols, width), F32)
     for at in range(0, assets, width):
         out = slice(at, at + width)
-        both = to2_ref[:, out].astype(F32) + 2 * own * to1_ref[:, out].astype(F32)
-        both = both + r2_ref[:, out].astype(F32) + 2 * other * r1_ref[:cols, out].astype(F32)
-        field = near2_ref[:, out].astype(F32) + 2 * gap * near1_ref[:, out].astype(F32)
-        field = field + gap * gap * near0_ref[:, out].astype(F32)
+        both = both_ref[:, out] + received_ref[:, out].astype(F32)
         q_ref[:, out] = both.astype(BF16)
-        total = total + both * field
-    moment_ref[0:1, :] = m0_ref[...]
-    moment_ref[1:5, :] = pairs_ref[0:4, :]
-    moment_ref[5:6, :] = pairs_ref[4:5, :] + jnp.sum(total.T, axis=0, keepdims=True)
-    moment_ref[6:8, :] = jnp.zeros((2, width), F32)
+        total = total + both * (field_ref[:, out] + near_ref[:, out].astype(F32))
+    moment_ref[...] = share_ref[...]
+    moment_ref[5:6, :] = share_ref[5:6, :] + jnp.sum(total.T, axis=0, keepdims=True)
 
 
 def cross_third_kernel(band_ref, known_ref, near_ref, far_ref, sum_ref):
@@ -285,7 +282,7 @@
         rows3_ref[out, :] = (sum_ref[:, out] + 0.5 * q_ref[:, out].astype(F32)).T
 
 
-def share(above, below):
+def ratio(above, below):
     return jnp.where(below == 0, 0.0, above / below)
 
 
@@ -309,7 +306,7 @@
         image = [shift * value for value in used] + [zero]
         for i, value in enumerate(used):
             image[i + 1] = image[i + 1] + value
-        alpha = share(now, inner(used, image))
+        alpha = ratio(now, inner(used, image))
         for i, value in enumerate(used):
             solution[i] = solution[i] + alpha * value
         for i, value in enumerate(image):
@@ -317,22 +314,32 @@
         if step + 1 < iters:
             left = residual[: step + 2]
             new = inner(left, left)
-            beta = share(new, now)
+            beta = ratio(new, now)
             direction = [r + beta * d for r, d in zip(residual[:iters], direction, strict=True)]
             now = new
     return solution, residual
 
 
-def combine_kernel(shift_ref, moment_ref, targets_ref, k1_ref, k2_ref, k3_ref, solution_ref, residual_ref):
+def combine_kernel(
+    shift_ref, moment_ref, targets_ref, k1_ref, k2_ref, k3_ref, solution_hbm, residual_hbm, held, sems
+):
     width = moment_ref.shape[1]
     m = [moment_ref[i : i + 1, :] for i in range(6)]
     x, r = scalars(m, shift_ref[...], 3)
-    for at in range(0, targets_ref.shape[0], width):
-        out = slice(at, at + width)
-        k0 = targets_ref[out, :]
-        k1, k2, k3 = k1_ref[out, :], k2_ref[out, :], k3_ref[out, :]
-        solution_ref[out, :] = x[0] * k0 + x[1] * k1 + x[2] * k2
-        residual_ref[out, :] = r[0] * k0 + r[1] * k1 + r[2] * k2 + r[3] * k3
+    assets = targets_ref.shape[0]
+    size = 2 * width
+    copies = []
+    for part in range(assets // size):
+        out = slice(part * size, (part + 1) * size)
+        k0, k1, k2, k3 = targets_ref[out, :], k1_ref[out, :], k2_ref[out, :], k3_ref[out, :]
+        held[0, out, :] = x[0] * k0 + x[1] * k1 + x[2] * k2
+        held[1, out, :] = r[0] * k0 + r[1] * k1 + r[2] * k2 + r[3] * k3
+        for i, target in enumerate((solution_hbm, residual_hbm)):
+            copy = pltpu.make_async_copy(held.at[i, out, :], target.at[out, :], sems.at[i, part])
+            copy.start()
+            copies.append(copy)
+    for copy in copies:
+        copy.wait()
 
 
 def near(value):
@@ -371,14 +378,6 @@
 def sum_step(value, axis, distance):
     count = lax.axis_size(axis)
     return value + lax.ppermute(value, axis, [(i, i ^ distance) for i in range(count)])
-
-
-def sum_four(value, axis, first, second):
-    count = lax.axis_size(axis)
-    total = value
-    for distance in (first, second, first + second):
-        total = total + lax.ppermute(value, axis, [(i, i ^ distance) for i in range(count)])
-    return total
 
 
 def sum_over(value, axis):
@@ -449,7 +448,7 @@
     to_near1, to_far1 = call(products_second_kernel, (rounded, message), (band, v1, means))
     received, near1 = back(to_far1), near(v1)
     far1 = forward(near1)
-    mean = sum_four(together(mean, to_near1)[0], "asset", distances[0], distances[-1])
+    mean = sum_step(together(mean, to_near1)[0], "asset", distances[0])
     joined = call(add_kernel, message, (to_near1, received, mean))
     q1 = near(joined)
     local1 = call(local_kernel, field, (band, v1))
@@ -465,30 +464,38 @@
     )
 
     to_near2, to_far2 = call(products_kernel, (rounded,) * 2, (band, v2))
-    near2 = near(together(v2, to_near2)[0])
+    received2 = back(to_far2)
+    local2 = call(local_kernel, field, (band, together(v2, to_near2)[0]), flops=5 * 10**9)
+    near2 = near(together(v2, local2)[0])
     far2 = forward(near2)
-    received2 = back(to_far2)
-    local2 = call(local_kernel, field, (band, v2))
-    shift = mean / devices
+    shift = sum_step(mean, "asset", distances[-1]) / devices
     out = shape(F32, assets, cols)
-    known, rows1, rows2, pairs = call(
+    known, rows1, rows2, share, both, field2 = call(
         settle_kernel,
-        (field, out, out, shape(F32, 8, cols)),
+        (field, out, out, shape(F32, 8, cols), field, field),
         (
             shift, means, ridge, k0, k1, k2, local0, local1, local2,
             before0, before1, after0, after1, qn0, qf0,
+            m0, to_near2, to_near1, received, near1, near0,
         ),
     )
     joined, moments = call(
-        form_kernel,
-        (rounded, shape(F32, 8, cols)),
-        (shift, means, m0, pairs, to_near2, to_near1, received2, received, near2, near1, near0),
+        form_kernel, (rounded, shape(F32, 8, cols)), (share, both, field2, received2, near2)
     )
     moments = sum_over(moments, "asset")
     q2 = near(joined)
     partial = call(cross_third_kernel, field, (band, known, near2, far2))
     rows3 = call(finish_third_kernel, out, (partial, q2))
-    return call(combine_kernel, (out, out), (shift, moments, targets, rows1, rows2, rows3))
+    return call(
+        combine_kernel,
+        (out, out),
+        (shift, moments, targets, rows1, rows2, rows3),
+        scratch=[
+            pltpu.VMEM((2, assets, cols), F32),
+            pltpu.SemaphoreType.DMA((2, rows // 2)),
+        ],
+        results=HBM,
+    )
 
 
 def solution(mesh):

time: 77.1 us -> 76.8 us (level)
  starting transfers between devices: 31.5 us -> 28.4 us
  waiting for transfers between devices: 28.1 us -> 31.1 us
    ppermute x1 -> x3, waiting for transfers between devices: 6.11 us -> 12.7 us  [sum_step(): lax.ppermute(value, axis, [(i, i ^ distance) for i in range(count)])]
    ppermute x3 -> x0, starting transfers between devices: 4.39 us -> none  [sum_four(): lax.ppermute(value, axis, [(i, i ^ distance) for i in range(count)])]
    ppermute x1 -> x3, starting transfers between devices: 0.07 us -> 3.35 us  [sum_step(): lax.ppermute(value, axis, [(i, i ^ distance) for i in range(count)])]
    ppermute x2, waiting for transfers between devices: 3.06 us -> 0.49 us  [back(): lax.ppermute(value, 'asset', [(i, (i + 2 if i % 2 else i - 2) % count) fo...]
    ppermute x3 -> x0, waiting for transfers between devices: 2.41 us -> none  [sum_four(): lax.ppermute(value, axis, [(i, i ^ distance) for i in range(count)])]
    ppermute x1, waiting for transfers between devices: 0.01 us -> 2.23 us  [far(): lax.ppermute(value, 'asset', [(i, (i + 1 if i % 2 else i - 1) % count) fo...]
    ppermute x6, waiting for transfers between devices: 4.38 us -> 3.12 us  [sum_over(): total = total + lax.ppermute(value, axis, route)]
    ppermute x6, waiting for transfers between devices: 1.7 us -> 2.75 us  [near(): return lax.ppermute(value, 'asset', [(i, i ^ 1) for i in range(count)])]
  transfers between devices with their start and end apart: 23 -> 22, of which waited for: 12 -> 11; matrix products, arithmetic and copies ran while one was open for 0% -> 0% of each run, Pallas kernels for 14% -> 14%
where the time goes in v5:
time: 76.8 us; the launch traced here: 76.6 us
  waiting for transfers between devices  31.1 us (40%)
  starting transfers between devices  28.4 us (37%)
  Pallas kernels  15.1 us (20%)
  local copies, waits for them, and re-layouts  1.17 us (2%)
  between operations  0.87 us (1%)
    pallas_call x19, Pallas kernels, call(): pl.pallas_call(kernel, out_shape=out_shape, in_specs=specs, out_specs=jax...  15.1 us
    ppermute x3, waiting for transfers between devices, sum_step(): lax.ppermute(value, axis, [(i, i ^ distance) for i in range(count)])  12.7 us
    ppermute x3, waiting for transfers between devices, forward(): lax.ppermute(value, 'asset', [(i, (i - 2 if i % 2 else i + 2) % count) fo...  9.81 us
    ppermute x6, starting transfers between devices, sum_over(): total = total + lax.ppermute(value, axis, route)  8 us
    ppermute x6, starting transfers between devices, near(): return lax.ppermute(value, 'asset', [(i, i ^ 1) for i in range(count)])  7.29 us
    ppermute x1, starting transfers between devices, far(): lax.ppermute(value, 'asset', [(i, (i + 1 if i % 2 else i - 1) % count) fo...  4.82 us
    ppermute x3, starting transfers between devices, sum_step(): lax.ppermute(value, axis, [(i, i ^ distance) for i in range(count)])  3.35 us
    ppermute x6, waiting for transfers between devices, sum_over(): total = total + lax.ppermute(value, axis, route)  3.12 us
  transfers between devices with their start and end apart: 22, of which 11 were waited for; matrix products, arithmetic and copies ran while one was open for 0% of the time, Pallas kernels for 14%

profile of v5, /device:TPU:0, one launch (start us, length us, event | category | flops | bytes accessed | tf_op | source)
XLA Modules:
  0.0 76.6 jit_solution(1519859397863212593)
XLA Ops:
  0.6 0.5 collective-permute-start
  1.2 1.1 %copy-done.1 = f32[1024,128]{1,0:T(8,128)S(1)} copy-done((f32[1024,128]{1,0:T(8,128)S(1)}, f32[1024,128]{1,0:T(8,128)}, u32[]{:S(2)}) %copy-start.1) | copy-done | bytes 524312
  2.3 0.2 shard_map.68
  2.5 2.6 %collective-permute-start.4 = (bf16[128,1024]{1,0:T(8,128)(2,1)S(1)}, bf16[128,1024]{1,0:T(8,128)(2,1)S(1)}, u32[]{:S(2)}, u32[]{:S(2)}) collective-permute-start(bf16[128,1024]{1,0:T(8,128)(2,1)S(1)} %get-tuple-element.46.v_ref), channel_id=1, source_target_pairs={{0,2},{2,0},{4,6},{6,4},{8,10},{10,8},{12,14},{14,12},{16,18},{18,... | collective-permute-start | bytes 786440 | tf_op jit(solution)/shard_map/ppermute | solution.py:347
  5.1 2.1 %shard_map.69 = (bf16[25,1024,128]{2,1,0:T(8,128)(2,1)S(1)}, f32[1,128]{1,0:T(1,128)S(1)}) custom-call(s32[8,16]{1,0:T(8,128)S(1)} %copy-done.4, s32[8]{0:T(128)S(1)} %copy-done.5, bf16[8,16,64,128]{3,2,1,0:T(8,128)(2,1)S(1)} %copy-done, f32[1,1024]{1,0:T(1,128)S(1)} %bitcast.1), custom_call_target="tpu_custom_call" | custom-call | tf_op jit(solution)/shard_map/pallas_call | solution.py:22
  7.2 0.0 collective-permute-done.part_ref
  7.2 1.2 %shard_map.70.band_ref = bf16[25,1024,128]{2,1,0:T(8,128)(2,1)S(1)} custom-call(s32[8,16]{1,0:T(8,128)S(1)} %copy-done.4, s32[8]{0:T(128)S(1)} %copy-done.5, bf16[8,16,64,128]{3,2,1,0:T(8,128)(2,1)S(1)} %collective-permute-done.part_ref, bf16[25,1024,128]{2,1,0:T(8,128)(2,1)S(1)} %get-tuple-element.42._), custom_call_target="tpu_custom_call", output_to_operand_aliasing={{}: (3, {})} | custom-call | tf_op jit(solution)/shard_map/pallas_call | solution.py:22
  8.5 0.5 shard_map.71
  9.1 4.8 %collective-permute-start.3 = (bf16[144,1024]{1,0:T(8,128)(2,1)S(1)}, bf16[144,1024]{1,0:T(8,128)(2,1)S(1)}, u32[]{:S(2)}, u32[]{:S(2)}) collective-permute-start(bf16[144,1024]{1,0:T(8,128)(2,1)S(1)} %get-tuple-element.49), channel_id=1, source_target_pairs={{0,30},{2,4},{4,2},{6,8},{8,6},{10,12},{12,10},{14,16},{16,14},{18... | collective-permute-start | bytes 884744 | tf_op jit(solution)/shard_map/ppermute | solution.py:352
  13.9 0.0 collective-permute-start.2
  13.9 1.1 %shard_map.72.local_ref.local0_ref = f32[128,1024]{1,0:T(8,128)S(1)} custom-call(bf16[25,1024,128]{2,1,0:T(8,128)(2,1)S(1)} %shard_map.70.band_ref, bf16[128,1024]{1,0:T(8,128)(2,1)S(1)} %get-tuple-element.46.v_ref), custom_call_target="tpu_custom_call" | custom-call | tf_op jit(solution)/shard_map/pallas_call | solution.py:22
  15.0 0.0 collective-permute-done.4.near_ref.near0_ref
  15.0 0.1 collective-permute-start.5
  15.1 1.3 %collective-permute-start.1 = (f32[1,128]{1,0:T(1,128)S(1)}, f32[1,128]{1,0:T(1,128)S(1)}, u32[]{:S(2)}, u32[]{:S(2)}) collective-permute-start(f32[1,128]{1,0:T(1,128)S(1)} %get-tuple-element.47), channel_id=1, source_target_pairs={{0,8},{2,10},{4,12},{6,14},{8,0},{10,2},{12,4},{14,6},{16,24},{18,... | collective-permute-start | bytes 1544 | tf_op jit(solution)/shard_map/ppermute | solution.py:380
  16.4 4.7 %collective-permute-done.1 = f32[1,128]{1,0:T(1,128)S(1)} collective-permute-done((f32[1,128]{1,0:T(1,128)S(1)}, f32[1,128]{1,0:T(1,128)S(1)}, u32[]{:S(2)}, u32[]{:S(2)}) %collective-permute-start.1) | collective-permute-done | bytes 544 | tf_op jit(solution)/shard_map/ppermute | solution.py:380
  21.1 2.2 %collective-permute-done.3.far_ref.qf0_ref = bf16[144,1024]{1,0:T(8,128)(2,1)S(1)} collective-permute-done((bf16[144,1024]{1,0:T(8,128)(2,1)S(1)}, bf16[144,1024]{1,0:T(8,128)(2,1)S(1)}, u32[]{:S(2)}, u32[]{:S(2)}) %collective-permute-start.3) | collective-permute-done | bytes 294944 | tf_op jit(solution)/shard_map/ppermute | solution.py:352
  23.3 2.1 %collective-permute-done.2.near_ref.qn0_ref = bf16[144,1024]{1,0:T(8,128)(2,1)S(1)} collective-permute-done((bf16[144,1024]{1,0:T(8,128)(2,1)S(1)}, bf16[144,1024]{1,0:T(8,128)(2,1)S(1)}, u32[]{:S(2)}, u32[]{:S(2)}) %collective-permute-start.2) | collective-permute-done | bytes 294944 | tf_op jit(solution)/shard_map/ppermute | solution.py:347
  25.4 0.1 shard_map.73
  25.5 1.9 %collective-permute-done.5.far_ref = bf16[128,1024]{1,0:T(8,128)(2,1)S(1)} collective-permute-done((bf16[128,1024]{1,0:T(8,128)(2,1)S(1)}, bf16[128,1024]{1,0:T(8,128)(2,1)S(1)}, u32[]{:S(2)}, u32[]{:S(2)}) %collective-permute-start.5) | collective-permute-done | bytes 262176 | tf_op jit(solution)/shard_map/ppermute | solution.py:359
  27.4 1.0 %shard_map.74 = (f32[128,1024]{1,0:T(8,128)S(1)}, bf16[128,1024]{1,0:T(8,128)(2,1)S(1)}, f32[128,1024]{1,0:T(8,128)S(1)}, f32[128,1024]{1,0:T(8,128)S(1)}) custom-call(bf16[25,1024,128]{2,1,0:T(8,128)(2,1)S(1)} %shard_map.70.band_ref, f32[128,1024]{1,0:T(8,128)S(1)} %get-tuple-element.50.sum_ref, f32[128,1024]{1,0:T(8,128)S(1)} %get-tuple-element.41.k_ref.k0_ref, ...), custom_call_target="tpu_custom_call" | custom-call | tf_op jit(solution)/shard_map/pallas_call | solution.py:22
  28.4 0.6 shard_map.77
  29.0 2.3 %collective-permute-start.8 = (bf16[144,1024]{1,0:T(8,128)(2,1)S(1)}, bf16[144,1024]{1,0:T(8,128)(2,1)S(1)}, u32[]{:S(2)}, u32[]{:S(2)}) collective-permute-start(bf16[144,1024]{1,0:T(8,128)(2,1)S(1)} %get-tuple-element.59), channel_id=1, source_target_pairs={{0,28},{2,6},{4,0},{6,10},{8,4},{10,14},{12,8},{14,18},{16,12},{18... | collective-permute-start | bytes 884744 | tf_op jit(solution)/shard_map/ppermute | solution.py:366
  31.3 0.0 collective-permute-start.6
  31.3 0.7 collective-permute-start.9
  31.9 4.9 %collective-permute-done.9 = f32[1,128]{1,0:T(1,128)S(1)} collective-permute-done((f32[1,128]{1,0:T(1,128)S(1)}, f32[1,128]{1,0:T(1,128)S(1)}, u32[]{:S(2)}, u32[]{:S(2)}) %collective-permute-start.9) | collective-permute-done | bytes 544 | tf_op jit(solution)/shard_map/ppermute | solution.py:380
  36.8 0.5 collective-permute-done.8.received_ref.r1_ref
  37.3 0.1 shard_map.78.own_ref
  37.5 3.3 %collective-permute-start.10 = (bf16[144,1024]{1,0:T(8,128)(2,1)S(1)}, bf16[144,1024]{1,0:T(8,128)(2,1)S(1)}, u32[]{:S(2)}, u32[]{:S(2)}) collective-permute-start(bf16[144,1024]{1,0:T(8,128)(2,1)S(1)} %shard_map.78.own_ref), channel_id=1, source_target_pairs={{0,2},{2,0},{4,6},{6,4},{8,10},{10,8},{12,14},{14,12},{16,18},{18,... | collective-permute-start | bytes 884744 | tf_op jit(solution)/shard_map/ppermute | solution.py:347
  40.7 0.0 collective-permute-done.6.near_ref.near1_ref
  40.7 0.0 collective-permute-start.7
  40.7 1.1 %shard_map.75.local_ref.local1_ref = f32[128,1024]{1,0:T(8,128)S(1)} custom-call(bf16[25,1024,128]{2,1,0:T(8,128)(2,1)S(1)} %shard_map.70.band_ref, bf16[128,1024]{1,0:T(8,128)(2,1)S(1)} %get-tuple-element.54.v_ref), custom_call_target="tpu_custom_call" | custom-call | tf_op jit(solution)/shard_map/pallas_call | solution.py:22
  41.9 7.9 %collective-permute-done.7.far_ref = bf16[128,1024]{1,0:T(8,128)(2,1)S(1)} collective-permute-done((bf16[128,1024]{1,0:T(8,128)(2,1)S(1)}, bf16[128,1024]{1,0:T(8,128)(2,1)S(1)}, u32[]{:S(2)}, u32[]{:S(2)}) %collective-permute-start.7) | collective-permute-done | bytes 262176 | tf_op jit(solution)/shard_map/ppermute | solution.py:359
  49.8 1.1 %shard_map.76 = (f32[128,1024]{1,0:T(8,128)S(1)}, f32[128,1024]{1,0:T(8,128)S(1)}, f32[128,1024]{1,0:T(8,128)S(1)}) custom-call(bf16[25,1024,128]{2,1,0:T(8,128)(2,1)S(1)} %shard_map.70.band_ref, f32[1,1024]{1,0:T(1,128)S(1)} %bitcast.4, f32[8,128]{1,0:T(8,128)S(1)} %get-tuple-element.51.mean_ref, f32[128,1024]{1,0:T(8,128)S(1)} %get-tuple-element.53.k_ref.k1_ref, ...), custom_call_target="tpu_custom_call" | custom-call | tf_op jit(solution)/shard_map/pallas_call | solution.py:22
  50.9 0.0 collective-permute-done.10.q_ref
  51.0 0.3 shard_map.79
  51.3 0.6 shard_map.80
  51.8 0.1 collective-permute-start.12
  51.9 1.1 %shard_map.81.local2_ref = f32[128,1024]{1,0:T(8,128)S(1)} custom-call(bf16[25,1024,128]{2,1,0:T(8,128)(2,1)S(1)} %shard_map.70.band_ref, bf16[128,1024]{1,0:T(8,128)(2,1)S(1)} %get-tuple-element.74.v_ref), custom_call_target="tpu_custom_call" | custom-call | flops 5000000000 | bytes 1048576 | tf_op jit(solution)/shard_map/pallas_call | solution.py:22
  53.0 0.1 collective-permute-start.13
  53.1 1.4 %collective-permute-start.11 = (f32[1,128]{1,0:T(1,128)S(1)}, f32[1,128]{1,0:T(1,128)S(1)}, u32[]{:S(2)}, u32[]{:S(2)}) collective-permute-start(f32[1,128]{1,0:T(1,128)S(1)} %get-tuple-element.62), channel_id=1, source_target_pairs={{0,16},{2,18},{4,20},{6,22},{8,24},{10,26},{12,28},{14,30},{16,0},... | collective-permute-start | bytes 1544 | tf_op jit(solution)/shard_map/ppermute | solution.py:380
  54.5 3.1 %collective-permute-done.11 = f32[1,128]{1,0:T(1,128)S(1)} collective-permute-done((f32[1,128]{1,0:T(1,128)S(1)}, f32[1,128]{1,0:T(1,128)S(1)}, u32[]{:S(2)}, u32[]{:S(2)}) %collective-permute-start.11) | collective-permute-done | bytes 544 | tf_op jit(solution)/shard_map/ppermute | solution.py:380
  57.6 1.2 %shard_map.82 = (f32[128,1024]{1,0:T(8,128)S(1)}, f32[1024,128]{1,0:T(8,128)S(1)}, f32[1024,128]{1,0:T(8,128)S(1)}, f32[8,128]{1,0:T(8,128)S(1)}, f32[128,1024]{1,0:T(8,128)S(1)}, /*index=5*/f32[128,1024]{1,0:T(8,128)S(1)}) custom-call(f32[1,128]{1,0:T(1,128)S(1)} %add_multiply_fusion.shift_ref, f32[8,128]{1,0:T(8,128)S(1)} %get-tuple-element.51.mean_ref, ...), custom_call_target="tpu_custom_call" | custom-call | tf_op jit(solution)/shard_map/pallas_call | solution.py:22
  58.9 0.0 copy-start.2
  58.9 0.0 collective-permute-done.12.received_ref
  58.9 0.6 collective-permute-done.13.near_ref
  59.5 0.2 shard_map.83
  59.7 2.8 %collective-permute-start.16 = (f32[8,128]{1,0:T(8,128)S(1)}, f32[8,128]{1,0:T(8,128)S(1)}, u32[]{:S(2)}, u32[]{:S(2)}) collective-permute-start(f32[8,128]{1,0:T(8,128)S(1)} %get-tuple-element.75), channel_id=1, source_target_pairs={{0,6},{2,4},{4,2},{6,0},{8,14},{10,12},{12,10},{14,8},{16,22},{18,... | collective-permute-start | bytes 12296 | tf_op jit(solution)/shard_map/ppermute | solution.py:390
  62.6 0.0 collective-permute-start.15
  62.6 0.7 collective-permute-start.14
  63.3 1.3 %collective-permute-start.21 = (bf16[128,1024]{1,0:T(8,128)(2,1)S(1)}, bf16[128,1024]{1,0:T(8,128)(2,1)S(1)}, u32[]{:S(2)}, u32[]{:S(2)}) collective-permute-start(bf16[128,1024]{1,0:T(8,128)(2,1)S(1)} %get-tuple-element.79), channel_id=1, source_target_pairs={{0,2},{2,0},{4,6},{6,4},{8,10},{10,8},{12,14},{14,12},{16,18},{18,... | collective-permute-start | bytes 786440 | tf_op jit(solution)/shard_map/ppermute | solution.py:347
  64.6 2.0 %collective-permute-start.20 = (bf16[128,1024]{1,0:T(8,128)(2,1)S(1)}, bf16[128,1024]{1,0:T(8,128)(2,1)S(1)}, u32[]{:S(2)}, u32[]{:S(2)}) collective-permute-start(bf16[128,1024]{1,0:T(8,128)(2,1)S(1)} %collective-permute-done.13.near_ref), channel_id=1, source_target_pairs={{0,4},{2,30},{4,8},{6,2},{8,12},{10,6},{12,16},{14,10},{16,20},{18... | collective-permute-start | bytes 786440 | tf_op jit(solution)/shard_map/ppermute | solution.py:359
  66.6 0.0 collective-permute-done.16
  66.6 0.0 collective-permute-done.15
  66.6 0.0 collective-permute-done.14
  66.7 3.1 %collective-permute-start.19 = (f32[8,128]{1,0:T(8,128)S(1)}, f32[8,128]{1,0:T(8,128)S(1)}, u32[]{:S(2)}, u32[]{:S(2)}) collective-permute-start(f32[8,128]{1,0:T(8,128)S(1)} %add_add_fusion.1), channel_id=1, source_target_pairs={{0,24},{2,26},{4,28},{6,30},{8,16},{10,18},{12,20},{14,22},{16,8},... | collective-permute-start | bytes 12296 | tf_op jit(solution)/shard_map/ppermute | solution.py:390
  69.7 0.0 collective-permute-start.18
  69.7 1.4 %collective-permute-start.17 = (f32[8,128]{1,0:T(8,128)S(1)}, f32[8,128]{1,0:T(8,128)S(1)}, u32[]{:S(2)}, u32[]{:S(2)}) collective-permute-start(f32[8,128]{1,0:T(8,128)S(1)} %add_add_fusion.1), channel_id=1, source_target_pairs={{0,8},{2,10},{4,12},{6,14},{8,0},{10,2},{12,4},{14,6},{16,24},{18,... | collective-permute-start | bytes 12296 | tf_op jit(solution)/shard_map/ppermute | solution.py:390
  71.1 1.0 %collective-permute-done.19 = f32[8,128]{1,0:T(8,128)S(1)} collective-permute-done((f32[8,128]{1,0:T(8,128)S(1)}, f32[8,128]{1,0:T(8,128)S(1)}, u32[]{:S(2)}, u32[]{:S(2)}) %collective-permute-start.19) | collective-permute-done | bytes 4128 | tf_op jit(solution)/shard_map/ppermute | solution.py:390
  72.1 2.1 %collective-permute-done.18 = f32[8,128]{1,0:T(8,128)S(1)} collective-permute-done((f32[8,128]{1,0:T(8,128)S(1)}, f32[8,128]{1,0:T(8,128)S(1)}, u32[]{:S(2)}, u32[]{:S(2)}) %collective-permute-start.18) | collective-permute-done | bytes 4128 | tf_op jit(solution)/shard_map/ppermute | solution.py:390
  74.2 0.0 collective-permute-done.17
  74.2 0.0 collective-permute-done.20.far_ref
  74.2 1.0 %shard_map.84.sum_ref = f32[128,1024]{1,0:T(8,128)S(1)} custom-call(bf16[25,1024,128]{2,1,0:T(8,128)(2,1)S(1)} %shard_map.70.band_ref, f32[128,1024]{1,0:T(8,128)S(1)} %get-tuple-element.78.known_ref, bf16[128,1024]{1,0:T(8,128)(2,1)S(1)} %collective-permute-done.13.near_ref, bf16[128,1024]{1,0:T(8,128)(2,1)S(1)} %collective-permute-done.20.far_ref), custom_call_target="tpu_custom_call" | custom-call | tf_op jit(solution)/shard_map/pallas_call | solution.py:22
  75.3 0.2 shard_map.85.k3_ref
  75.5 1.2 %shard_map.86 = (f32[1024,128]{1,0:T(8,128)}, f32[1024,128]{1,0:T(8,128)}) custom-call(f32[1,128]{1,0:T(1,128)S(1)} %add_multiply_fusion.shift_ref, f32[8,128]{1,0:T(8,128)S(1)} %add_add_fusion.moment_ref, f32[1024,128]{1,0:T(8,128)S(1)} %copy-done.2, f32[1024,128]{1,0:T(8,128)S(1)} %get-tuple-element.76.k1_ref, f32[1024,128]{1,0:T(8,128)S(1)} %get-tuple-element.77.k2_ref, ...), custom_call_target="tpu_custom_call" | custom-call | tf_op jit(solution)/shard_map/pallas_call | solution.py:22
  (16 shorter events, 0.0 us)
Async XLA Ops:
  0.6 4.5 %copy-start = (bf16[8,16,64,128]{3,2,1,0:T(8,128)(2,1)S(1)}, bf16[8,16,64,128]{3,2,1,0:T(8,128)(2,1)}, u32[]{:S(2)}) copy-start(bf16[8,16,64,128]{3,2,1,0:T(8,128)(2,1)} %part_ref.1) | copy-start | bytes 6291460
  0.6 6.6 %collective-permute-start = (bf16[8,16,64,128]{3,2,1,0:T(8,128)(2,1)}, bf16[8,16,64,128]{3,2,1,0:T(8,128)(2,1)S(1)}, u32[]{:S(2)}, u32[]{:S(2)}) collective-permute-start(bf16[8,16,64,128]{3,2,1,0:T(8,128)(2,1)} %part_ref.1), channel_id=1, source_target_pairs={{0,1},{1,0},{2,3},{3,2},{4,5},{5,4},{6,7},{7,6},{8,9},{9,8},{10,11... | collective-permute-start | bytes 6291464 | tf_op jit(solution)/shard_map/ppermute | solution.py:414
  1.2 1.1 %copy-start.1 = (f32[1024,128]{1,0:T(8,128)S(1)}, f32[1024,128]{1,0:T(8,128)}, u32[]{:S(2)}) copy-start(f32[1024,128]{1,0:T(8,128)} %targets_ref.3) | copy-start | bytes 1572868
  2.3 2.8 %copy-start.3 = (f32[1024]{0:T(1024)S(1)}, f32[1024]{0:T(1024)}, u32[]{:S(2)}) copy-start(f32[1024]{0:T(1024)} %param.6) | copy-start | bytes 12292
  2.3 2.8 %copy-start.4 = (s32[8,16]{1,0:T(8,128)S(1)}, s32[8,16]{1,0:T(8,128)}, u32[]{:S(2)}) copy-start(s32[8,16]{1,0:T(8,128)} %col_ref.3) | copy-start | bytes 1540
  2.3 2.8 %copy-start.5 = (s32[8]{0:T(128)S(1)}, s32[8]{0:T(128)}, u32[]{:S(2)}) copy-start(s32[8]{0:T(128)} %length_ref.3) | copy-start | bytes 100
  2.5 12.5 %collective-permute-start.4 = (bf16[128,1024]{1,0:T(8,128)(2,1)S(1)}, bf16[128,1024]{1,0:T(8,128)(2,1)S(1)}, u32[]{:S(2)}, u32[]{:S(2)}) collective-permute-start(bf16[128,1024]{1,0:T(8,128)(2,1)S(1)} %get-tuple-element.46.v_ref), channel_id=1, source_target_pairs={{0,2},{2,0},{4,6},{6,4},{8,10},{10,8},{12,14},{14,12},{16,18},{18,... | collective-permute-start | bytes 786440 | tf_op jit(solution)/shard_map/ppermute | solution.py:347
  9.1 14.3 %collective-permute-start.3 = (bf16[144,1024]{1,0:T(8,128)(2,1)S(1)}, bf16[144,1024]{1,0:T(8,128)(2,1)S(1)}, u32[]{:S(2)}, u32[]{:S(2)}) collective-permute-start(bf16[144,1024]{1,0:T(8,128)(2,1)S(1)} %get-tuple-element.49), channel_id=1, source_target_pairs={{0,30},{2,4},{4,2},{6,8},{8,6},{10,12},{12,10},{14,16},{16,14},{18... | collective-permute-start | bytes 884744 | tf_op jit(solution)/shard_map/ppermute | solution.py:352
  13.9 11.5 %collective-permute-start.2 = (bf16[144,1024]{1,0:T(8,128)(2,1)S(1)}, bf16[144,1024]{1,0:T(8,128)(2,1)S(1)}, u32[]{:S(2)}, u32[]{:S(2)}) collective-permute-start(bf16[144,1024]{1,0:T(8,128)(2,1)S(1)} %get-tuple-element.45.own_ref), channel_id=1, source_target_pairs={{0,2},{2,0},{4,6},{6,4},{8,10},{10,8},{12,14},{14,12},{16,18},{18,... | collective-permute-start | bytes 884744 | tf_op jit(solution)/shard_map/ppermute | solution.py:347
  15.0 12.4 %collective-permute-start.5 = (bf16[128,1024]{1,0:T(8,128)(2,1)S(1)}, bf16[128,1024]{1,0:T(8,128)(2,1)S(1)}, u32[]{:S(2)}, u32[]{:S(2)}) collective-permute-start(bf16[128,1024]{1,0:T(8,128)(2,1)S(1)} %collective-permute-done.4.near_ref.near0_ref), channel_id=1, source_target_pairs={{0,4},{2,30},{4,8},{6,2},{8,12},{10,6},{12,16},{14,10},{16,20},{18... | collective-permute-start | bytes 786440 | tf_op jit(solution)/shard_map/ppermute | solution.py:359
  15.1 6.0 %collective-permute-start.1 = (f32[1,128]{1,0:T(1,128)S(1)}, f32[1,128]{1,0:T(1,128)S(1)}, u32[]{:S(2)}, u32[]{:S(2)}) collective-permute-start(f32[1,128]{1,0:T(1,128)S(1)} %get-tuple-element.47), channel_id=1, source_target_pairs={{0,8},{2,10},{4,12},{6,14},{8,0},{10,2},{12,4},{14,6},{16,24},{18,... | collective-permute-start | bytes 1544 | tf_op jit(solution)/shard_map/ppermute | solution.py:380
  29.0 8.3 %collective-permute-start.8 = (bf16[144,1024]{1,0:T(8,128)(2,1)S(1)}, bf16[144,1024]{1,0:T(8,128)(2,1)S(1)}, u32[]{:S(2)}, u32[]{:S(2)}) collective-permute-start(bf16[144,1024]{1,0:T(8,128)(2,1)S(1)} %get-tuple-element.59), channel_id=1, source_target_pairs={{0,28},{2,6},{4,0},{6,10},{8,4},{10,14},{12,8},{14,18},{16,12},{18... | collective-permute-start | bytes 884744 | tf_op jit(solution)/shard_map/ppermute | solution.py:366
  31.3 9.5 %collective-permute-start.6 = (bf16[128,1024]{1,0:T(8,128)(2,1)S(1)}, bf16[128,1024]{1,0:T(8,128)(2,1)S(1)}, u32[]{:S(2)}, u32[]{:S(2)}) collective-permute-start(bf16[128,1024]{1,0:T(8,128)(2,1)S(1)} %get-tuple-element.54.v_ref), channel_id=1, source_target_pairs={{0,2},{2,0},{4,6},{6,4},{8,10},{10,8},{12,14},{14,12},{16,18},{18,... | collective-permute-start | bytes 786440 | tf_op jit(solution)/shard_map/ppermute | solution.py:347
  31.3 5.6 %collective-permute-start.9 = (f32[1,128]{1,0:T(1,128)S(1)}, f32[1,128]{1,0:T(1,128)S(1)}, u32[]{:S(2)}, u32[]{:S(2)}) collective-permute-start(f32[1,128]{1,0:T(1,128)S(1)} %add.27), channel_id=1, source_target_pairs={{0,4},{2,6},{4,0},{6,2},{8,12},{10,14},{12,8},{14,10},{16,20},{18,... | collective-permute-start | bytes 1544 | tf_op jit(solution)/shard_map/ppermute | solution.py:380
  37.5 13.5 %collective-permute-start.10 = (bf16[144,1024]{1,0:T(8,128)(2,1)S(1)}, bf16[144,1024]{1,0:T(8,128)(2,1)S(1)}, u32[]{:S(2)}, u32[]{:S(2)}) collective-permute-start(bf16[144,1024]{1,0:T(8,128)(2,1)S(1)} %shard_map.78.own_ref), channel_id=1, source_target_pairs={{0,2},{2,0},{4,6},{6,4},{8,10},{10,8},{12,14},{14,12},{16,18},{18,... | collective-permute-start | bytes 884744 | tf_op jit(solution)/shard_map/ppermute | solution.py:347
  40.7 9.1 %collective-permute-start.7 = (bf16[128,1024]{1,0:T(8,128)(2,1)S(1)}, bf16[128,1024]{1,0:T(8,128)(2,1)S(1)}, u32[]{:S(2)}, u32[]{:S(2)}) collective-permute-start(bf16[128,1024]{1,0:T(8,128)(2,1)S(1)} %collective-permute-done.6.near_ref.near1_ref), channel_id=1, source_target_pairs={{0,4},{2,30},{4,8},{6,2},{8,12},{10,6},{12,16},{14,10},{16,20},{18... | collective-permute-start | bytes 786440 | tf_op jit(solution)/shard_map/ppermute | solution.py:359
  51.8 7.0 %collective-permute-start.12 = (bf16[128,1024]{1,0:T(8,128)(2,1)S(1)}, bf16[128,1024]{1,0:T(8,128)(2,1)S(1)}, u32[]{:S(2)}, u32[]{:S(2)}) collective-permute-start(bf16[128,1024]{1,0:T(8,128)(2,1)S(1)} %get-tuple-element.73), channel_id=1, source_target_pairs={{0,28},{2,6},{4,0},{6,10},{8,4},{10,14},{12,8},{14,18},{16,12},{18... | collective-permute-start | bytes 786440 | tf_op jit(solution)/shard_map/ppermute | solution.py:366
  53.0 6.5 %collective-permute-start.13 = (bf16[128,1024]{1,0:T(8,128)(2,1)S(1)}, bf16[128,1024]{1,0:T(8,128)(2,1)S(1)}, u32[]{:S(2)}, u32[]{:S(2)}) collective-permute-start(bf16[128,1024]{1,0:T(8,128)(2,1)S(1)} %get-tuple-element.74.v_ref), channel_id=1, source_target_pairs={{0,2},{2,0},{4,6},{6,4},{8,10},{10,8},{12,14},{14,12},{16,18},{18,... | collective-permute-start | bytes 786440 | tf_op jit(solution)/shard_map/ppermute | solution.py:347
  53.1 4.5 %collective-permute-start.11 = (f32[1,128]{1,0:T(1,128)S(1)}, f32[1,128]{1,0:T(1,128)S(1)}, u32[]{:S(2)}, u32[]{:S(2)}) collective-permute-start(f32[1,128]{1,0:T(1,128)S(1)} %get-tuple-element.62), channel_id=1, source_target_pairs={{0,16},{2,18},{4,20},{6,22},{8,24},{10,26},{12,28},{14,30},{16,0},... | collective-permute-start | bytes 1544 | tf_op jit(solution)/shard_map/ppermute | solution.py:380
  58.9 16.6 %copy-start.2 = (f32[1024,128]{1,0:T(8,128)S(1)}, f32[1024,128]{1,0:T(8,128)}, u32[]{:S(2)}) copy-start(f32[1024,128]{1,0:T(8,128)} %targets_ref.3) | copy-start | bytes 1572868
  59.7 6.9 %collective-permute-start.16 = (f32[8,128]{1,0:T(8,128)S(1)}, f32[8,128]{1,0:T(8,128)S(1)}, u32[]{:S(2)}, u32[]{:S(2)}) collective-permute-start(f32[8,128]{1,0:T(8,128)S(1)} %get-tuple-element.75), channel_id=1, source_target_pairs={{0,6},{2,4},{4,2},{6,0},{8,14},{10,12},{12,10},{14,8},{16,22},{18,... | collective-permute-start | bytes 12296 | tf_op jit(solution)/shard_map/ppermute | solution.py:390
  62.6 4.1 %collective-permute-start.15 = (f32[8,128]{1,0:T(8,128)S(1)}, f32[8,128]{1,0:T(8,128)S(1)}, u32[]{:S(2)}, u32[]{:S(2)}) collective-permute-start(f32[8,128]{1,0:T(8,128)S(1)} %get-tuple-element.75), channel_id=1, source_target_pairs={{0,4},{2,6},{4,0},{6,2},{8,12},{10,14},{12,8},{14,10},{16,20},{18,... | collective-permute-start | bytes 12296 | tf_op jit(solution)/shard_map/ppermute | solution.py:390
  62.6 4.1 %collective-permute-start.14 = (f32[8,128]{1,0:T(8,128)S(1)}, f32[8,128]{1,0:T(8,128)S(1)}, u32[]{:S(2)}, u32[]{:S(2)}) collective-permute-start(f32[8,128]{1,0:T(8,128)S(1)} %get-tuple-element.75), channel_id=1, source_target_pairs={{0,2},{2,0},{4,6},{6,4},{8,10},{10,8},{12,14},{14,12},{16,18},{18,... | collective-permute-start | bytes 12296 | tf_op jit(solution)/shard_map/ppermute | solution.py:390
  63.3 12.0 %collective-permute-start.21 = (bf16[128,1024]{1,0:T(8,128)(2,1)S(1)}, bf16[128,1024]{1,0:T(8,128)(2,1)S(1)}, u32[]{:S(2)}, u32[]{:S(2)}) collective-permute-start(bf16[128,1024]{1,0:T(8,128)(2,1)S(1)} %get-tuple-element.79), channel_id=1, source_target_pairs={{0,2},{2,0},{4,6},{6,4},{8,10},{10,8},{12,14},{14,12},{16,18},{18,... | collective-permute-start | bytes 786440 | tf_op jit(solution)/shard_map/ppermute | solution.py:347
  64.6 9.6 %collective-permute-start.20 = (bf16[128,1024]{1,0:T(8,128)(2,1)S(1)}, bf16[128,1024]{1,0:T(8,128)(2,1)S(1)}, u32[]{:S(2)}, u32[]{:S(2)}) collective-permute-start(bf16[128,1024]{1,0:T(8,128)(2,1)S(1)} %collective-permute-done.13.near_ref), channel_id=1, source_target_pairs={{0,4},{2,30},{4,8},{6,2},{8,12},{10,6},{12,16},{14,10},{16,20},{18... | collective-permute-start | bytes 786440 | tf_op jit(solution)/shard_map/ppermute | solution.py:359
  66.7 5.5 %collective-permute-start.19 = (f32[8,128]{1,0:T(8,128)S(1)}, f32[8,128]{1,0:T(8,128)S(1)}, u32[]{:S(2)}, u32[]{:S(2)}) collective-permute-start(f32[8,128]{1,0:T(8,128)S(1)} %add_add_fusion.1), channel_id=1, source_target_pairs={{0,24},{2,26},{4,28},{6,30},{8,16},{10,18},{12,20},{14,22},{16,8},... | collective-permute-start | bytes 12296 | tf_op jit(solution)/shard_map/ppermute | solution.py:390
  69.7 4.5 %collective-permute-start.18 = (f32[8,128]{1,0:T(8,128)S(1)}, f32[8,128]{1,0:T(8,128)S(1)}, u32[]{:S(2)}, u32[]{:S(2)}) collective-permute-start(f32[8,128]{1,0:T(8,128)S(1)} %add_add_fusion.1), channel_id=1, source_target_pairs={{0,16},{2,18},{4,20},{6,22},{8,24},{10,26},{12,28},{14,30},{16,0},... | collective-permute-start | bytes 12296 | tf_op jit(solution)/shard_map/ppermute | solution.py:390
  69.7 4.5 %collective-permute-start.17 = (f32[8,128]{1,0:T(8,128)S(1)}, f32[8,128]{1,0:T(8,128)S(1)}, u32[]{:S(2)}, u32[]{:S(2)}) collective-permute-start(f32[8,128]{1,0:T(8,128)S(1)} %add_add_fusion.1), channel_id=1, source_target_pairs={{0,8},{2,10},{4,12},{6,14},{8,0},{10,2},{12,4},{14,6},{16,24},{18,... | collective-permute-start | bytes 12296 | tf_op jit(solution)/shard_map/ppermute | solution.py:390

commit v6 on v5

--- a/solution.py
+++ b/solution.py
@@ -167,7 +167,7 @@
 
 def gather_first_kernel(ridge_ref, k_ref, local_ref, own_ref, near_ref, far_ref, sum_ref, mean_ref):
     cols, width = k_ref.shape[0], mean_ref.shape[1]
-    means = [ref[cols : cols + 8, :width].astype(F32)[:1] for ref in (own_ref, near_ref, far_ref)]
+    means = [ref[cols : cols + 16, :width].astype(F32)[:1] for ref in (own_ref, near_ref, far_ref)]
     odd = is_odd(means[0].shape)
     means += [jnp.where(odd, means[1], means[2]), jnp.where(odd, means[2], means[1])]
     means.append(means[0] + means[1])
@@ -210,7 +210,7 @@
     k0_ref, k_ref, mean_ref, sum_ref, own_ref, q_ref, next_ref, rounded_ref, total_ref
 ):
     cols, width = k_ref.shape[0], total_ref.shape[1]
-    sums = [ref[cols : cols + 8, :width].astype(F32)[:1] for ref in (own_ref, q_ref)]
+    sums = [ref[cols : cols + 16, :width].astype(F32)[:1] for ref in (own_ref, q_ref)]
     total_ref[...] = sums[0] + sums[1]
     value = sum_ref[...] + 0.5 * q_ref[:cols, :].astype(F32)
     next_ref[...] = value
@@ -227,7 +227,7 @@
     cols, width = k0_ref.shape[0], moment_ref.shape[1]
     c = shift_ref[0:1, 0:1]
     own, mean_near, mean_far, mean_before, mean_after = (mean_ref[i : i + 1, 0:1] - c for i in range(5))
-    other = r1_ref[cols : cols + 8, :width].astype(F32)[:1, :1] - c
+    other = r1_ref[cols : cols + 16, :width].astype(F32)[:1, :1] - c
     totals = [jnp.zeros((cols, width), F32)] * 5
     for at in range(0, k0_ref.shape[1], width):
         out = slice(at, at + width)

time: 76.8 us -> 76.8 us (level)
  no operation moved by 1% of the time
where the time goes in v6:
time: 76.8 us; the launch traced here: 76.6 us
  waiting for transfers between devices  31.1 us (40%)
  starting transfers between devices  28.4 us (37%)
  Pallas kernels  15.1 us (20%)
  local copies, waits for them, and re-layouts  1.17 us (2%)
  between operations  0.87 us (1%)
    pallas_call x19, Pallas kernels, call(): pl.pallas_call(kernel, out_shape=out_shape, in_specs=specs, out_specs=jax...  15.1 us
    ppermute x3, waiting for transfers between devices, sum_step(): lax.ppermute(value, axis, [(i, i ^ distance) for i in range(count)])  12.7 us
    ppermute x3, waiting for transfers between devices, forward(): lax.ppermute(value, 'asset', [(i, (i - 2 if i % 2 else i + 2) % count) fo...  9.81 us
    ppermute x6, starting transfers between devices, sum_over(): total = total + lax.ppermute(value, axis, route)  8 us
    ppermute x6, starting transfers between devices, near(): return lax.ppermute(value, 'asset', [(i, i ^ 1) for i in range(count)])  7.29 us
    ppermute x1, starting transfers between devices, far(): lax.ppermute(value, 'asset', [(i, (i + 1 if i % 2 else i - 1) % count) fo...  4.82 us
    ppermute x3, starting transfers between devices, sum_step(): lax.ppermute(value, axis, [(i, i ^ distance) for i in range(count)])  3.35 us
    ppermute x6, waiting for transfers between devices, sum_over(): total = total + lax.ppermute(value, axis, route)  3.12 us
  transfers between devices with their start and end apart: 22, of which 11 were waited for; matrix products, arithmetic and copies ran while one was open for 0% of the time, Pallas kernels for 14%

profile of v6, /device:TPU:0, one launch (start us, length us, event | category | flops | bytes accessed | tf_op | source)
XLA Modules:
  0.0 76.6 jit_solution(1519859397863212593)
XLA Ops:
  0.6 0.5 collective-permute-start
  1.2 1.1 %copy-done.1 = f32[1024,128]{1,0:T(8,128)S(1)} copy-done((f32[1024,128]{1,0:T(8,128)S(1)}, f32[1024,128]{1,0:T(8,128)}, u32[]{:S(2)}) %copy-start.1) | copy-done | bytes 524312
  2.3 0.2 shard_map.68
  2.5 2.6 %collective-permute-start.4 = (bf16[128,1024]{1,0:T(8,128)(2,1)S(1)}, bf16[128,1024]{1,0:T(8,128)(2,1)S(1)}, u32[]{:S(2)}, u32[]{:S(2)}) collective-permute-start(bf16[128,1024]{1,0:T(8,128)(2,1)S(1)} %get-tuple-element.46.v_ref), channel_id=1, source_target_pairs={{0,2},{2,0},{4,6},{6,4},{8,10},{10,8},{12,14},{14,12},{16,18},{18,... | collective-permute-start | bytes 786440 | tf_op jit(solution)/shard_map/ppermute | solution.py:347
  5.1 2.1 %shard_map.69 = (bf16[25,1024,128]{2,1,0:T(8,128)(2,1)S(1)}, f32[1,128]{1,0:T(1,128)S(1)}) custom-call(s32[8,16]{1,0:T(8,128)S(1)} %copy-done.4, s32[8]{0:T(128)S(1)} %copy-done.5, bf16[8,16,64,128]{3,2,1,0:T(8,128)(2,1)S(1)} %copy-done, f32[1,1024]{1,0:T(1,128)S(1)} %bitcast.1), custom_call_target="tpu_custom_call" | custom-call | tf_op jit(solution)/shard_map/pallas_call | solution.py:22
  7.2 0.0 collective-permute-done.part_ref
  7.2 1.2 %shard_map.70.band_ref = bf16[25,1024,128]{2,1,0:T(8,128)(2,1)S(1)} custom-call(s32[8,16]{1,0:T(8,128)S(1)} %copy-done.4, s32[8]{0:T(128)S(1)} %copy-done.5, bf16[8,16,64,128]{3,2,1,0:T(8,128)(2,1)S(1)} %collective-permute-done.part_ref, bf16[25,1024,128]{2,1,0:T(8,128)(2,1)S(1)} %get-tuple-element.42._), custom_call_target="tpu_custom_call", output_to_operand_aliasing={{}: (3, {})} | custom-call | tf_op jit(solution)/shard_map/pallas_call | solution.py:22
  8.5 0.5 shard_map.71
  9.1 4.8 %collective-permute-start.3 = (bf16[144,1024]{1,0:T(8,128)(2,1)S(1)}, bf16[144,1024]{1,0:T(8,128)(2,1)S(1)}, u32[]{:S(2)}, u32[]{:S(2)}) collective-permute-start(bf16[144,1024]{1,0:T(8,128)(2,1)S(1)} %get-tuple-element.49), channel_id=1, source_target_pairs={{0,30},{2,4},{4,2},{6,8},{8,6},{10,12},{12,10},{14,16},{16,14},{18... | collective-permute-start | bytes 884744 | tf_op jit(solution)/shard_map/ppermute | solution.py:352
  13.9 0.0 collective-permute-start.2
  13.9 1.1 %shard_map.72.local_ref.local0_ref = f32[128,1024]{1,0:T(8,128)S(1)} custom-call(bf16[25,1024,128]{2,1,0:T(8,128)(2,1)S(1)} %shard_map.70.band_ref, bf16[128,1024]{1,0:T(8,128)(2,1)S(1)} %get-tuple-element.46.v_ref), custom_call_target="tpu_custom_call" | custom-call | tf_op jit(solution)/shard_map/pallas_call | solution.py:22
  15.0 0.0 collective-permute-done.4.near_ref.near0_ref
  15.0 0.1 collective-permute-start.5
  15.1 1.3 %collective-permute-start.1 = (f32[1,128]{1,0:T(1,128)S(1)}, f32[1,128]{1,0:T(1,128)S(1)}, u32[]{:S(2)}, u32[]{:S(2)}) collective-permute-start(f32[1,128]{1,0:T(1,128)S(1)} %get-tuple-element.47), channel_id=1, source_target_pairs={{0,8},{2,10},{4,12},{6,14},{8,0},{10,2},{12,4},{14,6},{16,24},{18,... | collective-permute-start | bytes 1544 | tf_op jit(solution)/shard_map/ppermute | solution.py:380
  16.4 4.7 %collective-permute-done.1 = f32[1,128]{1,0:T(1,128)S(1)} collective-permute-done((f32[1,128]{1,0:T(1,128)S(1)}, f32[1,128]{1,0:T(1,128)S(1)}, u32[]{:S(2)}, u32[]{:S(2)}) %collective-permute-start.1) | collective-permute-done | bytes 544 | tf_op jit(solution)/shard_map/ppermute | solution.py:380
  21.1 2.2 %collective-permute-done.3.far_ref.qf0_ref = bf16[144,1024]{1,0:T(8,128)(2,1)S(1)} collective-permute-done((bf16[144,1024]{1,0:T(8,128)(2,1)S(1)}, bf16[144,1024]{1,0:T(8,128)(2,1)S(1)}, u32[]{:S(2)}, u32[]{:S(2)}) %collective-permute-start.3) | collective-permute-done | bytes 294944 | tf_op jit(solution)/shard_map/ppermute | solution.py:352
  23.3 2.1 %collective-permute-done.2.near_ref.qn0_ref = bf16[144,1024]{1,0:T(8,128)(2,1)S(1)} collective-permute-done((bf16[144,1024]{1,0:T(8,128)(2,1)S(1)}, bf16[144,1024]{1,0:T(8,128)(2,1)S(1)}, u32[]{:S(2)}, u32[]{:S(2)}) %collective-permute-start.2) | collective-permute-done | bytes 294944 | tf_op jit(solution)/shard_map/ppermute | solution.py:347
  25.4 0.1 shard_map.73
  25.5 1.9 %collective-permute-done.5.far_ref = bf16[128,1024]{1,0:T(8,128)(2,1)S(1)} collective-permute-done((bf16[128,1024]{1,0:T(8,128)(2,1)S(1)}, bf16[128,1024]{1,0:T(8,128)(2,1)S(1)}, u32[]{:S(2)}, u32[]{:S(2)}) %collective-permute-start.5) | collective-permute-done | bytes 262176 | tf_op jit(solution)/shard_map/ppermute | solution.py:359
  27.4 1.0 %shard_map.74 = (f32[128,1024]{1,0:T(8,128)S(1)}, bf16[128,1024]{1,0:T(8,128)(2,1)S(1)}, f32[128,1024]{1,0:T(8,128)S(1)}, f32[128,1024]{1,0:T(8,128)S(1)}) custom-call(bf16[25,1024,128]{2,1,0:T(8,128)(2,1)S(1)} %shard_map.70.band_ref, f32[128,1024]{1,0:T(8,128)S(1)} %get-tuple-element.50.sum_ref, f32[128,1024]{1,0:T(8,128)S(1)} %get-tuple-element.41.k_ref.k0_ref, ...), custom_call_target="tpu_custom_call" | custom-call | tf_op jit(solution)/shard_map/pallas_call | solution.py:22
  28.4 0.6 shard_map.77
  29.0 2.3 %collective-permute-start.8 = (bf16[144,1024]{1,0:T(8,128)(2,1)S(1)}, bf16[144,1024]{1,0:T(8,128)(2,1)S(1)}, u32[]{:S(2)}, u32[]{:S(2)}) collective-permute-start(bf16[144,1024]{1,0:T(8,128)(2,1)S(1)} %get-tuple-element.59), channel_id=1, source_target_pairs={{0,28},{2,6},{4,0},{6,10},{8,4},{10,14},{12,8},{14,18},{16,12},{18... | collective-permute-start | bytes 884744 | tf_op jit(solution)/shard_map/ppermute | solution.py:366
  31.3 0.0 collective-permute-start.6
  31.3 0.7 collective-permute-start.9
  31.9 4.9 %collective-permute-done.9 = f32[1,128]{1,0:T(1,128)S(1)} collective-permute-done((f32[1,128]{1,0:T(1,128)S(1)}, f32[1,128]{1,0:T(1,128)S(1)}, u32[]{:S(2)}, u32[]{:S(2)}) %collective-permute-start.9) | collective-permute-done | bytes 544 | tf_op jit(solution)/shard_map/ppermute | solution.py:380
  36.8 0.5 collective-permute-done.8.received_ref.r1_ref
  37.3 0.1 shard_map.78.own_ref
  37.5 3.3 %collective-permute-start.10 = (bf16[144,1024]{1,0:T(8,128)(2,1)S(1)}, bf16[144,1024]{1,0:T(8,128)(2,1)S(1)}, u32[]{:S(2)}, u32[]{:S(2)}) collective-permute-start(bf16[144,1024]{1,0:T(8,128)(2,1)S(1)} %shard_map.78.own_ref), channel_id=1, source_target_pairs={{0,2},{2,0},{4,6},{6,4},{8,10},{10,8},{12,14},{14,12},{16,18},{18,... | collective-permute-start | bytes 884744 | tf_op jit(solution)/shard_map/ppermute | solution.py:347
  40.7 0.0 collective-permute-done.6.near_ref.near1_ref
  40.7 0.0 collective-permute-start.7
  40.7 1.1 %shard_map.75.local_ref.local1_ref = f32[128,1024]{1,0:T(8,128)S(1)} custom-call(bf16[25,1024,128]{2,1,0:T(8,128)(2,1)S(1)} %shard_map.70.band_ref, bf16[128,1024]{1,0:T(8,128)(2,1)S(1)} %get-tuple-element.54.v_ref), custom_call_target="tpu_custom_call" | custom-call | tf_op jit(solution)/shard_map/pallas_call | solution.py:22
  41.9 7.9 %collective-permute-done.7.far_ref = bf16[128,1024]{1,0:T(8,128)(2,1)S(1)} collective-permute-done((bf16[128,1024]{1,0:T(8,128)(2,1)S(1)}, bf16[128,1024]{1,0:T(8,128)(2,1)S(1)}, u32[]{:S(2)}, u32[]{:S(2)}) %collective-permute-start.7) | collective-permute-done | bytes 262176 | tf_op jit(solution)/shard_map/ppermute | solution.py:359
  49.8 1.1 %shard_map.76 = (f32[128,1024]{1,0:T(8,128)S(1)}, f32[128,1024]{1,0:T(8,128)S(1)}, f32[128,1024]{1,0:T(8,128)S(1)}) custom-call(bf16[25,1024,128]{2,1,0:T(8,128)(2,1)S(1)} %shard_map.70.band_ref, f32[1,1024]{1,0:T(1,128)S(1)} %bitcast.4, f32[8,128]{1,0:T(8,128)S(1)} %get-tuple-element.51.mean_ref, f32[128,1024]{1,0:T(8,128)S(1)} %get-tuple-element.53.k_ref.k1_ref, ...), custom_call_target="tpu_custom_call" | custom-call | tf_op jit(solution)/shard_map/pallas_call | solution.py:22
  50.9 0.0 collective-permute-done.10.q_ref
  51.0 0.3 shard_map.79
  51.3 0.6 shard_map.80
  51.8 0.1 collective-permute-start.12
  51.9 1.1 %shard_map.81.local2_ref = f32[128,1024]{1,0:T(8,128)S(1)} custom-call(bf16[25,1024,128]{2,1,0:T(8,128)(2,1)S(1)} %shard_map.70.band_ref, bf16[128,1024]{1,0:T(8,128)(2,1)S(1)} %get-tuple-element.74.v_ref), custom_call_target="tpu_custom_call" | custom-call | flops 5000000000 | bytes 1048576 | tf_op jit(solution)/shard_map/pallas_call | solution.py:22
  53.0 0.1 collective-permute-start.13
  53.1 1.4 %collective-permute-start.11 = (f32[1,128]{1,0:T(1,128)S(1)}, f32[1,128]{1,0:T(1,128)S(1)}, u32[]{:S(2)}, u32[]{:S(2)}) collective-permute-start(f32[1,128]{1,0:T(1,128)S(1)} %get-tuple-element.62), channel_id=1, source_target_pairs={{0,16},{2,18},{4,20},{6,22},{8,24},{10,26},{12,28},{14,30},{16,0},... | collective-permute-start | bytes 1544 | tf_op jit(solution)/shard_map/ppermute | solution.py:380
  54.5 3.1 %collective-permute-done.11 = f32[1,128]{1,0:T(1,128)S(1)} collective-permute-done((f32[1,128]{1,0:T(1,128)S(1)}, f32[1,128]{1,0:T(1,128)S(1)}, u32[]{:S(2)}, u32[]{:S(2)}) %collective-permute-start.11) | collective-permute-done | bytes 544 | tf_op jit(solution)/shard_map/ppermute | solution.py:380
  57.6 1.2 %shard_map.82 = (f32[128,1024]{1,0:T(8,128)S(1)}, f32[1024,128]{1,0:T(8,128)S(1)}, f32[1024,128]{1,0:T(8,128)S(1)}, f32[8,128]{1,0:T(8,128)S(1)}, f32[128,1024]{1,0:T(8,128)S(1)}, /*index=5*/f32[128,1024]{1,0:T(8,128)S(1)}) custom-call(f32[1,128]{1,0:T(1,128)S(1)} %add_multiply_fusion.shift_ref, f32[8,128]{1,0:T(8,128)S(1)} %get-tuple-element.51.mean_ref, ...), custom_call_target="tpu_custom_call" | custom-call | tf_op jit(solution)/shard_map/pallas_call | solution.py:22
  58.9 0.0 copy-start.2
  58.9 0.0 collective-permute-done.12.received_ref
  58.9 0.6 collective-permute-done.13.near_ref
  59.5 0.2 shard_map.83
  59.7 2.8 %collective-permute-start.16 = (f32[8,128]{1,0:T(8,128)S(1)}, f32[8,128]{1,0:T(8,128)S(1)}, u32[]{:S(2)}, u32[]{:S(2)}) collective-permute-start(f32[8,128]{1,0:T(8,128)S(1)} %get-tuple-element.75), channel_id=1, source_target_pairs={{0,6},{2,4},{4,2},{6,0},{8,14},{10,12},{12,10},{14,8},{16,22},{18,... | collective-permute-start | bytes 12296 | tf_op jit(solution)/shard_map/ppermute | solution.py:390
  62.6 0.0 collective-permute-start.15
  62.6 0.7 collective-permute-start.14
  63.3 1.3 %collective-permute-start.21 = (bf16[128,1024]{1,0:T(8,128)(2,1)S(1)}, bf16[128,1024]{1,0:T(8,128)(2,1)S(1)}, u32[]{:S(2)}, u32[]{:S(2)}) collective-permute-start(bf16[128,1024]{1,0:T(8,128)(2,1)S(1)} %get-tuple-element.79), channel_id=1, source_target_pairs={{0,2},{2,0},{4,6},{6,4},{8,10},{10,8},{12,14},{14,12},{16,18},{18,... | collective-permute-start | bytes 786440 | tf_op jit(solution)/shard_map/ppermute | solution.py:347
  64.6 2.0 %collective-permute-start.20 = (bf16[128,1024]{1,0:T(8,128)(2,1)S(1)}, bf16[128,1024]{1,0:T(8,128)(2,1)S(1)}, u32[]{:S(2)}, u32[]{:S(2)}) collective-permute-start(bf16[128,1024]{1,0:T(8,128)(2,1)S(1)} %collective-permute-done.13.near_ref), channel_id=1, source_target_pairs={{0,4},{2,30},{4,8},{6,2},{8,12},{10,6},{12,16},{14,10},{16,20},{18... | collective-permute-start | bytes 786440 | tf_op jit(solution)/shard_map/ppermute | solution.py:359
  66.6 0.0 collective-permute-done.16
  66.6 0.0 collective-permute-done.15
  66.6 0.0 collective-permute-done.14
  66.7 3.1 %collective-permute-start.19 = (f32[8,128]{1,0:T(8,128)S(1)}, f32[8,128]{1,0:T(8,128)S(1)}, u32[]{:S(2)}, u32[]{:S(2)}) collective-permute-start(f32[8,128]{1,0:T(8,128)S(1)} %add_add_fusion.1), channel_id=1, source_target_pairs={{0,24},{2,26},{4,28},{6,30},{8,16},{10,18},{12,20},{14,22},{16,8},... | collective-permute-start | bytes 12296 | tf_op jit(solution)/shard_map/ppermute | solution.py:390
  69.7 0.0 collective-permute-start.18
  69.7 1.4 %collective-permute-start.17 = (f32[8,128]{1,0:T(8,128)S(1)}, f32[8,128]{1,0:T(8,128)S(1)}, u32[]{:S(2)}, u32[]{:S(2)}) collective-permute-start(f32[8,128]{1,0:T(8,128)S(1)} %add_add_fusion.1), channel_id=1, source_target_pairs={{0,8},{2,10},{4,12},{6,14},{8,0},{10,2},{12,4},{14,6},{16,24},{18,... | collective-permute-start | bytes 12296 | tf_op jit(solution)/shard_map/ppermute | solution.py:390
  71.1 1.0 %collective-permute-done.19 = f32[8,128]{1,0:T(8,128)S(1)} collective-permute-done((f32[8,128]{1,0:T(8,128)S(1)}, f32[8,128]{1,0:T(8,128)S(1)}, u32[]{:S(2)}, u32[]{:S(2)}) %collective-permute-start.19) | collective-permute-done | bytes 4128 | tf_op jit(solution)/shard_map/ppermute | solution.py:390
  72.1 2.1 %collective-permute-done.18 = f32[8,128]{1,0:T(8,128)S(1)} collective-permute-done((f32[8,128]{1,0:T(8,128)S(1)}, f32[8,128]{1,0:T(8,128)S(1)}, u32[]{:S(2)}, u32[]{:S(2)}) %collective-permute-start.18) | collective-permute-done | bytes 4128 | tf_op jit(solution)/shard_map/ppermute | solution.py:390
  74.2 0.0 collective-permute-done.17
  74.2 0.0 collective-permute-done.20.far_ref
  74.2 1.0 %shard_map.84.sum_ref = f32[128,1024]{1,0:T(8,128)S(1)} custom-call(bf16[25,1024,128]{2,1,0:T(8,128)(2,1)S(1)} %shard_map.70.band_ref, f32[128,1024]{1,0:T(8,128)S(1)} %get-tuple-element.78.known_ref, bf16[128,1024]{1,0:T(8,128)(2,1)S(1)} %collective-permute-done.13.near_ref, bf16[128,1024]{1,0:T(8,128)(2,1)S(1)} %collective-permute-done.20.far_ref), custom_call_target="tpu_custom_call" | custom-call | tf_op jit(solution)/shard_map/pallas_call | solution.py:22
  75.3 0.2 shard_map.85.k3_ref
  75.5 1.2 %shard_map.86 = (f32[1024,128]{1,0:T(8,128)}, f32[1024,128]{1,0:T(8,128)}) custom-call(f32[1,128]{1,0:T(1,128)S(1)} %add_multiply_fusion.shift_ref, f32[8,128]{1,0:T(8,128)S(1)} %add_add_fusion.moment_ref, f32[1024,128]{1,0:T(8,128)S(1)} %copy-done.2, f32[1024,128]{1,0:T(8,128)S(1)} %get-tuple-element.76.k1_ref, f32[1024,128]{1,0:T(8,128)S(1)} %get-tuple-element.77.k2_ref, ...), custom_call_target="tpu_custom_call" | custom-call | tf_op jit(solution)/shard_map/pallas_call | solution.py:22
  (16 shorter events, 0.0 us)
Async XLA Ops:
  0.6 4.5 %copy-start = (bf16[8,16,64,128]{3,2,1,0:T(8,128)(2,1)S(1)}, bf16[8,16,64,128]{3,2,1,0:T(8,128)(2,1)}, u32[]{:S(2)}) copy-start(bf16[8,16,64,128]{3,2,1,0:T(8,128)(2,1)} %part_ref.1) | copy-start | bytes 6291460
  0.6 6.6 %collective-permute-start = (bf16[8,16,64,128]{3,2,1,0:T(8,128)(2,1)}, bf16[8,16,64,128]{3,2,1,0:T(8,128)(2,1)S(1)}, u32[]{:S(2)}, u32[]{:S(2)}) collective-permute-start(bf16[8,16,64,128]{3,2,1,0:T(8,128)(2,1)} %part_ref.1), channel_id=1, source_target_pairs={{0,1},{1,0},{2,3},{3,2},{4,5},{5,4},{6,7},{7,6},{8,9},{9,8},{10,11... | collective-permute-start | bytes 6291464 | tf_op jit(solution)/shard_map/ppermute | solution.py:414
  1.2 1.1 %copy-start.1 = (f32[1024,128]{1,0:T(8,128)S(1)}, f32[1024,128]{1,0:T(8,128)}, u32[]{:S(2)}) copy-start(f32[1024,128]{1,0:T(8,128)} %targets_ref.3) | copy-start | bytes 1572868
  2.3 2.8 %copy-start.3 = (f32[1024]{0:T(1024)S(1)}, f32[1024]{0:T(1024)}, u32[]{:S(2)}) copy-start(f32[1024]{0:T(1024)} %param.6) | copy-start | bytes 12292
  2.3 2.8 %copy-start.4 = (s32[8,16]{1,0:T(8,128)S(1)}, s32[8,16]{1,0:T(8,128)}, u32[]{:S(2)}) copy-start(s32[8,16]{1,0:T(8,128)} %col_ref.3) | copy-start | bytes 1540
  2.3 2.8 %copy-start.5 = (s32[8]{0:T(128)S(1)}, s32[8]{0:T(128)}, u32[]{:S(2)}) copy-start(s32[8]{0:T(128)} %length_ref.3) | copy-start | bytes 100
  2.5 12.5 %collective-permute-start.4 = (bf16[128,1024]{1,0:T(8,128)(2,1)S(1)}, bf16[128,1024]{1,0:T(8,128)(2,1)S(1)}, u32[]{:S(2)}, u32[]{:S(2)}) collective-permute-start(bf16[128,1024]{1,0:T(8,128)(2,1)S(1)} %get-tuple-element.46.v_ref), channel_id=1, source_target_pairs={{0,2},{2,0},{4,6},{6,4},{8,10},{10,8},{12,14},{14,12},{16,18},{18,... | collective-permute-start | bytes 786440 | tf_op jit(solution)/shard_map/ppermute | solution.py:347
  9.1 14.3 %collective-permute-start.3 = (bf16[144,1024]{1,0:T(8,128)(2,1)S(1)}, bf16[144,1024]{1,0:T(8,128)(2,1)S(1)}, u32[]{:S(2)}, u32[]{:S(2)}) collective-permute-start(bf16[144,1024]{1,0:T(8,128)(2,1)S(1)} %get-tuple-element.49), channel_id=1, source_target_pairs={{0,30},{2,4},{4,2},{6,8},{8,6},{10,12},{12,10},{14,16},{16,14},{18... | collective-permute-start | bytes 884744 | tf_op jit(solution)/shard_map/ppermute | solution.py:352
  13.9 11.5 %collective-permute-start.2 = (bf16[144,1024]{1,0:T(8,128)(2,1)S(1)}, bf16[144,1024]{1,0:T(8,128)(2,1)S(1)}, u32[]{:S(2)}, u32[]{:S(2)}) collective-permute-start(bf16[144,1024]{1,0:T(8,128)(2,1)S(1)} %get-tuple-element.45.own_ref), channel_id=1, source_target_pairs={{0,2},{2,0},{4,6},{6,4},{8,10},{10,8},{12,14},{14,12},{16,18},{18,... | collective-permute-start | bytes 884744 | tf_op jit(solution)/shard_map/ppermute | solution.py:347
  15.0 12.4 %collective-permute-start.5 = (bf16[128,1024]{1,0:T(8,128)(2,1)S(1)}, bf16[128,1024]{1,0:T(8,128)(2,1)S(1)}, u32[]{:S(2)}, u32[]{:S(2)}) collective-permute-start(bf16[128,1024]{1,0:T(8,128)(2,1)S(1)} %collective-permute-done.4.near_ref.near0_ref), channel_id=1, source_target_pairs={{0,4},{2,30},{4,8},{6,2},{8,12},{10,6},{12,16},{14,10},{16,20},{18... | collective-permute-start | bytes 786440 | tf_op jit(solution)/shard_map/ppermute | solution.py:359
  15.1 6.0 %collective-permute-start.1 = (f32[1,128]{1,0:T(1,128)S(1)}, f32[1,128]{1,0:T(1,128)S(1)}, u32[]{:S(2)}, u32[]{:S(2)}) collective-permute-start(f32[1,128]{1,0:T(1,128)S(1)} %get-tuple-element.47), channel_id=1, source_target_pairs={{0,8},{2,10},{4,12},{6,14},{8,0},{10,2},{12,4},{14,6},{16,24},{18,... | collective-permute-start | bytes 1544 | tf_op jit(solution)/shard_map/ppermute | solution.py:380
  29.0 8.3 %collective-permute-start.8 = (bf16[144,1024]{1,0:T(8,128)(2,1)S(1)}, bf16[144,1024]{1,0:T(8,128)(2,1)S(1)}, u32[]{:S(2)}, u32[]{:S(2)}) collective-permute-start(bf16[144,1024]{1,0:T(8,128)(2,1)S(1)} %get-tuple-element.59), channel_id=1, source_target_pairs={{0,28},{2,6},{4,0},{6,10},{8,4},{10,14},{12,8},{14,18},{16,12},{18... | collective-permute-start | bytes 884744 | tf_op jit(solution)/shard_map/ppermute | solution.py:366
  31.3 9.5 %collective-permute-start.6 = (bf16[128,1024]{1,0:T(8,128)(2,1)S(1)}, bf16[128,1024]{1,0:T(8,128)(2,1)S(1)}, u32[]{:S(2)}, u32[]{:S(2)}) collective-permute-start(bf16[128,1024]{1,0:T(8,128)(2,1)S(1)} %get-tuple-element.54.v_ref), channel_id=1, source_target_pairs={{0,2},{2,0},{4,6},{6,4},{8,10},{10,8},{12,14},{14,12},{16,18},{18,... | collective-permute-start | bytes 786440 | tf_op jit(solution)/shard_map/ppermute | solution.py:347
  31.3 5.6 %collective-permute-start.9 = (f32[1,128]{1,0:T(1,128)S(1)}, f32[1,128]{1,0:T(1,128)S(1)}, u32[]{:S(2)}, u32[]{:S(2)}) collective-permute-start(f32[1,128]{1,0:T(1,128)S(1)} %add.27), channel_id=1, source_target_pairs={{0,4},{2,6},{4,0},{6,2},{8,12},{10,14},{12,8},{14,10},{16,20},{18,... | collective-permute-start | bytes 1544 | tf_op jit(solution)/shard_map/ppermute | solution.py:380
  37.5 13.5 %collective-permute-start.10 = (bf16[144,1024]{1,0:T(8,128)(2,1)S(1)}, bf16[144,1024]{1,0:T(8,128)(2,1)S(1)}, u32[]{:S(2)}, u32[]{:S(2)}) collective-permute-start(bf16[144,1024]{1,0:T(8,128)(2,1)S(1)} %shard_map.78.own_ref), channel_id=1, source_target_pairs={{0,2},{2,0},{4,6},{6,4},{8,10},{10,8},{12,14},{14,12},{16,18},{18,... | collective-permute-start | bytes 884744 | tf_op jit(solution)/shard_map/ppermute | solution.py:347
  40.7 9.1 %collective-permute-start.7 = (bf16[128,1024]{1,0:T(8,128)(2,1)S(1)}, bf16[128,1024]{1,0:T(8,128)(2,1)S(1)}, u32[]{:S(2)}, u32[]{:S(2)}) collective-permute-start(bf16[128,1024]{1,0:T(8,128)(2,1)S(1)} %collective-permute-done.6.near_ref.near1_ref), channel_id=1, source_target_pairs={{0,4},{2,30},{4,8},{6,2},{8,12},{10,6},{12,16},{14,10},{16,20},{18... | collective-permute-start | bytes 786440 | tf_op jit(solution)/shard_map/ppermute | solution.py:359
  51.8 7.0 %collective-permute-start.12 = (bf16[128,1024]{1,0:T(8,128)(2,1)S(1)}, bf16[128,1024]{1,0:T(8,128)(2,1)S(1)}, u32[]{:S(2)}, u32[]{:S(2)}) collective-permute-start(bf16[128,1024]{1,0:T(8,128)(2,1)S(1)} %get-tuple-element.73), channel_id=1, source_target_pairs={{0,28},{2,6},{4,0},{6,10},{8,4},{10,14},{12,8},{14,18},{16,12},{18... | collective-permute-start | bytes 786440 | tf_op jit(solution)/shard_map/ppermute | solution.py:366
  53.0 6.5 %collective-permute-start.13 = (bf16[128,1024]{1,0:T(8,128)(2,1)S(1)}, bf16[128,1024]{1,0:T(8,128)(2,1)S(1)}, u32[]{:S(2)}, u32[]{:S(2)}) collective-permute-start(bf16[128,1024]{1,0:T(8,128)(2,1)S(1)} %get-tuple-element.74.v_ref), channel_id=1, source_target_pairs={{0,2},{2,0},{4,6},{6,4},{8,10},{10,8},{12,14},{14,12},{16,18},{18,... | collective-permute-start | bytes 786440 | tf_op jit(solution)/shard_map/ppermute | solution.py:347
  53.1 4.5 %collective-permute-start.11 = (f32[1,128]{1,0:T(1,128)S(1)}, f32[1,128]{1,0:T(1,128)S(1)}, u32[]{:S(2)}, u32[]{:S(2)}) collective-permute-start(f32[1,128]{1,0:T(1,128)S(1)} %get-tuple-element.62), channel_id=1, source_target_pairs={{0,16},{2,18},{4,20},{6,22},{8,24},{10,26},{12,28},{14,30},{16,0},... | collective-permute-start | bytes 1544 | tf_op jit(solution)/shard_map/ppermute | solution.py:380
  58.9 16.6 %copy-start.2 = (f32[1024,128]{1,0:T(8,128)S(1)}, f32[1024,128]{1,0:T(8,128)}, u32[]{:S(2)}) copy-start(f32[1024,128]{1,0:T(8,128)} %targets_ref.3) | copy-start | bytes 1572868
  59.7 6.9 %collective-permute-start.16 = (f32[8,128]{1,0:T(8,128)S(1)}, f32[8,128]{1,0:T(8,128)S(1)}, u32[]{:S(2)}, u32[]{:S(2)}) collective-permute-start(f32[8,128]{1,0:T(8,128)S(1)} %get-tuple-element.75), channel_id=1, source_target_pairs={{0,6},{2,4},{4,2},{6,0},{8,14},{10,12},{12,10},{14,8},{16,22},{18,... | collective-permute-start | bytes 12296 | tf_op jit(solution)/shard_map/ppermute | solution.py:390
  62.6 4.1 %collective-permute-start.15 = (f32[8,128]{1,0:T(8,128)S(1)}, f32[8,128]{1,0:T(8,128)S(1)}, u32[]{:S(2)}, u32[]{:S(2)}) collective-permute-start(f32[8,128]{1,0:T(8,128)S(1)} %get-tuple-element.75), channel_id=1, source_target_pairs={{0,4},{2,6},{4,0},{6,2},{8,12},{10,14},{12,8},{14,10},{16,20},{18,... | collective-permute-start | bytes 12296 | tf_op jit(solution)/shard_map/ppermute | solution.py:390
  62.6 4.1 %collective-permute-start.14 = (f32[8,128]{1,0:T(8,128)S(1)}, f32[8,128]{1,0:T(8,128)S(1)}, u32[]{:S(2)}, u32[]{:S(2)}) collective-permute-start(f32[8,128]{1,0:T(8,128)S(1)} %get-tuple-element.75), channel_id=1, source_target_pairs={{0,2},{2,0},{4,6},{6,4},{8,10},{10,8},{12,14},{14,12},{16,18},{18,... | collective-permute-start | bytes 12296 | tf_op jit(solution)/shard_map/ppermute | solution.py:390
  63.3 12.0 %collective-permute-start.21 = (bf16[128,1024]{1,0:T(8,128)(2,1)S(1)}, bf16[128,1024]{1,0:T(8,128)(2,1)S(1)}, u32[]{:S(2)}, u32[]{:S(2)}) collective-permute-start(bf16[128,1024]{1,0:T(8,128)(2,1)S(1)} %get-tuple-element.79), channel_id=1, source_target_pairs={{0,2},{2,0},{4,6},{6,4},{8,10},{10,8},{12,14},{14,12},{16,18},{18,... | collective-permute-start | bytes 786440 | tf_op jit(solution)/shard_map/ppermute | solution.py:347
  64.6 9.6 %collective-permute-start.20 = (bf16[128,1024]{1,0:T(8,128)(2,1)S(1)}, bf16[128,1024]{1,0:T(8,128)(2,1)S(1)}, u32[]{:S(2)}, u32[]{:S(2)}) collective-permute-start(bf16[128,1024]{1,0:T(8,128)(2,1)S(1)} %collective-permute-done.13.near_ref), channel_id=1, source_target_pairs={{0,4},{2,30},{4,8},{6,2},{8,12},{10,6},{12,16},{14,10},{16,20},{18... | collective-permute-start | bytes 786440 | tf_op jit(solution)/shard_map/ppermute | solution.py:359
  66.7 5.5 %collective-permute-start.19 = (f32[8,128]{1,0:T(8,128)S(1)}, f32[8,128]{1,0:T(8,128)S(1)}, u32[]{:S(2)}, u32[]{:S(2)}) collective-permute-start(f32[8,128]{1,0:T(8,128)S(1)} %add_add_fusion.1), channel_id=1, source_target_pairs={{0,24},{2,26},{4,28},{6,30},{8,16},{10,18},{12,20},{14,22},{16,8},... | collective-permute-start | bytes 12296 | tf_op jit(solution)/shard_map/ppermute | solution.py:390
  69.7 4.5 %collective-permute-start.18 = (f32[8,128]{1,0:T(8,128)S(1)}, f32[8,128]{1,0:T(8,128)S(1)}, u32[]{:S(2)}, u32[]{:S(2)}) collective-permute-start(f32[8,128]{1,0:T(8,128)S(1)} %add_add_fusion.1), channel_id=1, source_target_pairs={{0,16},{2,18},{4,20},{6,22},{8,24},{10,26},{12,28},{14,30},{16,0},... | collective-permute-start | bytes 12296 | tf_op jit(solution)/shard_map/ppermute | solution.py:390
  69.7 4.5 %collective-permute-start.17 = (f32[8,128]{1,0:T(8,128)S(1)}, f32[8,128]{1,0:T(8,128)S(1)}, u32[]{:S(2)}, u32[]{:S(2)}) collective-permute-start(f32[8,128]{1,0:T(8,128)S(1)} %add_add_fusion.1), channel_id=1, source_target_pairs={{0,8},{2,10},{4,12},{6,14},{8,0},{10,2},{12,4},{14,6},{16,24},{18,... | collective-permute-start | bytes 12296 | tf_op jit(solution)/shard_map/ppermute | solution.py:390

commit v7 on v6

--- a/solution.py
+++ b/solution.py
@@ -275,13 +275,6 @@
         sum_ref[:, out] = known_ref[:, out] + 0.5 * (first + second)
 
 
-def finish_third_kernel(sum_ref, q_ref, rows3_ref):
-    width = rows3_ref.shape[1]
-    for at in range(0, sum_ref.shape[1], width):
-        out = slice(at, at + width)
-        rows3_ref[out, :] = (sum_ref[:, out] + 0.5 * q_ref[:, out].astype(F32)).T
-
-
 def ratio(above, below):
     return jnp.where(below == 0, 0.0, above / below)
 
@@ -321,7 +314,7 @@
 
 
 def combine_kernel(
-    shift_ref, moment_ref, targets_ref, k1_ref, k2_ref, k3_ref, solution_hbm, residual_hbm, held, sems
+    shift_ref, moment_ref, targets_ref, k1_ref, k2_ref, sum_ref, q_ref, solution_hbm, residual_hbm, held, sems
 ):
     width = moment_ref.shape[1]
     m = [moment_ref[i : i + 1, :] for i in range(6)]
@@ -331,7 +324,8 @@
     copies = []
     for part in range(assets // size):
         out = slice(part * size, (part + 1) * size)
-        k0, k1, k2, k3 = targets_ref[out, :], k1_ref[out, :], k2_ref[out, :], k3_ref[out, :]
+        k0, k1, k2 = targets_ref[out, :], k1_ref[out, :], k2_ref[out, :]
+        k3 = (sum_ref[:, out] + 0.5 * q_ref[:, out].astype(F32)).T
         held[0, out, :] = x[0] * k0 + x[1] * k1 + x[2] * k2
         held[1, out, :] = r[0] * k0 + r[1] * k1 + r[2] * k2 + r[3] * k3
         for i, target in enumerate((solution_hbm, residual_hbm)):
@@ -485,11 +479,10 @@
     moments = sum_over(moments, "asset")
     q2 = near(joined)
     partial = call(cross_third_kernel, field, (band, known, near2, far2))
-    rows3 = call(finish_third_kernel, out, (partial, q2))
     return call(
         combine_kernel,
         (out, out),
-        (shift, moments, targets, rows1, rows2, rows3),
+        (shift, moments, targets, rows1, rows2, partial, q2),
         scratch=[
             pltpu.VMEM((2, assets, cols), F32),
             pltpu.SemaphoreType.DMA((2, rows // 2)),

time: 76.8 us -> 76.6 us (level)
    pallas_call x19 -> x18, Pallas kernels: 15.1 us -> 14.9 us  [call(): pl.pallas_call(kernel, out_shape=out_shape, in_specs=specs, out_specs=jax...]
where the time goes in v7:
time: 76.6 us; the launch traced here: 76.5 us
  waiting for transfers between devices  31.1 us (41%)
  starting transfers between devices  28.4 us (37%)
  Pallas kernels  14.9 us (19%)
  local copies, waits for them, and re-layouts  1.17 us (2%)
  between operations  0.86 us (1%)
    pallas_call x18, Pallas kernels, call(): pl.pallas_call(kernel, out_shape=out_shape, in_specs=specs, out_specs=jax...  14.9 us
    ppermute x3, waiting for transfers between devices, sum_step(): lax.ppermute(value, axis, [(i, i ^ distance) for i in range(count)])  12.7 us
    ppermute x3, waiting for transfers between devices, forward(): lax.ppermute(value, 'asset', [(i, (i - 2 if i % 2 else i + 2) % count) fo...  9.81 us
    ppermute x6, starting transfers between devices, sum_over(): total = total + lax.ppermute(value, axis, route)  8 us
    ppermute x6, starting transfers between devices, near(): return lax.ppermute(value, 'asset', [(i, i ^ 1) for i in range(count)])  7.29 us
    ppermute x1, starting transfers between devices, far(): lax.ppermute(value, 'asset', [(i, (i + 1 if i % 2 else i - 1) % count) fo...  4.82 us
    ppermute x3, starting transfers between devices, sum_step(): lax.ppermute(value, axis, [(i, i ^ distance) for i in range(count)])  3.37 us
    ppermute x6, waiting for transfers between devices, sum_over(): total = total + lax.ppermute(value, axis, route)  3.14 us
  transfers between devices with their start and end apart: 22, of which 11 were waited for; matrix products, arithmetic and copies ran while one was open for 0% of the time, Pallas kernels for 14%

profile of v7, /device:TPU:0, one launch (start us, length us, event | category | flops | bytes accessed | tf_op | source)
XLA Modules:
  0.0 76.5 jit_solution(13131322488676751439)
XLA Ops:
  0.6 0.5 collective-permute-start
  1.2 1.1 %copy-done.1 = f32[1024,128]{1,0:T(8,128)S(1)} copy-done((f32[1024,128]{1,0:T(8,128)S(1)}, f32[1024,128]{1,0:T(8,128)}, u32[]{:S(2)}) %copy-start.1) | copy-done | bytes 524312
  2.3 0.2 shard_map.68
  2.5 2.6 %collective-permute-start.4 = (bf16[128,1024]{1,0:T(8,128)(2,1)S(1)}, bf16[128,1024]{1,0:T(8,128)(2,1)S(1)}, u32[]{:S(2)}, u32[]{:S(2)}) collective-permute-start(bf16[128,1024]{1,0:T(8,128)(2,1)S(1)} %get-tuple-element.46.v_ref), channel_id=1, source_target_pairs={{0,2},{2,0},{4,6},{6,4},{8,10},{10,8},{12,14},{14,12},{16,18},{18,... | collective-permute-start | bytes 786440 | tf_op jit(solution)/shard_map/ppermute | solution.py:341
  5.1 2.1 %shard_map.69 = (bf16[25,1024,128]{2,1,0:T(8,128)(2,1)S(1)}, f32[1,128]{1,0:T(1,128)S(1)}) custom-call(s32[8,16]{1,0:T(8,128)S(1)} %copy-done.4, s32[8]{0:T(128)S(1)} %copy-done.5, bf16[8,16,64,128]{3,2,1,0:T(8,128)(2,1)S(1)} %copy-done, f32[1,1024]{1,0:T(1,128)S(1)} %bitcast.1), custom_call_target="tpu_custom_call" | custom-call | tf_op jit(solution)/shard_map/pallas_call | solution.py:22
  7.2 0.0 collective-permute-done.part_ref
  7.2 1.2 %shard_map.70.band_ref = bf16[25,1024,128]{2,1,0:T(8,128)(2,1)S(1)} custom-call(s32[8,16]{1,0:T(8,128)S(1)} %copy-done.4, s32[8]{0:T(128)S(1)} %copy-done.5, bf16[8,16,64,128]{3,2,1,0:T(8,128)(2,1)S(1)} %collective-permute-done.part_ref, bf16[25,1024,128]{2,1,0:T(8,128)(2,1)S(1)} %get-tuple-element.42._), custom_call_target="tpu_custom_call", output_to_operand_aliasing={{}: (3, {})} | custom-call | tf_op jit(solution)/shard_map/pallas_call | solution.py:22
  8.5 0.5 shard_map.71
  9.1 4.8 %collective-permute-start.3 = (bf16[144,1024]{1,0:T(8,128)(2,1)S(1)}, bf16[144,1024]{1,0:T(8,128)(2,1)S(1)}, u32[]{:S(2)}, u32[]{:S(2)}) collective-permute-start(bf16[144,1024]{1,0:T(8,128)(2,1)S(1)} %get-tuple-element.49), channel_id=1, source_target_pairs={{0,30},{2,4},{4,2},{6,8},{8,6},{10,12},{12,10},{14,16},{16,14},{18... | collective-permute-start | bytes 884744 | tf_op jit(solution)/shard_map/ppermute | solution.py:346
  13.9 0.0 collective-permute-start.2
  13.9 1.1 %shard_map.72.local_ref.local0_ref = f32[128,1024]{1,0:T(8,128)S(1)} custom-call(bf16[25,1024,128]{2,1,0:T(8,128)(2,1)S(1)} %shard_map.70.band_ref, bf16[128,1024]{1,0:T(8,128)(2,1)S(1)} %get-tuple-element.46.v_ref), custom_call_target="tpu_custom_call" | custom-call | tf_op jit(solution)/shard_map/pallas_call | solution.py:22
  15.0 0.0 collective-permute-done.4.near_ref.near0_ref
  15.0 0.1 collective-permute-start.5
  15.1 1.3 %collective-permute-start.1 = (f32[1,128]{1,0:T(1,128)S(1)}, f32[1,128]{1,0:T(1,128)S(1)}, u32[]{:S(2)}, u32[]{:S(2)}) collective-permute-start(f32[1,128]{1,0:T(1,128)S(1)} %get-tuple-element.47), channel_id=1, source_target_pairs={{0,8},{2,10},{4,12},{6,14},{8,0},{10,2},{12,4},{14,6},{16,24},{18,... | collective-permute-start | bytes 1544 | tf_op jit(solution)/shard_map/ppermute | solution.py:374
  16.4 4.7 %collective-permute-done.1 = f32[1,128]{1,0:T(1,128)S(1)} collective-permute-done((f32[1,128]{1,0:T(1,128)S(1)}, f32[1,128]{1,0:T(1,128)S(1)}, u32[]{:S(2)}, u32[]{:S(2)}) %collective-permute-start.1) | collective-permute-done | bytes 544 | tf_op jit(solution)/shard_map/ppermute | solution.py:374
  21.1 2.2 %collective-permute-done.3.far_ref.qf0_ref = bf16[144,1024]{1,0:T(8,128)(2,1)S(1)} collective-permute-done((bf16[144,1024]{1,0:T(8,128)(2,1)S(1)}, bf16[144,1024]{1,0:T(8,128)(2,1)S(1)}, u32[]{:S(2)}, u32[]{:S(2)}) %collective-permute-start.3) | collective-permute-done | bytes 294944 | tf_op jit(solution)/shard_map/ppermute | solution.py:346
  23.3 2.1 %collective-permute-done.2.near_ref.qn0_ref = bf16[144,1024]{1,0:T(8,128)(2,1)S(1)} collective-permute-done((bf16[144,1024]{1,0:T(8,128)(2,1)S(1)}, bf16[144,1024]{1,0:T(8,128)(2,1)S(1)}, u32[]{:S(2)}, u32[]{:S(2)}) %collective-permute-start.2) | collective-permute-done | bytes 294944 | tf_op jit(solution)/shard_map/ppermute | solution.py:341
  25.4 0.1 shard_map.73
  25.5 1.9 %collective-permute-done.5.far_ref = bf16[128,1024]{1,0:T(8,128)(2,1)S(1)} collective-permute-done((bf16[128,1024]{1,0:T(8,128)(2,1)S(1)}, bf16[128,1024]{1,0:T(8,128)(2,1)S(1)}, u32[]{:S(2)}, u32[]{:S(2)}) %collective-permute-start.5) | collective-permute-done | bytes 262176 | tf_op jit(solution)/shard_map/ppermute | solution.py:353
  27.4 1.0 %shard_map.74 = (f32[128,1024]{1,0:T(8,128)S(1)}, bf16[128,1024]{1,0:T(8,128)(2,1)S(1)}, f32[128,1024]{1,0:T(8,128)S(1)}, f32[128,1024]{1,0:T(8,128)S(1)}) custom-call(bf16[25,1024,128]{2,1,0:T(8,128)(2,1)S(1)} %shard_map.70.band_ref, f32[128,1024]{1,0:T(8,128)S(1)} %get-tuple-element.50.sum_ref, f32[128,1024]{1,0:T(8,128)S(1)} %get-tuple-element.41.k_ref.k0_ref, ...), custom_call_target="tpu_custom_call" | custom-call | tf_op jit(solution)/shard_map/pallas_call | solution.py:22
  28.4 0.6 shard_map.77
  29.0 2.3 %collective-permute-start.8 = (bf16[144,1024]{1,0:T(8,128)(2,1)S(1)}, bf16[144,1024]{1,0:T(8,128)(2,1)S(1)}, u32[]{:S(2)}, u32[]{:S(2)}) collective-permute-start(bf16[144,1024]{1,0:T(8,128)(2,1)S(1)} %get-tuple-element.59), channel_id=1, source_target_pairs={{0,28},{2,6},{4,0},{6,10},{8,4},{10,14},{12,8},{14,18},{16,12},{18... | collective-permute-start | bytes 884744 | tf_op jit(solution)/shard_map/ppermute | solution.py:360
  31.3 0.0 collective-permute-start.6
  31.3 0.7 collective-permute-start.9
  31.9 4.9 %collective-permute-done.9 = f32[1,128]{1,0:T(1,128)S(1)} collective-permute-done((f32[1,128]{1,0:T(1,128)S(1)}, f32[1,128]{1,0:T(1,128)S(1)}, u32[]{:S(2)}, u32[]{:S(2)}) %collective-permute-start.9) | collective-permute-done | bytes 544 | tf_op jit(solution)/shard_map/ppermute | solution.py:374
  36.8 0.5 collective-permute-done.8.received_ref.r1_ref
  37.3 0.1 shard_map.78.own_ref
  37.5 3.3 %collective-permute-start.10 = (bf16[144,1024]{1,0:T(8,128)(2,1)S(1)}, bf16[144,1024]{1,0:T(8,128)(2,1)S(1)}, u32[]{:S(2)}, u32[]{:S(2)}) collective-permute-start(bf16[144,1024]{1,0:T(8,128)(2,1)S(1)} %shard_map.78.own_ref), channel_id=1, source_target_pairs={{0,2},{2,0},{4,6},{6,4},{8,10},{10,8},{12,14},{14,12},{16,18},{18,... | collective-permute-start | bytes 884744 | tf_op jit(solution)/shard_map/ppermute | solution.py:341
  40.7 0.0 collective-permute-done.6.near_ref.near1_ref
  40.7 0.0 collective-permute-start.7
  40.7 1.1 %shard_map.75.local_ref.local1_ref = f32[128,1024]{1,0:T(8,128)S(1)} custom-call(bf16[25,1024,128]{2,1,0:T(8,128)(2,1)S(1)} %shard_map.70.band_ref, bf16[128,1024]{1,0:T(8,128)(2,1)S(1)} %get-tuple-element.54.v_ref), custom_call_target="tpu_custom_call" | custom-call | tf_op jit(solution)/shard_map/pallas_call | solution.py:22
  41.9 7.9 %collective-permute-done.7.far_ref = bf16[128,1024]{1,0:T(8,128)(2,1)S(1)} collective-permute-done((bf16[128,1024]{1,0:T(8,128)(2,1)S(1)}, bf16[128,1024]{1,0:T(8,128)(2,1)S(1)}, u32[]{:S(2)}, u32[]{:S(2)}) %collective-permute-start.7) | collective-permute-done | bytes 262176 | tf_op jit(solution)/shard_map/ppermute | solution.py:353
  49.8 1.1 %shard_map.76 = (f32[128,1024]{1,0:T(8,128)S(1)}, f32[128,1024]{1,0:T(8,128)S(1)}, f32[128,1024]{1,0:T(8,128)S(1)}) custom-call(bf16[25,1024,128]{2,1,0:T(8,128)(2,1)S(1)} %shard_map.70.band_ref, f32[1,1024]{1,0:T(1,128)S(1)} %bitcast.4, f32[8,128]{1,0:T(8,128)S(1)} %get-tuple-element.51.mean_ref, f32[128,1024]{1,0:T(8,128)S(1)} %get-tuple-element.53.k_ref.k1_ref, ...), custom_call_target="tpu_custom_call" | custom-call | tf_op jit(solution)/shard_map/pallas_call | solution.py:22
  50.9 0.0 collective-permute-done.10.q_ref
  51.0 0.3 shard_map.79
  51.3 0.6 shard_map.80
  51.8 0.1 collective-permute-start.12
  51.9 1.1 %shard_map.81.local2_ref = f32[128,1024]{1,0:T(8,128)S(1)} custom-call(bf16[25,1024,128]{2,1,0:T(8,128)(2,1)S(1)} %shard_map.70.band_ref, bf16[128,1024]{1,0:T(8,128)(2,1)S(1)} %get-tuple-element.74.v_ref), custom_call_target="tpu_custom_call" | custom-call | flops 5000000000 | bytes 1048576 | tf_op jit(solution)/shard_map/pallas_call | solution.py:22
  53.0 0.1 collective-permute-start.13
  53.1 1.4 %collective-permute-start.11 = (f32[1,128]{1,0:T(1,128)S(1)}, f32[1,128]{1,0:T(1,128)S(1)}, u32[]{:S(2)}, u32[]{:S(2)}) collective-permute-start(f32[1,128]{1,0:T(1,128)S(1)} %get-tuple-element.62), channel_id=1, source_target_pairs={{0,16},{2,18},{4,20},{6,22},{8,24},{10,26},{12,28},{14,30},{16,0},... | collective-permute-start | bytes 1544 | tf_op jit(solution)/shard_map/ppermute | solution.py:374
  54.5 3.1 %collective-permute-done.11 = f32[1,128]{1,0:T(1,128)S(1)} collective-permute-done((f32[1,128]{1,0:T(1,128)S(1)}, f32[1,128]{1,0:T(1,128)S(1)}, u32[]{:S(2)}, u32[]{:S(2)}) %collective-permute-start.11) | collective-permute-done | bytes 544 | tf_op jit(solution)/shard_map/ppermute | solution.py:374
  57.6 1.2 %shard_map.82 = (f32[128,1024]{1,0:T(8,128)S(1)}, f32[1024,128]{1,0:T(8,128)S(1)}, f32[1024,128]{1,0:T(8,128)S(1)}, f32[8,128]{1,0:T(8,128)S(1)}, f32[128,1024]{1,0:T(8,128)S(1)}, /*index=5*/f32[128,1024]{1,0:T(8,128)S(1)}) custom-call(f32[1,128]{1,0:T(1,128)S(1)} %add_multiply_fusion.shift_ref, f32[8,128]{1,0:T(8,128)S(1)} %get-tuple-element.51.mean_ref, ...), custom_call_target="tpu_custom_call" | custom-call | tf_op jit(solution)/shard_map/pallas_call | solution.py:22
  58.9 0.0 copy-start.2
  58.9 0.0 collective-permute-done.12.received_ref
  58.9 0.6 collective-permute-done.13.near_ref
  59.5 0.2 shard_map.83
  59.7 2.8 %collective-permute-start.16 = (f32[8,128]{1,0:T(8,128)S(1)}, f32[8,128]{1,0:T(8,128)S(1)}, u32[]{:S(2)}, u32[]{:S(2)}) collective-permute-start(f32[8,128]{1,0:T(8,128)S(1)} %get-tuple-element.75), channel_id=1, source_target_pairs={{0,6},{2,4},{4,2},{6,0},{8,14},{10,12},{12,10},{14,8},{16,22},{18,... | collective-permute-start | bytes 12296 | tf_op jit(solution)/shard_map/ppermute | solution.py:384
  62.6 0.0 collective-permute-start.15
  62.6 0.7 collective-permute-start.14
  63.3 1.3 %collective-permute-start.21 = (bf16[128,1024]{1,0:T(8,128)(2,1)S(1)}, bf16[128,1024]{1,0:T(8,128)(2,1)S(1)}, u32[]{:S(2)}, u32[]{:S(2)}) collective-permute-start(bf16[128,1024]{1,0:T(8,128)(2,1)S(1)} %get-tuple-element.79), channel_id=1, source_target_pairs={{0,2},{2,0},{4,6},{6,4},{8,10},{10,8},{12,14},{14,12},{16,18},{18,... | collective-permute-start | bytes 786440 | tf_op jit(solution)/shard_map/ppermute | solution.py:341
  64.6 2.0 %collective-permute-start.20 = (bf16[128,1024]{1,0:T(8,128)(2,1)S(1)}, bf16[128,1024]{1,0:T(8,128)(2,1)S(1)}, u32[]{:S(2)}, u32[]{:S(2)}) collective-permute-start(bf16[128,1024]{1,0:T(8,128)(2,1)S(1)} %collective-permute-done.13.near_ref), channel_id=1, source_target_pairs={{0,4},{2,30},{4,8},{6,2},{8,12},{10,6},{12,16},{14,10},{16,20},{18... | collective-permute-start | bytes 786440 | tf_op jit(solution)/shard_map/ppermute | solution.py:353
  66.6 0.0 collective-permute-done.16
  66.6 0.0 collective-permute-done.15
  66.6 0.0 collective-permute-done.14
  66.7 3.1 %collective-permute-start.19 = (f32[8,128]{1,0:T(8,128)S(1)}, f32[8,128]{1,0:T(8,128)S(1)}, u32[]{:S(2)}, u32[]{:S(2)}) collective-permute-start(f32[8,128]{1,0:T(8,128)S(1)} %add_add_fusion.1), channel_id=1, source_target_pairs={{0,24},{2,26},{4,28},{6,30},{8,16},{10,18},{12,20},{14,22},{16,8},... | collective-permute-start | bytes 12296 | tf_op jit(solution)/shard_map/ppermute | solution.py:384
  69.7 0.0 collective-permute-start.18
  69.7 1.4 %collective-permute-start.17 = (f32[8,128]{1,0:T(8,128)S(1)}, f32[8,128]{1,0:T(8,128)S(1)}, u32[]{:S(2)}, u32[]{:S(2)}) collective-permute-start(f32[8,128]{1,0:T(8,128)S(1)} %add_add_fusion.1), channel_id=1, source_target_pairs={{0,8},{2,10},{4,12},{6,14},{8,0},{10,2},{12,4},{14,6},{16,24},{18,... | collective-permute-start | bytes 12296 | tf_op jit(solution)/shard_map/ppermute | solution.py:384
  71.1 1.0 %collective-permute-done.19 = f32[8,128]{1,0:T(8,128)S(1)} collective-permute-done((f32[8,128]{1,0:T(8,128)S(1)}, f32[8,128]{1,0:T(8,128)S(1)}, u32[]{:S(2)}, u32[]{:S(2)}) %collective-permute-start.19) | collective-permute-done | bytes 4128 | tf_op jit(solution)/shard_map/ppermute | solution.py:384
  72.1 2.1 %collective-permute-done.18 = f32[8,128]{1,0:T(8,128)S(1)} collective-permute-done((f32[8,128]{1,0:T(8,128)S(1)}, f32[8,128]{1,0:T(8,128)S(1)}, u32[]{:S(2)}, u32[]{:S(2)}) %collective-permute-start.18) | collective-permute-done | bytes 4128 | tf_op jit(solution)/shard_map/ppermute | solution.py:384
  74.2 0.0 collective-permute-done.17
  74.2 0.0 collective-permute-done.20.far_ref
  74.3 1.0 %shard_map.84.sum_ref = f32[128,1024]{1,0:T(8,128)S(1)} custom-call(bf16[25,1024,128]{2,1,0:T(8,128)(2,1)S(1)} %shard_map.70.band_ref, f32[128,1024]{1,0:T(8,128)S(1)} %get-tuple-element.78.known_ref, bf16[128,1024]{1,0:T(8,128)(2,1)S(1)} %collective-permute-done.13.near_ref, bf16[128,1024]{1,0:T(8,128)(2,1)S(1)} %collective-permute-done.20.far_ref), custom_call_target="tpu_custom_call" | custom-call | tf_op jit(solution)/shard_map/pallas_call | solution.py:22
  75.2 0.0 collective-permute-done.21.q_ref
  75.3 1.2 %shard_map.85 = (f32[1024,128]{1,0:T(8,128)}, f32[1024,128]{1,0:T(8,128)}) custom-call(f32[1,128]{1,0:T(1,128)S(1)} %add_multiply_fusion.shift_ref, f32[8,128]{1,0:T(8,128)S(1)} %add_add_fusion.moment_ref, f32[1024,128]{1,0:T(8,128)S(1)} %copy-done.2, f32[1024,128]{1,0:T(8,128)S(1)} %get-tuple-element.76.k1_ref, f32[1024,128]{1,0:T(8,128)S(1)} %get-tuple-element.77.k2_ref, ...), custom_call_target="tpu_custom_call" | custom-call | tf_op jit(solution)/shard_map/pallas_call | solution.py:22
  (15 shorter events, 0.0 us)
Async XLA Ops:
  0.6 4.5 %copy-start = (bf16[8,16,64,128]{3,2,1,0:T(8,128)(2,1)S(1)}, bf16[8,16,64,128]{3,2,1,0:T(8,128)(2,1)}, u32[]{:S(2)}) copy-start(bf16[8,16,64,128]{3,2,1,0:T(8,128)(2,1)} %part_ref.1) | copy-start | bytes 6291460
  0.6 6.6 %collective-permute-start = (bf16[8,16,64,128]{3,2,1,0:T(8,128)(2,1)}, bf16[8,16,64,128]{3,2,1,0:T(8,128)(2,1)S(1)}, u32[]{:S(2)}, u32[]{:S(2)}) collective-permute-start(bf16[8,16,64,128]{3,2,1,0:T(8,128)(2,1)} %part_ref.1), channel_id=1, source_target_pairs={{0,1},{1,0},{2,3},{3,2},{4,5},{5,4},{6,7},{7,6},{8,9},{9,8},{10,11... | collective-permute-start | bytes 6291464 | tf_op jit(solution)/shard_map/ppermute | solution.py:408
  1.2 1.1 %copy-start.1 = (f32[1024,128]{1,0:T(8,128)S(1)}, f32[1024,128]{1,0:T(8,128)}, u32[]{:S(2)}) copy-start(f32[1024,128]{1,0:T(8,128)} %targets_ref.3) | copy-start | bytes 1572868
  2.3 2.8 %copy-start.3 = (f32[1024]{0:T(1024)S(1)}, f32[1024]{0:T(1024)}, u32[]{:S(2)}) copy-start(f32[1024]{0:T(1024)} %param.6) | copy-start | bytes 12292
  2.3 2.8 %copy-start.4 = (s32[8,16]{1,0:T(8,128)S(1)}, s32[8,16]{1,0:T(8,128)}, u32[]{:S(2)}) copy-start(s32[8,16]{1,0:T(8,128)} %col_ref.3) | copy-start | bytes 1540
  2.3 2.8 %copy-start.5 = (s32[8]{0:T(128)S(1)}, s32[8]{0:T(128)}, u32[]{:S(2)}) copy-start(s32[8]{0:T(128)} %length_ref.3) | copy-start | bytes 100
  2.5 12.5 %collective-permute-start.4 = (bf16[128,1024]{1,0:T(8,128)(2,1)S(1)}, bf16[128,1024]{1,0:T(8,128)(2,1)S(1)}, u32[]{:S(2)}, u32[]{:S(2)}) collective-permute-start(bf16[128,1024]{1,0:T(8,128)(2,1)S(1)} %get-tuple-element.46.v_ref), channel_id=1, source_target_pairs={{0,2},{2,0},{4,6},{6,4},{8,10},{10,8},{12,14},{14,12},{16,18},{18,... | collective-permute-start | bytes 786440 | tf_op jit(solution)/shard_map/ppermute | solution.py:341
  9.1 14.3 %collective-permute-start.3 = (bf16[144,1024]{1,0:T(8,128)(2,1)S(1)}, bf16[144,1024]{1,0:T(8,128)(2,1)S(1)}, u32[]{:S(2)}, u32[]{:S(2)}) collective-permute-start(bf16[144,1024]{1,0:T(8,128)(2,1)S(1)} %get-tuple-element.49), channel_id=1, source_target_pairs={{0,30},{2,4},{4,2},{6,8},{8,6},{10,12},{12,10},{14,16},{16,14},{18... | collective-permute-start | bytes 884744 | tf_op jit(solution)/shard_map/ppermute | solution.py:346
  13.9 11.5 %collective-permute-start.2 = (bf16[144,1024]{1,0:T(8,128)(2,1)S(1)}, bf16[144,1024]{1,0:T(8,128)(2,1)S(1)}, u32[]{:S(2)}, u32[]{:S(2)}) collective-permute-start(bf16[144,1024]{1,0:T(8,128)(2,1)S(1)} %get-tuple-element.45.own_ref), channel_id=1, source_target_pairs={{0,2},{2,0},{4,6},{6,4},{8,10},{10,8},{12,14},{14,12},{16,18},{18,... | collective-permute-start | bytes 884744 | tf_op jit(solution)/shard_map/ppermute | solution.py:341
  15.0 12.4 %collective-permute-start.5 = (bf16[128,1024]{1,0:T(8,128)(2,1)S(1)}, bf16[128,1024]{1,0:T(8,128)(2,1)S(1)}, u32[]{:S(2)}, u32[]{:S(2)}) collective-permute-start(bf16[128,1024]{1,0:T(8,128)(2,1)S(1)} %collective-permute-done.4.near_ref.near0_ref), channel_id=1, source_target_pairs={{0,4},{2,30},{4,8},{6,2},{8,12},{10,6},{12,16},{14,10},{16,20},{18... | collective-permute-start | bytes 786440 | tf_op jit(solution)/shard_map/ppermute | solution.py:353
  15.1 6.0 %collective-permute-start.1 = (f32[1,128]{1,0:T(1,128)S(1)}, f32[1,128]{1,0:T(1,128)S(1)}, u32[]{:S(2)}, u32[]{:S(2)}) collective-permute-start(f32[1,128]{1,0:T(1,128)S(1)} %get-tuple-element.47), channel_id=1, source_target_pairs={{0,8},{2,10},{4,12},{6,14},{8,0},{10,2},{12,4},{14,6},{16,24},{18,... | collective-permute-start | bytes 1544 | tf_op jit(solution)/shard_map/ppermute | solution.py:374
  29.0 8.4 %collective-permute-start.8 = (bf16[144,1024]{1,0:T(8,128)(2,1)S(1)}, bf16[144,1024]{1,0:T(8,128)(2,1)S(1)}, u32[]{:S(2)}, u32[]{:S(2)}) collective-permute-start(bf16[144,1024]{1,0:T(8,128)(2,1)S(1)} %get-tuple-element.59), channel_id=1, source_target_pairs={{0,28},{2,6},{4,0},{6,10},{8,4},{10,14},{12,8},{14,18},{16,12},{18... | collective-permute-start | bytes 884744 | tf_op jit(solution)/shard_map/ppermute | solution.py:360
  31.3 9.5 %collective-permute-start.6 = (bf16[128,1024]{1,0:T(8,128)(2,1)S(1)}, bf16[128,1024]{1,0:T(8,128)(2,1)S(1)}, u32[]{:S(2)}, u32[]{:S(2)}) collective-permute-start(bf16[128,1024]{1,0:T(8,128)(2,1)S(1)} %get-tuple-element.54.v_ref), channel_id=1, source_target_pairs={{0,2},{2,0},{4,6},{6,4},{8,10},{10,8},{12,14},{14,12},{16,18},{18,... | collective-permute-start | bytes 786440 | tf_op jit(solution)/shard_map/ppermute | solution.py:341
  31.3 5.6 %collective-permute-start.9 = (f32[1,128]{1,0:T(1,128)S(1)}, f32[1,128]{1,0:T(1,128)S(1)}, u32[]{:S(2)}, u32[]{:S(2)}) collective-permute-start(f32[1,128]{1,0:T(1,128)S(1)} %add.27), channel_id=1, source_target_pairs={{0,4},{2,6},{4,0},{6,2},{8,12},{10,14},{12,8},{14,10},{16,20},{18,... | collective-permute-start | bytes 1544 | tf_op jit(solution)/shard_map/ppermute | solution.py:374
  37.5 13.5 %collective-permute-start.10 = (bf16[144,1024]{1,0:T(8,128)(2,1)S(1)}, bf16[144,1024]{1,0:T(8,128)(2,1)S(1)}, u32[]{:S(2)}, u32[]{:S(2)}) collective-permute-start(bf16[144,1024]{1,0:T(8,128)(2,1)S(1)} %shard_map.78.own_ref), channel_id=1, source_target_pairs={{0,2},{2,0},{4,6},{6,4},{8,10},{10,8},{12,14},{14,12},{16,18},{18,... | collective-permute-start | bytes 884744 | tf_op jit(solution)/shard_map/ppermute | solution.py:341
  40.7 9.1 %collective-permute-start.7 = (bf16[128,1024]{1,0:T(8,128)(2,1)S(1)}, bf16[128,1024]{1,0:T(8,128)(2,1)S(1)}, u32[]{:S(2)}, u32[]{:S(2)}) collective-permute-start(bf16[128,1024]{1,0:T(8,128)(2,1)S(1)} %collective-permute-done.6.near_ref.near1_ref), channel_id=1, source_target_pairs={{0,4},{2,30},{4,8},{6,2},{8,12},{10,6},{12,16},{14,10},{16,20},{18... | collective-permute-start | bytes 786440 | tf_op jit(solution)/shard_map/ppermute | solution.py:353
  51.8 7.0 %collective-permute-start.12 = (bf16[128,1024]{1,0:T(8,128)(2,1)S(1)}, bf16[128,1024]{1,0:T(8,128)(2,1)S(1)}, u32[]{:S(2)}, u32[]{:S(2)}) collective-permute-start(bf16[128,1024]{1,0:T(8,128)(2,1)S(1)} %get-tuple-element.73), channel_id=1, source_target_pairs={{0,28},{2,6},{4,0},{6,10},{8,4},{10,14},{12,8},{14,18},{16,12},{18... | collective-permute-start | bytes 786440 | tf_op jit(solution)/shard_map/ppermute | solution.py:360
  53.0 6.5 %collective-permute-start.13 = (bf16[128,1024]{1,0:T(8,128)(2,1)S(1)}, bf16[128,1024]{1,0:T(8,128)(2,1)S(1)}, u32[]{:S(2)}, u32[]{:S(2)}) collective-permute-start(bf16[128,1024]{1,0:T(8,128)(2,1)S(1)} %get-tuple-element.74.v_ref), channel_id=1, source_target_pairs={{0,2},{2,0},{4,6},{6,4},{8,10},{10,8},{12,14},{14,12},{16,18},{18,... | collective-permute-start | bytes 786440 | tf_op jit(solution)/shard_map/ppermute | solution.py:341
  53.1 4.5 %collective-permute-start.11 = (f32[1,128]{1,0:T(1,128)S(1)}, f32[1,128]{1,0:T(1,128)S(1)}, u32[]{:S(2)}, u32[]{:S(2)}) collective-permute-start(f32[1,128]{1,0:T(1,128)S(1)} %get-tuple-element.62), channel_id=1, source_target_pairs={{0,16},{2,18},{4,20},{6,22},{8,24},{10,26},{12,28},{14,30},{16,0},... | collective-permute-start | bytes 1544 | tf_op jit(solution)/shard_map/ppermute | solution.py:374
  58.9 16.4 %copy-start.2 = (f32[1024,128]{1,0:T(8,128)S(1)}, f32[1024,128]{1,0:T(8,128)}, u32[]{:S(2)}) copy-start(f32[1024,128]{1,0:T(8,128)} %targets_ref.3) | copy-start | bytes 1572868
  59.7 6.9 %collective-permute-start.16 = (f32[8,128]{1,0:T(8,128)S(1)}, f32[8,128]{1,0:T(8,128)S(1)}, u32[]{:S(2)}, u32[]{:S(2)}) collective-permute-start(f32[8,128]{1,0:T(8,128)S(1)} %get-tuple-element.75), channel_id=1, source_target_pairs={{0,6},{2,4},{4,2},{6,0},{8,14},{10,12},{12,10},{14,8},{16,22},{18,... | collective-permute-start | bytes 12296 | tf_op jit(solution)/shard_map/ppermute | solution.py:384
  62.6 4.1 %collective-permute-start.15 = (f32[8,128]{1,0:T(8,128)S(1)}, f32[8,128]{1,0:T(8,128)S(1)}, u32[]{:S(2)}, u32[]{:S(2)}) collective-permute-start(f32[8,128]{1,0:T(8,128)S(1)} %get-tuple-element.75), channel_id=1, source_target_pairs={{0,4},{2,6},{4,0},{6,2},{8,12},{10,14},{12,8},{14,10},{16,20},{18,... | collective-permute-start | bytes 12296 | tf_op jit(solution)/shard_map/ppermute | solution.py:384
  62.6 4.1 %collective-permute-start.14 = (f32[8,128]{1,0:T(8,128)S(1)}, f32[8,128]{1,0:T(8,128)S(1)}, u32[]{:S(2)}, u32[]{:S(2)}) collective-permute-start(f32[8,128]{1,0:T(8,128)S(1)} %get-tuple-element.75), channel_id=1, source_target_pairs={{0,2},{2,0},{4,6},{6,4},{8,10},{10,8},{12,14},{14,12},{16,18},{18,... | collective-permute-start | bytes 12296 | tf_op jit(solution)/shard_map/ppermute | solution.py:384
  63.3 12.0 %collective-permute-start.21 = (bf16[128,1024]{1,0:T(8,128)(2,1)S(1)}, bf16[128,1024]{1,0:T(8,128)(2,1)S(1)}, u32[]{:S(2)}, u32[]{:S(2)}) collective-permute-start(bf16[128,1024]{1,0:T(8,128)(2,1)S(1)} %get-tuple-element.79), channel_id=1, source_target_pairs={{0,2},{2,0},{4,6},{6,4},{8,10},{10,8},{12,14},{14,12},{16,18},{18,... | collective-permute-start | bytes 786440 | tf_op jit(solution)/shard_map/ppermute | solution.py:341
  64.6 9.6 %collective-permute-start.20 = (bf16[128,1024]{1,0:T(8,128)(2,1)S(1)}, bf16[128,1024]{1,0:T(8,128)(2,1)S(1)}, u32[]{:S(2)}, u32[]{:S(2)}) collective-permute-start(bf16[128,1024]{1,0:T(8,128)(2,1)S(1)} %collective-permute-done.13.near_ref), channel_id=1, source_target_pairs={{0,4},{2,30},{4,8},{6,2},{8,12},{10,6},{12,16},{14,10},{16,20},{18... | collective-permute-start | bytes 786440 | tf_op jit(solution)/shard_map/ppermute | solution.py:353
  66.7 5.5 %collective-permute-start.19 = (f32[8,128]{1,0:T(8,128)S(1)}, f32[8,128]{1,0:T(8,128)S(1)}, u32[]{:S(2)}, u32[]{:S(2)}) collective-permute-start(f32[8,128]{1,0:T(8,128)S(1)} %add_add_fusion.1), channel_id=1, source_target_pairs={{0,24},{2,26},{4,28},{6,30},{8,16},{10,18},{12,20},{14,22},{16,8},... | collective-permute-start | bytes 12296 | tf_op jit(solution)/shard_map/ppermute | solution.py:384
  69.7 4.5 %collective-permute-start.18 = (f32[8,128]{1,0:T(8,128)S(1)}, f32[8,128]{1,0:T(8,128)S(1)}, u32[]{:S(2)}, u32[]{:S(2)}) collective-permute-start(f32[8,128]{1,0:T(8,128)S(1)} %add_add_fusion.1), channel_id=1, source_target_pairs={{0,16},{2,18},{4,20},{6,22},{8,24},{10,26},{12,28},{14,30},{16,0},... | collective-permute-start | bytes 12296 | tf_op jit(solution)/shard_map/ppermute | solution.py:384
  69.7 4.5 %collective-permute-start.17 = (f32[8,128]{1,0:T(8,128)S(1)}, f32[8,128]{1,0:T(8,128)S(1)}, u32[]{:S(2)}, u32[]{:S(2)}) collective-permute-start(f32[8,128]{1,0:T(8,128)S(1)} %add_add_fusion.1), channel_id=1, source_target_pairs={{0,8},{2,10},{4,12},{6,14},{8,0},{10,2},{12,4},{14,6},{16,24},{18,... | collective-permute-start | bytes 12296 | tf_op jit(solution)/shard_map/ppermute | solution.py:384

commit v8 on v7

--- a/solution.py
+++ b/solution.py
@@ -268,13 +268,6 @@
     moment_ref[5:6, :] = share_ref[5:6, :] + jnp.sum(total.T, axis=0, keepdims=True)
 
 
-def cross_third_kernel(band_ref, known_ref, near_ref, far_ref, sum_ref):
-    before, after = neighbours(near_ref, far_ref, known_ref.shape[0])
-    for j in range(0, band_ref.shape[0] // 3, 2):
-        out, first, second = forward_products(band_ref, before, after, j)
-        sum_ref[:, out] = known_ref[:, out] + 0.5 * (first + second)
-
-
 def ratio(above, below):
     return jnp.where(below == 0, 0.0, above / below)
 
@@ -314,24 +307,33 @@
 
 
 def combine_kernel(
-    shift_ref, moment_ref, targets_ref, k1_ref, k2_ref, sum_ref, q_ref, solution_hbm, residual_hbm, held, sems
+    shift_ref, moment_ref, targets_ref, k1_ref, k2_ref, band_ref, known_ref, near_ref, far_ref, q_ref,
+    solution_hbm, residual_hbm, held, sems
 ):
-    width = moment_ref.shape[1]
+    cols, width = known_ref.shape[0], moment_ref.shape[1]
     m = [moment_ref[i : i + 1, :] for i in range(6)]
-    x, r = scalars(m, shift_ref[...], 3)
-    assets = targets_ref.shape[0]
+    x, r = scalars(m, shift_ref[0:1, :], 3)
     size = 2 * width
+    parts = range(targets_ref.shape[0] // size)
     copies = []
-    for part in range(assets // size):
+
+    def leave(kind, target, part, out):
+        copy = pltpu.make_async_copy(held.at[kind, out, :], target.at[out, :], sems.at[kind, part])
+        copy.start()
+        copies.append(copy)
+
+    for part in parts:
         out = slice(part * size, (part + 1) * size)
         k0, k1, k2 = targets_ref[out, :], k1_ref[out, :], k2_ref[out, :]
-        k3 = (sum_ref[:, out] + 0.5 * q_ref[:, out].astype(F32)).T
         held[0, out, :] = x[0] * k0 + x[1] * k1 + x[2] * k2
+        leave(0, solution_hbm, part, out)
+    before, after = neighbours(near_ref, far_ref, cols)
+    for part in parts:
+        out, first, second = forward_products(band_ref, before, after, 2 * part)
+        k3 = (known_ref[:, out] + 0.5 * (first + second + q_ref[:, out].astype(F32))).T
+        k0, k1, k2 = targets_ref[out, :], k1_ref[out, :], k2_ref[out, :]
         held[1, out, :] = r[0] * k0 + r[1] * k1 + r[2] * k2 + r[3] * k3
-        for i, target in enumerate((solution_hbm, residual_hbm)):
-            copy = pltpu.make_async_copy(held.at[i, out, :], target.at[out, :], sems.at[i, part])
-            copy.start()
-            copies.append(copy)
+        leave(1, residual_hbm, part, out)
     for copy in copies:
         copy.wait()
 
@@ -478,11 +480,10 @@
     )
     moments = sum_over(moments, "asset")
     q2 = near(joined)
-    partial = call(cross_third_kernel, field, (band, known, near2, far2))
     return call(
         combine_kernel,
         (out, out),
-        (shift, moments, targets, rows1, rows2, partial, q2),
+        (shift, moments, targets, rows1, rows2, band, known, near2, far2, q2),
         scratch=[
             pltpu.VMEM((2, assets, cols), F32),
             pltpu.SemaphoreType.DMA((2, rows // 2)),

time: 76.6 us -> 76.4 us (level)
    pallas_call x18 -> x17, Pallas kernels: 14.9 us -> 14.7 us  [call(): pl.pallas_call(kernel, out_shape=out_shape, in_specs=specs, out_specs=jax...]
  transfers between devices with their start and end apart: 22 -> 22, of which waited for: 11 -> 11; matrix products, arithmetic and copies ran while one was open for 0% -> 0% of each run, Pallas kernels for 14% -> 13%
where the time goes in v8:
time: 76.4 us; the launch traced here: 76.2 us
  waiting for transfers between devices  31.2 us (41%)
  starting transfers between devices  28.3 us (37%)
  Pallas kernels  14.7 us (19%)
  local copies, waits for them, and re-layouts  1.17 us (2%)
  between operations  0.85 us (1%)
    pallas_call x17, Pallas kernels, call(): pl.pallas_call(kernel, out_shape=out_shape, in_specs=specs, out_specs=jax...  14.7 us
    ppermute x3, waiting for transfers between devices, sum_step(): lax.ppermute(value, axis, [(i, i ^ distance) for i in range(count)])  12.8 us
    ppermute x3, waiting for transfers between devices, forward(): lax.ppermute(value, 'asset', [(i, (i - 2 if i % 2 else i + 2) % count) fo...  9.81 us
    ppermute x6, starting transfers between devices, sum_over(): total = total + lax.ppermute(value, axis, route)  8 us
    ppermute x6, starting transfers between devices, near(): return lax.ppermute(value, 'asset', [(i, i ^ 1) for i in range(count)])  7.28 us
    ppermute x1, starting transfers between devices, far(): lax.ppermute(value, 'asset', [(i, (i + 1 if i % 2 else i - 1) % count) fo...  4.82 us
    ppermute x3, starting transfers between devices, sum_step(): lax.ppermute(value, axis, [(i, i ^ distance) for i in range(count)])  3.31 us
    ppermute x6, waiting for transfers between devices, sum_over(): total = total + lax.ppermute(value, axis, route)  3.13 us
  transfers between devices with their start and end apart: 22, of which 11 were waited for; matrix products, arithmetic and copies ran while one was open for 0% of the time, Pallas kernels for 13%

profile of v8, /device:TPU:0, one launch (start us, length us, event | category | flops | bytes accessed | tf_op | source)
XLA Modules:
  0.0 76.2 jit_solution(8603978504536510305)
XLA Ops:
  0.6 0.5 collective-permute-start
  1.2 1.1 %copy-done.1 = f32[1024,128]{1,0:T(8,128)S(1)} copy-done((f32[1024,128]{1,0:T(8,128)S(1)}, f32[1024,128]{1,0:T(8,128)}, u32[]{:S(2)}) %copy-start.1) | copy-done | bytes 524312
  2.3 0.2 shard_map.68
  2.5 2.6 %collective-permute-start.4 = (bf16[128,1024]{1,0:T(8,128)(2,1)S(1)}, bf16[128,1024]{1,0:T(8,128)(2,1)S(1)}, u32[]{:S(2)}, u32[]{:S(2)}) collective-permute-start(bf16[128,1024]{1,0:T(8,128)(2,1)S(1)} %get-tuple-element.46.v_ref), channel_id=1, source_target_pairs={{0,2},{2,0},{4,6},{6,4},{8,10},{10,8},{12,14},{14,12},{16,18},{18,... | collective-permute-start | bytes 786440 | tf_op jit(solution)/shard_map/ppermute | solution.py:343
  5.1 0.0 copy-done.3
  5.1 2.1 %shard_map.69 = (bf16[25,1024,128]{2,1,0:T(8,128)(2,1)S(1)}, f32[1,128]{1,0:T(1,128)S(1)}) custom-call(s32[8,16]{1,0:T(8,128)S(1)} %copy-done.4, s32[8]{0:T(128)S(1)} %copy-done.5, bf16[8,16,64,128]{3,2,1,0:T(8,128)(2,1)S(1)} %copy-done, f32[1,1024]{1,0:T(1,128)S(1)} %bitcast.1), custom_call_target="tpu_custom_call" | custom-call | tf_op jit(solution)/shard_map/pallas_call | solution.py:22
  7.2 0.0 collective-permute-done.part_ref
  7.2 1.2 %shard_map.70.band_ref = bf16[25,1024,128]{2,1,0:T(8,128)(2,1)S(1)} custom-call(s32[8,16]{1,0:T(8,128)S(1)} %copy-done.4, s32[8]{0:T(128)S(1)} %copy-done.5, bf16[8,16,64,128]{3,2,1,0:T(8,128)(2,1)S(1)} %collective-permute-done.part_ref, bf16[25,1024,128]{2,1,0:T(8,128)(2,1)S(1)} %get-tuple-element.42._), custom_call_target="tpu_custom_call", output_to_operand_aliasing={{}: (3, {})} | custom-call | tf_op jit(solution)/shard_map/pallas_call | solution.py:22
  8.5 0.5 shard_map.71
  9.1 4.8 %collective-permute-start.3 = (bf16[144,1024]{1,0:T(8,128)(2,1)S(1)}, bf16[144,1024]{1,0:T(8,128)(2,1)S(1)}, u32[]{:S(2)}, u32[]{:S(2)}) collective-permute-start(bf16[144,1024]{1,0:T(8,128)(2,1)S(1)} %get-tuple-element.49), channel_id=1, source_target_pairs={{0,30},{2,4},{4,2},{6,8},{8,6},{10,12},{12,10},{14,16},{16,14},{18... | collective-permute-start | bytes 884744 | tf_op jit(solution)/shard_map/ppermute | solution.py:348
  13.9 0.0 collective-permute-start.2
  13.9 1.1 %shard_map.72.local_ref.local0_ref = f32[128,1024]{1,0:T(8,128)S(1)} custom-call(bf16[25,1024,128]{2,1,0:T(8,128)(2,1)S(1)} %shard_map.70.band_ref, bf16[128,1024]{1,0:T(8,128)(2,1)S(1)} %get-tuple-element.46.v_ref), custom_call_target="tpu_custom_call" | custom-call | tf_op jit(solution)/shard_map/pallas_call | solution.py:22
  15.0 0.0 collective-permute-done.4.near_ref.near0_ref
  15.0 0.1 collective-permute-start.5
  15.1 1.3 %collective-permute-start.1 = (f32[1,128]{1,0:T(1,128)S(1)}, f32[1,128]{1,0:T(1,128)S(1)}, u32[]{:S(2)}, u32[]{:S(2)}) collective-permute-start(f32[1,128]{1,0:T(1,128)S(1)} %get-tuple-element.47), channel_id=1, source_target_pairs={{0,8},{2,10},{4,12},{6,14},{8,0},{10,2},{12,4},{14,6},{16,24},{18,... | collective-permute-start | bytes 1544 | tf_op jit(solution)/shard_map/ppermute | solution.py:376
  16.4 4.7 %collective-permute-done.1 = f32[1,128]{1,0:T(1,128)S(1)} collective-permute-done((f32[1,128]{1,0:T(1,128)S(1)}, f32[1,128]{1,0:T(1,128)S(1)}, u32[]{:S(2)}, u32[]{:S(2)}) %collective-permute-start.1) | collective-permute-done | bytes 544 | tf_op jit(solution)/shard_map/ppermute | solution.py:376
  21.1 2.2 %collective-permute-done.3.far_ref.qf0_ref = bf16[144,1024]{1,0:T(8,128)(2,1)S(1)} collective-permute-done((bf16[144,1024]{1,0:T(8,128)(2,1)S(1)}, bf16[144,1024]{1,0:T(8,128)(2,1)S(1)}, u32[]{:S(2)}, u32[]{:S(2)}) %collective-permute-start.3) | collective-permute-done | bytes 294944 | tf_op jit(solution)/shard_map/ppermute | solution.py:348
  23.3 2.1 %collective-permute-done.2.near_ref.qn0_ref = bf16[144,1024]{1,0:T(8,128)(2,1)S(1)} collective-permute-done((bf16[144,1024]{1,0:T(8,128)(2,1)S(1)}, bf16[144,1024]{1,0:T(8,128)(2,1)S(1)}, u32[]{:S(2)}, u32[]{:S(2)}) %collective-permute-start.2) | collective-permute-done | bytes 294944 | tf_op jit(solution)/shard_map/ppermute | solution.py:343
  25.4 0.1 shard_map.73
  25.5 1.9 %collective-permute-done.5.far_ref = bf16[128,1024]{1,0:T(8,128)(2,1)S(1)} collective-permute-done((bf16[128,1024]{1,0:T(8,128)(2,1)S(1)}, bf16[128,1024]{1,0:T(8,128)(2,1)S(1)}, u32[]{:S(2)}, u32[]{:S(2)}) %collective-permute-start.5) | collective-permute-done | bytes 262176 | tf_op jit(solution)/shard_map/ppermute | solution.py:355
  27.4 1.0 %shard_map.74 = (f32[128,1024]{1,0:T(8,128)S(1)}, bf16[128,1024]{1,0:T(8,128)(2,1)S(1)}, f32[128,1024]{1,0:T(8,128)S(1)}, f32[128,1024]{1,0:T(8,128)S(1)}) custom-call(bf16[25,1024,128]{2,1,0:T(8,128)(2,1)S(1)} %shard_map.70.band_ref, f32[128,1024]{1,0:T(8,128)S(1)} %get-tuple-element.50.sum_ref, f32[128,1024]{1,0:T(8,128)S(1)} %get-tuple-element.41.k_ref.k0_ref, ...), custom_call_target="tpu_custom_call" | custom-call | tf_op jit(solution)/shard_map/pallas_call | solution.py:22
  28.4 0.6 shard_map.77
  29.0 2.3 %collective-permute-start.8 = (bf16[144,1024]{1,0:T(8,128)(2,1)S(1)}, bf16[144,1024]{1,0:T(8,128)(2,1)S(1)}, u32[]{:S(2)}, u32[]{:S(2)}) collective-permute-start(bf16[144,1024]{1,0:T(8,128)(2,1)S(1)} %get-tuple-element.59), channel_id=1, source_target_pairs={{0,28},{2,6},{4,0},{6,10},{8,4},{10,14},{12,8},{14,18},{16,12},{18... | collective-permute-start | bytes 884744 | tf_op jit(solution)/shard_map/ppermute | solution.py:362
  31.3 0.0 collective-permute-start.6
  31.3 0.7 collective-permute-start.9
  31.9 4.9 %collective-permute-done.9 = f32[1,128]{1,0:T(1,128)S(1)} collective-permute-done((f32[1,128]{1,0:T(1,128)S(1)}, f32[1,128]{1,0:T(1,128)S(1)}, u32[]{:S(2)}, u32[]{:S(2)}) %collective-permute-start.9) | collective-permute-done | bytes 544 | tf_op jit(solution)/shard_map/ppermute | solution.py:376
  36.8 0.5 collective-permute-done.8.received_ref.r1_ref
  37.3 0.1 shard_map.78.own_ref
  37.5 3.3 %collective-permute-start.10 = (bf16[144,1024]{1,0:T(8,128)(2,1)S(1)}, bf16[144,1024]{1,0:T(8,128)(2,1)S(1)}, u32[]{:S(2)}, u32[]{:S(2)}) collective-permute-start(bf16[144,1024]{1,0:T(8,128)(2,1)S(1)} %shard_map.78.own_ref), channel_id=1, source_target_pairs={{0,2},{2,0},{4,6},{6,4},{8,10},{10,8},{12,14},{14,12},{16,18},{18,... | collective-permute-start | bytes 884744 | tf_op jit(solution)/shard_map/ppermute | solution.py:343
  40.7 0.0 collective-permute-done.6.near_ref.near1_ref
  40.7 0.0 collective-permute-start.7
  40.7 1.1 %shard_map.75.local_ref.local1_ref = f32[128,1024]{1,0:T(8,128)S(1)} custom-call(bf16[25,1024,128]{2,1,0:T(8,128)(2,1)S(1)} %shard_map.70.band_ref, bf16[128,1024]{1,0:T(8,128)(2,1)S(1)} %get-tuple-element.54.v_ref), custom_call_target="tpu_custom_call" | custom-call | tf_op jit(solution)/shard_map/pallas_call | solution.py:22
  41.9 7.9 %collective-permute-done.7.far_ref = bf16[128,1024]{1,0:T(8,128)(2,1)S(1)} collective-permute-done((bf16[128,1024]{1,0:T(8,128)(2,1)S(1)}, bf16[128,1024]{1,0:T(8,128)(2,1)S(1)}, u32[]{:S(2)}, u32[]{:S(2)}) %collective-permute-start.7) | collective-permute-done | bytes 262176 | tf_op jit(solution)/shard_map/ppermute | solution.py:355
  49.8 1.1 %shard_map.76 = (f32[128,1024]{1,0:T(8,128)S(1)}, f32[128,1024]{1,0:T(8,128)S(1)}, f32[128,1024]{1,0:T(8,128)S(1)}) custom-call(bf16[25,1024,128]{2,1,0:T(8,128)(2,1)S(1)} %shard_map.70.band_ref, f32[1,1024]{1,0:T(1,128)S(1)} %bitcast.4, f32[8,128]{1,0:T(8,128)S(1)} %get-tuple-element.51.mean_ref, f32[128,1024]{1,0:T(8,128)S(1)} %get-tuple-element.53.k_ref.k1_ref, ...), custom_call_target="tpu_custom_call" | custom-call | tf_op jit(solution)/shard_map/pallas_call | solution.py:22
  50.9 0.0 collective-permute-done.10.q_ref
  51.0 0.3 shard_map.79
  51.3 0.6 shard_map.80
  51.8 0.1 collective-permute-start.12
  51.9 1.1 %shard_map.81.local2_ref = f32[128,1024]{1,0:T(8,128)S(1)} custom-call(bf16[25,1024,128]{2,1,0:T(8,128)(2,1)S(1)} %shard_map.70.band_ref, bf16[128,1024]{1,0:T(8,128)(2,1)S(1)} %get-tuple-element.74.v_ref), custom_call_target="tpu_custom_call" | custom-call | flops 5000000000 | bytes 1048576 | tf_op jit(solution)/shard_map/pallas_call | solution.py:22
  53.0 0.0 copy-start.2
  53.0 0.1 collective-permute-start.13
  53.1 1.4 %collective-permute-start.11 = (f32[1,128]{1,0:T(1,128)S(1)}, f32[1,128]{1,0:T(1,128)S(1)}, u32[]{:S(2)}, u32[]{:S(2)}) collective-permute-start(f32[1,128]{1,0:T(1,128)S(1)} %get-tuple-element.62), channel_id=1, source_target_pairs={{0,16},{2,18},{4,20},{6,22},{8,24},{10,26},{12,28},{14,30},{16,0},... | collective-permute-start | bytes 1544 | tf_op jit(solution)/shard_map/ppermute | solution.py:376
  54.5 3.1 %collective-permute-done.11 = f32[1,128]{1,0:T(1,128)S(1)} collective-permute-done((f32[1,128]{1,0:T(1,128)S(1)}, f32[1,128]{1,0:T(1,128)S(1)}, u32[]{:S(2)}, u32[]{:S(2)}) %collective-permute-start.11) | collective-permute-done | bytes 544 | tf_op jit(solution)/shard_map/ppermute | solution.py:376
  57.6 1.2 %shard_map.82 = (f32[128,1024]{1,0:T(8,128)S(1)}, f32[1024,128]{1,0:T(8,128)S(1)}, f32[1024,128]{1,0:T(8,128)S(1)}, f32[8,128]{1,0:T(8,128)S(1)}, f32[128,1024]{1,0:T(8,128)S(1)}, /*index=5*/f32[128,1024]{1,0:T(8,128)S(1)}) custom-call(f32[1,128]{1,0:T(1,128)S(1)} %add_multiply_fusion.shift_ref, f32[8,128]{1,0:T(8,128)S(1)} %get-tuple-element.51.mean_ref, ...), custom_call_target="tpu_custom_call" | custom-call | tf_op jit(solution)/shard_map/pallas_call | solution.py:22
  58.9 0.0 collective-permute-done.12.received_ref
  58.9 0.6 collective-permute-done.13.near_ref
  59.5 0.2 shard_map.83
  59.7 2.8 %collective-permute-start.16 = (f32[8,128]{1,0:T(8,128)S(1)}, f32[8,128]{1,0:T(8,128)S(1)}, u32[]{:S(2)}, u32[]{:S(2)}) collective-permute-start(f32[8,128]{1,0:T(8,128)S(1)} %get-tuple-element.75), channel_id=1, source_target_pairs={{0,6},{2,4},{4,2},{6,0},{8,14},{10,12},{12,10},{14,8},{16,22},{18,... | collective-permute-start | bytes 12296 | tf_op jit(solution)/shard_map/ppermute | solution.py:386
  62.6 0.0 collective-permute-start.15
  62.6 0.7 collective-permute-start.14
  63.3 1.3 %collective-permute-start.21 = (bf16[128,1024]{1,0:T(8,128)(2,1)S(1)}, bf16[128,1024]{1,0:T(8,128)(2,1)S(1)}, u32[]{:S(2)}, u32[]{:S(2)}) collective-permute-start(bf16[128,1024]{1,0:T(8,128)(2,1)S(1)} %get-tuple-element.79), channel_id=1, source_target_pairs={{0,2},{2,0},{4,6},{6,4},{8,10},{10,8},{12,14},{14,12},{16,18},{18,... | collective-permute-start | bytes 786440 | tf_op jit(solution)/shard_map/ppermute | solution.py:343
  64.6 2.0 %collective-permute-start.20 = (bf16[128,1024]{1,0:T(8,128)(2,1)S(1)}, bf16[128,1024]{1,0:T(8,128)(2,1)S(1)}, u32[]{:S(2)}, u32[]{:S(2)}) collective-permute-start(bf16[128,1024]{1,0:T(8,128)(2,1)S(1)} %collective-permute-done.13.near_ref), channel_id=1, source_target_pairs={{0,4},{2,30},{4,8},{6,2},{8,12},{10,6},{12,16},{14,10},{16,20},{18... | collective-permute-start | bytes 786440 | tf_op jit(solution)/shard_map/ppermute | solution.py:355
  66.6 0.0 collective-permute-done.16
  66.6 0.0 collective-permute-done.15
  66.6 0.0 collective-permute-done.14
  66.7 3.1 %collective-permute-start.19 = (f32[8,128]{1,0:T(8,128)S(1)}, f32[8,128]{1,0:T(8,128)S(1)}, u32[]{:S(2)}, u32[]{:S(2)}) collective-permute-start(f32[8,128]{1,0:T(8,128)S(1)} %add_add_fusion.1), channel_id=1, source_target_pairs={{0,24},{2,26},{4,28},{6,30},{8,16},{10,18},{12,20},{14,22},{16,8},... | collective-permute-start | bytes 12296 | tf_op jit(solution)/shard_map/ppermute | solution.py:386
  69.7 0.0 collective-permute-start.18
  69.7 1.4 %collective-permute-start.17 = (f32[8,128]{1,0:T(8,128)S(1)}, f32[8,128]{1,0:T(8,128)S(1)}, u32[]{:S(2)}, u32[]{:S(2)}) collective-permute-start(f32[8,128]{1,0:T(8,128)S(1)} %add_add_fusion.1), channel_id=1, source_target_pairs={{0,8},{2,10},{4,12},{6,14},{8,0},{10,2},{12,4},{14,6},{16,24},{18,... | collective-permute-start | bytes 12296 | tf_op jit(solution)/shard_map/ppermute | solution.py:386
  71.1 1.0 %collective-permute-done.19 = f32[8,128]{1,0:T(8,128)S(1)} collective-permute-done((f32[8,128]{1,0:T(8,128)S(1)}, f32[8,128]{1,0:T(8,128)S(1)}, u32[]{:S(2)}, u32[]{:S(2)}) %collective-permute-start.19) | collective-permute-done | bytes 4128 | tf_op jit(solution)/shard_map/ppermute | solution.py:386
  72.1 2.1 %collective-permute-done.18 = f32[8,128]{1,0:T(8,128)S(1)} collective-permute-done((f32[8,128]{1,0:T(8,128)S(1)}, f32[8,128]{1,0:T(8,128)S(1)}, u32[]{:S(2)}, u32[]{:S(2)}) %collective-permute-start.18) | collective-permute-done | bytes 4128 | tf_op jit(solution)/shard_map/ppermute | solution.py:386
  74.2 0.0 collective-permute-done.17
  74.2 0.0 collective-permute-done.21.q_ref
  74.3 0.0 collective-permute-done.20.far_ref
  74.3 2.0 %shard_map.84 = (f32[1024,128]{1,0:T(8,128)}, f32[1024,128]{1,0:T(8,128)}) custom-call(f32[1,128]{1,0:T(1,128)S(1)} %add_multiply_fusion.shift_ref, f32[8,128]{1,0:T(8,128)S(1)} %add_add_fusion.moment_ref, f32[1024,128]{1,0:T(8,128)S(1)} %copy-done.2, f32[1024,128]{1,0:T(8,128)S(1)} %get-tuple-element.76.k1_ref, f32[1024,128]{1,0:T(8,128)S(1)} %get-tuple-element.77.k2_ref, ...), custom_call_target="tpu_custom_call" | custom-call | tf_op jit(solution)/shard_map/pallas_call | solution.py:22
  (14 shorter events, 0.0 us)
Async XLA Ops:
  0.6 4.5 %copy-start = (bf16[8,16,64,128]{3,2,1,0:T(8,128)(2,1)S(1)}, bf16[8,16,64,128]{3,2,1,0:T(8,128)(2,1)}, u32[]{:S(2)}) copy-start(bf16[8,16,64,128]{3,2,1,0:T(8,128)(2,1)} %part_ref.1) | copy-start | bytes 6291460
  0.6 6.6 %collective-permute-start = (bf16[8,16,64,128]{3,2,1,0:T(8,128)(2,1)}, bf16[8,16,64,128]{3,2,1,0:T(8,128)(2,1)S(1)}, u32[]{:S(2)}, u32[]{:S(2)}) collective-permute-start(bf16[8,16,64,128]{3,2,1,0:T(8,128)(2,1)} %part_ref.1), channel_id=1, source_target_pairs={{0,1},{1,0},{2,3},{3,2},{4,5},{5,4},{6,7},{7,6},{8,9},{9,8},{10,11... | collective-permute-start | bytes 6291464 | tf_op jit(solution)/shard_map/ppermute | solution.py:410
  1.2 1.1 %copy-start.1 = (f32[1024,128]{1,0:T(8,128)S(1)}, f32[1024,128]{1,0:T(8,128)}, u32[]{:S(2)}) copy-start(f32[1024,128]{1,0:T(8,128)} %targets_ref.3) | copy-start | bytes 1572868
  2.3 2.8 %copy-start.3 = (f32[1024]{0:T(1024)S(1)}, f32[1024]{0:T(1024)}, u32[]{:S(2)}) copy-start(f32[1024]{0:T(1024)} %param.6) | copy-start | bytes 12292
  2.3 2.8 %copy-start.4 = (s32[8,16]{1,0:T(8,128)S(1)}, s32[8,16]{1,0:T(8,128)}, u32[]{:S(2)}) copy-start(s32[8,16]{1,0:T(8,128)} %col_ref.3) | copy-start | bytes 1540
  2.3 2.8 %copy-start.5 = (s32[8]{0:T(128)S(1)}, s32[8]{0:T(128)}, u32[]{:S(2)}) copy-start(s32[8]{0:T(128)} %length_ref.3) | copy-start | bytes 100
  2.5 12.5 %collective-permute-start.4 = (bf16[128,1024]{1,0:T(8,128)(2,1)S(1)}, bf16[128,1024]{1,0:T(8,128)(2,1)S(1)}, u32[]{:S(2)}, u32[]{:S(2)}) collective-permute-start(bf16[128,1024]{1,0:T(8,128)(2,1)S(1)} %get-tuple-element.46.v_ref), channel_id=1, source_target_pairs={{0,2},{2,0},{4,6},{6,4},{8,10},{10,8},{12,14},{14,12},{16,18},{18,... | collective-permute-start | bytes 786440 | tf_op jit(solution)/shard_map/ppermute | solution.py:343
  9.1 14.3 %collective-permute-start.3 = (bf16[144,1024]{1,0:T(8,128)(2,1)S(1)}, bf16[144,1024]{1,0:T(8,128)(2,1)S(1)}, u32[]{:S(2)}, u32[]{:S(2)}) collective-permute-start(bf16[144,1024]{1,0:T(8,128)(2,1)S(1)} %get-tuple-element.49), channel_id=1, source_target_pairs={{0,30},{2,4},{4,2},{6,8},{8,6},{10,12},{12,10},{14,16},{16,14},{18... | collective-permute-start | bytes 884744 | tf_op jit(solution)/shard_map/ppermute | solution.py:348
  13.9 11.5 %collective-permute-start.2 = (bf16[144,1024]{1,0:T(8,128)(2,1)S(1)}, bf16[144,1024]{1,0:T(8,128)(2,1)S(1)}, u32[]{:S(2)}, u32[]{:S(2)}) collective-permute-start(bf16[144,1024]{1,0:T(8,128)(2,1)S(1)} %get-tuple-element.45.own_ref), channel_id=1, source_target_pairs={{0,2},{2,0},{4,6},{6,4},{8,10},{10,8},{12,14},{14,12},{16,18},{18,... | collective-permute-start | bytes 884744 | tf_op jit(solution)/shard_map/ppermute | solution.py:343
  15.0 12.4 %collective-permute-start.5 = (bf16[128,1024]{1,0:T(8,128)(2,1)S(1)}, bf16[128,1024]{1,0:T(8,128)(2,1)S(1)}, u32[]{:S(2)}, u32[]{:S(2)}) collective-permute-start(bf16[128,1024]{1,0:T(8,128)(2,1)S(1)} %collective-permute-done.4.near_ref.near0_ref), channel_id=1, source_target_pairs={{0,4},{2,30},{4,8},{6,2},{8,12},{10,6},{12,16},{14,10},{16,20},{18... | collective-permute-start | bytes 786440 | tf_op jit(solution)/shard_map/ppermute | solution.py:355
  15.1 6.0 %collective-permute-start.1 = (f32[1,128]{1,0:T(1,128)S(1)}, f32[1,128]{1,0:T(1,128)S(1)}, u32[]{:S(2)}, u32[]{:S(2)}) collective-permute-start(f32[1,128]{1,0:T(1,128)S(1)} %get-tuple-element.47), channel_id=1, source_target_pairs={{0,8},{2,10},{4,12},{6,14},{8,0},{10,2},{12,4},{14,6},{16,24},{18,... | collective-permute-start | bytes 1544 | tf_op jit(solution)/shard_map/ppermute | solution.py:376
  29.0 8.3 %collective-permute-start.8 = (bf16[144,1024]{1,0:T(8,128)(2,1)S(1)}, bf16[144,1024]{1,0:T(8,128)(2,1)S(1)}, u32[]{:S(2)}, u32[]{:S(2)}) collective-permute-start(bf16[144,1024]{1,0:T(8,128)(2,1)S(1)} %get-tuple-element.59), channel_id=1, source_target_pairs={{0,28},{2,6},{4,0},{6,10},{8,4},{10,14},{12,8},{14,18},{16,12},{18... | collective-permute-start | bytes 884744 | tf_op jit(solution)/shard_map/ppermute | solution.py:362
  31.3 9.5 %collective-permute-start.6 = (bf16[128,1024]{1,0:T(8,128)(2,1)S(1)}, bf16[128,1024]{1,0:T(8,128)(2,1)S(1)}, u32[]{:S(2)}, u32[]{:S(2)}) collective-permute-start(bf16[128,1024]{1,0:T(8,128)(2,1)S(1)} %get-tuple-element.54.v_ref), channel_id=1, source_target_pairs={{0,2},{2,0},{4,6},{6,4},{8,10},{10,8},{12,14},{14,12},{16,18},{18,... | collective-permute-start | bytes 786440 | tf_op jit(solution)/shard_map/ppermute | solution.py:343
  31.3 5.6 %collective-permute-start.9 = (f32[1,128]{1,0:T(1,128)S(1)}, f32[1,128]{1,0:T(1,128)S(1)}, u32[]{:S(2)}, u32[]{:S(2)}) collective-permute-start(f32[1,128]{1,0:T(1,128)S(1)} %add.27), channel_id=1, source_target_pairs={{0,4},{2,6},{4,0},{6,2},{8,12},{10,14},{12,8},{14,10},{16,20},{18,... | collective-permute-start | bytes 1544 | tf_op jit(solution)/shard_map/ppermute | solution.py:376
  37.5 13.5 %collective-permute-start.10 = (bf16[144,1024]{1,0:T(8,128)(2,1)S(1)}, bf16[144,1024]{1,0:T(8,128)(2,1)S(1)}, u32[]{:S(2)}, u32[]{:S(2)}) collective-permute-start(bf16[144,1024]{1,0:T(8,128)(2,1)S(1)} %shard_map.78.own_ref), channel_id=1, source_target_pairs={{0,2},{2,0},{4,6},{6,4},{8,10},{10,8},{12,14},{14,12},{16,18},{18,... | collective-permute-start | bytes 884744 | tf_op jit(solution)/shard_map/ppermute | solution.py:343
  40.7 9.1 %collective-permute-start.7 = (bf16[128,1024]{1,0:T(8,128)(2,1)S(1)}, bf16[128,1024]{1,0:T(8,128)(2,1)S(1)}, u32[]{:S(2)}, u32[]{:S(2)}) collective-permute-start(bf16[128,1024]{1,0:T(8,128)(2,1)S(1)} %collective-permute-done.6.near_ref.near1_ref), channel_id=1, source_target_pairs={{0,4},{2,30},{4,8},{6,2},{8,12},{10,6},{12,16},{14,10},{16,20},{18... | collective-permute-start | bytes 786440 | tf_op jit(solution)/shard_map/ppermute | solution.py:355
  51.8 7.0 %collective-permute-start.12 = (bf16[128,1024]{1,0:T(8,128)(2,1)S(1)}, bf16[128,1024]{1,0:T(8,128)(2,1)S(1)}, u32[]{:S(2)}, u32[]{:S(2)}) collective-permute-start(bf16[128,1024]{1,0:T(8,128)(2,1)S(1)} %get-tuple-element.73), channel_id=1, source_target_pairs={{0,28},{2,6},{4,0},{6,10},{8,4},{10,14},{12,8},{14,18},{16,12},{18... | collective-permute-start | bytes 786440 | tf_op jit(solution)/shard_map/ppermute | solution.py:362
  53.0 21.2 %copy-start.2 = (f32[1024,128]{1,0:T(8,128)S(1)}, f32[1024,128]{1,0:T(8,128)}, u32[]{:S(2)}) copy-start(f32[1024,128]{1,0:T(8,128)} %targets_ref.3) | copy-start | bytes 1572868
  53.0 6.5 %collective-permute-start.13 = (bf16[128,1024]{1,0:T(8,128)(2,1)S(1)}, bf16[128,1024]{1,0:T(8,128)(2,1)S(1)}, u32[]{:S(2)}, u32[]{:S(2)}) collective-permute-start(bf16[128,1024]{1,0:T(8,128)(2,1)S(1)} %get-tuple-element.74.v_ref), channel_id=1, source_target_pairs={{0,2},{2,0},{4,6},{6,4},{8,10},{10,8},{12,14},{14,12},{16,18},{18,... | collective-permute-start | bytes 786440 | tf_op jit(solution)/shard_map/ppermute | solution.py:343
  53.1 4.5 %collective-permute-start.11 = (f32[1,128]{1,0:T(1,128)S(1)}, f32[1,128]{1,0:T(1,128)S(1)}, u32[]{:S(2)}, u32[]{:S(2)}) collective-permute-start(f32[1,128]{1,0:T(1,128)S(1)} %get-tuple-element.62), channel_id=1, source_target_pairs={{0,16},{2,18},{4,20},{6,22},{8,24},{10,26},{12,28},{14,30},{16,0},... | collective-permute-start | bytes 1544 | tf_op jit(solution)/shard_map/ppermute | solution.py:376
  59.7 6.9 %collective-permute-start.16 = (f32[8,128]{1,0:T(8,128)S(1)}, f32[8,128]{1,0:T(8,128)S(1)}, u32[]{:S(2)}, u32[]{:S(2)}) collective-permute-start(f32[8,128]{1,0:T(8,128)S(1)} %get-tuple-element.75), channel_id=1, source_target_pairs={{0,6},{2,4},{4,2},{6,0},{8,14},{10,12},{12,10},{14,8},{16,22},{18,... | collective-permute-start | bytes 12296 | tf_op jit(solution)/shard_map/ppermute | solution.py:386
  62.6 4.1 %collective-permute-start.15 = (f32[8,128]{1,0:T(8,128)S(1)}, f32[8,128]{1,0:T(8,128)S(1)}, u32[]{:S(2)}, u32[]{:S(2)}) collective-permute-start(f32[8,128]{1,0:T(8,128)S(1)} %get-tuple-element.75), channel_id=1, source_target_pairs={{0,4},{2,6},{4,0},{6,2},{8,12},{10,14},{12,8},{14,10},{16,20},{18,... | collective-permute-start | bytes 12296 | tf_op jit(solution)/shard_map/ppermute | solution.py:386
  62.6 4.1 %collective-permute-start.14 = (f32[8,128]{1,0:T(8,128)S(1)}, f32[8,128]{1,0:T(8,128)S(1)}, u32[]{:S(2)}, u32[]{:S(2)}) collective-permute-start(f32[8,128]{1,0:T(8,128)S(1)} %get-tuple-element.75), channel_id=1, source_target_pairs={{0,2},{2,0},{4,6},{6,4},{8,10},{10,8},{12,14},{14,12},{16,18},{18,... | collective-permute-start | bytes 12296 | tf_op jit(solution)/shard_map/ppermute | solution.py:386
  63.3 11.0 %collective-permute-start.21 = (bf16[128,1024]{1,0:T(8,128)(2,1)S(1)}, bf16[128,1024]{1,0:T(8,128)(2,1)S(1)}, u32[]{:S(2)}, u32[]{:S(2)}) collective-permute-start(bf16[128,1024]{1,0:T(8,128)(2,1)S(1)} %get-tuple-element.79), channel_id=1, source_target_pairs={{0,2},{2,0},{4,6},{6,4},{8,10},{10,8},{12,14},{14,12},{16,18},{18,... | collective-permute-start | bytes 786440 | tf_op jit(solution)/shard_map/ppermute | solution.py:343
  64.6 9.6 %collective-permute-start.20 = (bf16[128,1024]{1,0:T(8,128)(2,1)S(1)}, bf16[128,1024]{1,0:T(8,128)(2,1)S(1)}, u32[]{:S(2)}, u32[]{:S(2)}) collective-permute-start(bf16[128,1024]{1,0:T(8,128)(2,1)S(1)} %collective-permute-done.13.near_ref), channel_id=1, source_target_pairs={{0,4},{2,30},{4,8},{6,2},{8,12},{10,6},{12,16},{14,10},{16,20},{18... | collective-permute-start | bytes 786440 | tf_op jit(solution)/shard_map/ppermute | solution.py:355
  66.7 5.5 %collective-permute-start.19 = (f32[8,128]{1,0:T(8,128)S(1)}, f32[8,128]{1,0:T(8,128)S(1)}, u32[]{:S(2)}, u32[]{:S(2)}) collective-permute-start(f32[8,128]{1,0:T(8,128)S(1)} %add_add_fusion.1), channel_id=1, source_target_pairs={{0,24},{2,26},{4,28},{6,30},{8,16},{10,18},{12,20},{14,22},{16,8},... | collective-permute-start | bytes 12296 | tf_op jit(solution)/shard_map/ppermute | solution.py:386
  69.7 4.5 %collective-permute-start.18 = (f32[8,128]{1,0:T(8,128)S(1)}, f32[8,128]{1,0:T(8,128)S(1)}, u32[]{:S(2)}, u32[]{:S(2)}) collective-permute-start(f32[8,128]{1,0:T(8,128)S(1)} %add_add_fusion.1), channel_id=1, source_target_pairs={{0,16},{2,18},{4,20},{6,22},{8,24},{10,26},{12,28},{14,30},{16,0},... | collective-permute-start | bytes 12296 | tf_op jit(solution)/shard_map/ppermute | solution.py:386
  69.7 4.5 %collective-permute-start.17 = (f32[8,128]{1,0:T(8,128)S(1)}, f32[8,128]{1,0:T(8,128)S(1)}, u32[]{:S(2)}, u32[]{:S(2)}) collective-permute-start(f32[8,128]{1,0:T(8,128)S(1)} %add_add_fusion.1), channel_id=1, source_target_pairs={{0,8},{2,10},{4,12},{6,14},{8,0},{10,2},{12,4},{14,6},{16,24},{18,... | collective-permute-start | bytes 12296 | tf_op jit(solution)/shard_map/ppermute | solution.py:386
